TPU v7x, 32 devices: a whole 2x2x4 slice. The times are simulated.
32 devices in a mesh: tm: 8 (over z, core), box: 4 (over y, x).
Axes of the slice: x: 2, y: 2, z: 4, core: 2. Of those that a mesh axis runs over, the one named last changes fastest.
Arguments:
- traces: bfloat16 [6, 128, 65536], P(None, 'tm', 'box'), may hold values from -6 to 6
- projection: bfloat16 [4, 128, 128, 128], P('box', 'tm'), may hold values from -0.5 to 0.5
- owner_route: int32 [4, 128, 1], P('box', 'tm'), may hold values from 0 to 3; in each aligned block of 16 rows (0 to 15, 16 to 31, ..., all dimensions but the last counted through in order) at most 5 rows name the same one
- face_slot: int32 [4, 128, 1], P('box', 'tm'), may hold values from 0 to 3
- face_weight: float32 [128, 128], P(('tm', 'box')), may hold values from 0.2 to 2
Outputs:
- face_load: bfloat16 [128, 6, 128, 128], P(('tm', 'box'))
Inputs may be any that keep to these rules, and one draw needn't show every extreme that they name: `owner_route`: in the aligned blocks of 16 rows (the rows of one device), no owner is named by more than 5 rows, a bound that some block reaches.
All inputs are finite; a program needn't handle non-finite values.
Results may differ from a plain program's by a relative error of at most 0.005.
Values may be sent and summed in bfloat16 or wider, within the bound.
No kernel may reach another device: no remote copies, remote signals or barrier semaphores. Data moves between devices by JAX's collectives and lax.ppermute only.
A program may use at most 192 MiB of HBM per device.

v0:
```python
import jax
import jax.numpy as jnp
from jax import lax
from jax.sharding import PartitionSpec as P


def ranks_within(owners):
    blocks = owners.shape[-1]
    same = owners[..., :, None] == owners[..., None, :]
    before = jnp.arange(blocks)[None, :] < jnp.arange(blocks)[:, None]
    return jnp.sum((same & before).astype(jnp.int32), axis=-1)


def per_device(traces, projection, owner_route, face_slot, face_weight):
    nodes = projection.shape[-1]
    blocks = projection.shape[1]
    slots_dev = face_weight.shape[0]
    boxes = lax.axis_size("box")
    bucket = blocks // boxes + 1
    matrices = projection[0]
    pointwise = lax.all_to_all(traces, "tm", split_axis=2, concat_axis=1, tiled=True)
    count = pointwise.shape[0]
    shaped = pointwise.reshape(count, pointwise.shape[1], blocks, nodes)
    result = jnp.einsum("csjn,jnm->jcsm", shaped, matrices, preferred_element_type=jnp.float32)
    faces = result.astype(jnp.bfloat16)
    own_owner = owner_route[0, :, 0]
    own_slot = face_slot[0, :, 0]
    own_rank = ranks_within(own_owner)
    target_owner = jnp.arange(boxes)[:, None, None]
    target_rank = jnp.arange(bucket)[None, :, None]
    chosen = (own_owner[None, None, :] == target_owner) & (own_rank[None, None, :] == target_rank)
    chosen = chosen.reshape(boxes * bucket, blocks)
    picker = chosen.astype(jnp.bfloat16)
    outgoing = jnp.einsum(
        "kj,jcsn->kcsn", picker, faces, preferred_element_type=jnp.float32
    ).astype(jnp.bfloat16)
    outgoing = outgoing.reshape((boxes, bucket) + faces.shape[1:])
    samples = faces.shape[2]
    filled = jnp.sum(chosen.astype(jnp.float32), axis=1)
    slot_sum = jnp.sum(chosen.astype(jnp.float32) * own_slot[None, :].astype(jnp.float32), axis=1)
    tag_value = slot_sum + (filled - 1.0)
    tag_grid = jnp.broadcast_to(
        tag_value.reshape(boxes, bucket, 1, 1, 1), (boxes, bucket, 1, samples, 1)
    ).astype(jnp.bfloat16)
    arrived = lax.all_to_all(outgoing, "box", split_axis=0, concat_axis=0, tiled=True)
    tagged = lax.all_to_all(tag_grid, "box", split_axis=0, concat_axis=0, tiled=True)
    width = arrived.shape[3]
    flat = arrived.reshape((boxes * bucket,) + arrived.shape[2:])
    tag_flat = tagged.reshape(boxes * bucket, width).astype(jnp.float32)
    placing = (
        tag_flat[None, :, :] == jnp.arange(slots_dev, dtype=jnp.float32)[:, None, None]
    ).astype(jnp.bfloat16)
    gathered = jnp.einsum("fks,kcsn->fcsn", placing, flat, preferred_element_type=jnp.float32)
    return (gathered * face_weight[:, None, None, :]).astype(jnp.bfloat16)


def solution(mesh):
    return jax.shard_map(
        per_device,
        mesh=mesh,
        in_specs=(
            P(None, "tm", "box"),
            P("box", "tm", None, None),
            P("box", "tm", None),
            P("box", "tm", None),
            P(("tm", "box"), None),
        ),
        out_specs=P(("tm", "box"), None, None, None),
        check_vma=False,
    )
```

profile of v0, /device:TPU:0, one launch (start us, length us, event | category | flops | bytes accessed | tf_op | source)
XLA Modules:
  0.0 268.9 jit_solution(5230005541196042914)
XLA Ops:
  0.0 0.0 copy-start
  0.0 26.7 %copy.23 = bf16[6,16,16384]{1,0,2:T(8,128)(2,1)} copy(bf16[6,16,16384]{2,1,0:T(8,128)(2,1)} %param.5) | data formatting | bytes 6291456 | tf_op args[0]
  26.7 29.7 %reshape.113 = bf16[8,2,98304]{2,1,0:T(2,128)(2,1)} reshape(bf16[16384,6,16]{2,1,0:T(8,128)(2,1)} %bitcast.35) | data formatting | bytes 6291456
  56.4 0.0 copy-start.2
  56.4 0.0 copy-start.3
  56.4 6.5 %all-to-all-start = ((bf16[8,2,98304]{2,1,0:T(2,128)(2,1)}), bf16[8,2,98304]{2,1,0:T(2,128)(2,1)}, u32[]{:S(2)}, u32[]{:S(2)}) async-start(bf16[8,2,98304]{2,1,0:T(2,128)(2,1)} %reshape.113), calls=%async_computation | async-start | bytes 6291456 | tf_op jit(solution)/shard_map/all_to_all | solution.py:21
  62.9 0.0 copy-done.2
  62.9 0.2 convert_reduce_fusion.1
  63.1 0.0 copy-done.3
  63.1 0.1 convert_reduce_fusion
  63.2 71.3 %all-to-all-done = bf16[8,2,98304]{2,1,0:T(2,128)(2,1)} async-done(((bf16[8,2,98304]{2,1,0:T(2,128)(2,1)}), bf16[8,2,98304]{2,1,0:T(2,128)(2,1)}, u32[]{:S(2)}, u32[]{:S(2)}) %all-to-all-start) | async-done | bytes 3145760 | tf_op jit(solution)/shard_map/all_to_all | solution.py:21
  134.5 0.7 broadcast_in_dim.2
  135.2 3.7 %all-to-all-start.2 = ((bf16[4,5,1,128,1]{3,1,4,2,0:T(8,128)(2,1)}), bf16[4,5,1,128,1]{3,1,4,2,0:T(8,128)(2,1)S(1)}, u32[]{:S(2)}, u32[]{:S(2)}) async-start(bf16[4,5,1,128,1]{3,1,4,2,0:T(8,128)(2,1)} %broadcast_in_dim.2), calls=%async_computation.2 | async-start | bytes 16384 | tf_op jit(solution)/shard_map/all_to_all | solution.py:46
  138.9 33.4 %reshape.114 = bf16[16384,6,16]{2,1,0:T(8,128)(2,1)} reshape(bf16[8,2,98304]{2,1,0:T(2,128)(2,1)} %all-to-all-done) | data formatting | bytes 6291456
  172.3 31.0 %copy.24 = bf16[6,16,8,2048]{3,1,2,0:T(8,128)(2,1)} copy(bf16[6,16,8,2048]{1,0,3,2:T(8,128)(2,1)} %bitcast.34) | data formatting | bytes 6291456 | tf_op jit(solution)/shard_map/all_to_all | solution.py:21
  203.3 2.9 %copy.36 = bf16[96,8,16,128]{3,2,1,0:T(8,128)(2,1)S(1)} copy(bf16[96,8,16,128]{3,1,2,0:T(8,128)(2,1)} %bitcast.37) | data formatting | bytes 6291456
  206.2 0.0 copy-done
  206.2 1.0 fusion.9
  207.2 2.3 fusion.6
  209.5 2.9 %copy.28 = bf16[20,6,128,128]{3,2,1,0:T(8,128)(2,1)} copy(bf16[20,6,128,128]{3,0,2,1:T(8,128)(2,1)S(1)} %fusion.6) | data formatting | bytes 7864320 | tf_op jit(solution)/shard_map/convert_element_type | solution.py:36
  212.4 0.0 all-to-all-done.2
  212.4 0.0 copy-start.1
  212.4 5.2 %all-to-all-start.1 = ((bf16[4,5,6,128,128]{4,3,2,1,0:T(8,128)(2,1)}), bf16[4,5,6,128,128]{4,3,2,1,0:T(8,128)(2,1)}, u32[]{:S(2)}, u32[]{:S(2)}) async-start(bf16[4,5,6,128,128]{4,3,2,1,0:T(8,128)(2,1)} %bitcast.36), calls=%async_computation.1 | async-start | bytes 7864320 | tf_op jit(solution)/shard_map/all_to_all | solution.py:45
  217.6 0.1 copy.29
  217.7 44.3 %all-to-all-done.1 = bf16[4,5,6,128,128]{4,3,2,1,0:T(8,128)(2,1)} async-done(((bf16[4,5,6,128,128]{4,3,2,1,0:T(8,128)(2,1)}), bf16[4,5,6,128,128]{4,3,2,1,0:T(8,128)(2,1)}, u32[]{:S(2)}, u32[]{:S(2)}) %all-to-all-start.1) | async-done | bytes 3932192 | tf_op jit(solution)/shard_map/all_to_all | solution.py:45
  262.0 0.0 copy-done.1
  262.0 5.8 %fusion.12 = bf16[4,6,128,128]{3,0,1,2:T(4,128)(2,1)S(1)} fusion(bf16[20,6,128,128]{3,2,1,0:T(8,128)(2,1)} %bitcast.8, f32[4,128]{1,0:T(4,128)S(1)} %copy-done.1, f32[20,128]{0,1:T(8,128)S(1)} %copy.29), kind=kOutput, calls=%fused_computation.9 | convolution fusion | flops 16525312 | bytes 4730880 | tf_op jit(solution)/shard_map/fks,kcsn->fcsn/dot_general | solution.py:53
  267.8 1.1 copy.31
  (7 shorter events, 0.1 us)
Async XLA Ops:
  0.0 206.2 %copy-start = (bf16[1,16,128,128]{3,2,1,0:T(8,128)(2,1)S(1)}, bf16[1,16,128,128]{3,2,1,0:T(8,128)(2,1)}, u32[]{:S(2)}) copy-start(bf16[1,16,128,128]{3,2,1,0:T(8,128)(2,1)} %param.6) | copy-start | bytes 1572868
  56.4 6.5 %copy-start.2 = (s32[1,16,1]{1,2,0:T(1,128)S(1)}, s32[1,16,1]{1,2,0:T(1,128)}, u32[]{:S(2)}) copy-start(s32[1,16,1]{1,2,0:T(1,128)} %param.7) | copy-start | bytes 196
  56.4 6.7 %copy-start.3 = (s32[1,16,1]{1,2,0:T(1,128)S(1)}, s32[1,16,1]{1,2,0:T(1,128)}, u32[]{:S(2)}) copy-start(s32[1,16,1]{1,2,0:T(1,128)} %param.8) | copy-start | bytes 196
  56.4 78.1 %all-to-all-start = ((bf16[8,2,98304]{2,1,0:T(2,128)(2,1)}), bf16[8,2,98304]{2,1,0:T(2,128)(2,1)}, u32[]{:S(2)}, u32[]{:S(2)}) async-start(bf16[8,2,98304]{2,1,0:T(2,128)(2,1)} %reshape.113), calls=%async_computation | async-start | bytes 6291456 | tf_op jit(solution)/shard_map/all_to_all | solution.py:21
  135.2 77.2 %all-to-all-start.2 = ((bf16[4,5,1,128,1]{3,1,4,2,0:T(8,128)(2,1)}), bf16[4,5,1,128,1]{3,1,4,2,0:T(8,128)(2,1)S(1)}, u32[]{:S(2)}, u32[]{:S(2)}) async-start(bf16[4,5,1,128,1]{3,1,4,2,0:T(8,128)(2,1)} %broadcast_in_dim.2), calls=%async_computation.2 | async-start | bytes 16384 | tf_op jit(solution)/shard_map/all_to_all | solution.py:46
  212.4 49.6 %copy-start.1 = (f32[4,128]{1,0:T(4,128)S(1)}, f32[4,128]{1,0:T(4,128)}, u32[]{:S(2)}) copy-start(f32[4,128]{1,0:T(4,128)} %param.9) | copy-start | bytes 6148
  212.4 49.6 %all-to-all-start.1 = ((bf16[4,5,6,128,128]{4,3,2,1,0:T(8,128)(2,1)}), bf16[4,5,6,128,128]{4,3,2,1,0:T(8,128)(2,1)}, u32[]{:S(2)}, u32[]{:S(2)}) async-start(bf16[4,5,6,128,128]{4,3,2,1,0:T(8,128)(2,1)} %bitcast.36), calls=%async_computation.1 | async-start | bytes 7864320 | tf_op jit(solution)/shard_map/all_to_all | solution.py:45
where the time goes:
time: 271 us; the launch traced here: 269 us
  local copies, waits for them, and re-layouts  128 us (47%)
  waiting for transfers between devices  116 us (43%)
  starting transfers between devices  15.3 us (6%)
  matrix products  9.08 us (3%)
    unnamed x12, local copies, waits for them, and re-layouts  92.7 us
    all_to_all x1, waiting for transfers between devices, per_device(): lax.all_to_all(traces, 'tm', split_axis=2, concat_axis=1, tiled=True)  71.3 us
    all_to_all x1, waiting for transfers between devices, per_device(): lax.all_to_all(outgoing, 'box', split_axis=0, concat_axis=0, tiled=True)  44.3 us
    all_to_all x1, local copies, waits for them, and re-layouts, per_device(): lax.all_to_all(traces, 'tm', split_axis=2, concat_axis=1, tiled=True)  31 us
    all_to_all x1, starting transfers between devices, per_device(): lax.all_to_all(traces, 'tm', split_axis=2, concat_axis=1, tiled=True)  6.46 us
    dot_general x1, matrix products, per_device(): jnp.einsum('fks,kcsn->fcsn', placing, flat, preferred_element_type=jnp.fl...  5.81 us
  transfers between devices with their start and end apart: 3, of which 2 were waited for; matrix products, arithmetic and copies ran while one was open for 27% of the time, Pallas kernels for 0%

commit v1 on v0

v1 whole, which is shorter than its diff:
```python
import functools

import jax
import jax.numpy as jnp
import numpy as np
from jax import lax
from jax.experimental import pallas as pl
from jax.experimental.pallas import tpu as pltpu
from jax.sharding import PartitionSpec as P

CORES = 2
IDS = 4


def pick_kernel(ids, x_ref, o_ref):
    o_ref[...] = x_ref[...]


def pick(ids, traces, chips, width):
    comp, samples, _ = traces.shape
    block = (comp, samples, width)
    return pl.pallas_call(
        pick_kernel,
        grid_spec=pltpu.PrefetchScalarGridSpec(
            num_scalar_prefetch=1,
            grid=(chips,),
            in_specs=[pl.BlockSpec(block, lambda i, ids: (0, 0, CORES * i + 1 - ids[0]))],
            out_specs=pl.BlockSpec(block, lambda i, ids: (0, 0, i)),
        ),
        out_shape=jax.ShapeDtypeStruct((comp, samples, width * chips), traces.dtype),
        name="pick",
    )(ids, traces)


def interpolate_kernel(turn, count, boxes, ids, targets, own_ref, far_ref, *rest):
    sources, outs, (mats, acc, sem) = rest[:count], rest[count:count + boxes], rest[count + boxes:]
    core, box, which = ids[turn * IDS], ids[turn * IDS + 2], ids[turn * IDS + 3]
    for i, source in enumerate(sources):
        @pl.when(which == i)
        def _():
            pltpu.make_async_copy(source, mats, sem).start()
    acc[...] = jnp.zeros_like(acc)
    pltpu.make_async_copy(sources[0], mats, sem).wait()
    blocks, nodes, _ = mats.shape
    comp, samples, _ = own_ref.shape
    slots = acc.shape[0] // boxes
    for j in range(blocks):
        target = targets[j]
        for ref, half in ((own_ref, core), (far_ref, 1 - core)):
            x = ref[:, :, j * nodes:(j + 1) * nodes]
            if samples % 16:
                x = x.astype(jnp.float32).reshape(comp * samples, nodes).astype(x.dtype)
            else:
                x = x.reshape(comp * samples, nodes)
            y = jnp.dot(x, mats[j], preferred_element_type=jnp.float32)
            acc[target, :, half] += y.reshape(comp, samples, nodes)
    for d, out in enumerate(outs):
        for s in range(slots):
            part = acc[(box ^ d) * slots + s]
            out[s] = part.reshape(comp, 2 * samples, nodes).astype(out.dtype)


def interpolate(turn, ids, targets, traces, far, sources, boxes, slots):
    blocks, nodes, _ = sources[0].shape
    comp, samples, _ = traces.shape
    width = blocks * nodes
    block = (comp, samples, width)
    shape = (slots, comp, 2 * samples, nodes)
    n = blocks * comp * CORES * samples
    return pl.pallas_call(
        functools.partial(interpolate_kernel, turn, len(sources), boxes),
        grid_spec=pltpu.PrefetchScalarGridSpec(
            num_scalar_prefetch=2,
            grid=(1,),
            in_specs=[
                pl.BlockSpec(block, lambda i, ids, t: (0, 0, CORES * ids[turn * IDS + 1] + ids[turn * IDS])),
                pl.BlockSpec(block, lambda i, ids, t: (0, 0, ids[turn * IDS + 1])),
            ] + [pl.BlockSpec(memory_space=pl.ANY)] * len(sources),
            out_specs=[pl.BlockSpec(shape, lambda i, ids, t: (0, 0, 0, 0))] * boxes,
            scratch_shapes=[
                pltpu.VMEM(sources[0].shape, sources[0].dtype),
                pltpu.VMEM((boxes * slots, comp, CORES, samples, nodes), jnp.float32),
                pltpu.SemaphoreType.DMA,
            ],
        ),
        out_shape=[
            jax.ShapeDtypeStruct(shape, jnp.bfloat16 if d else jnp.float32) for d in range(boxes)
        ],
        compiler_params=pltpu.CompilerParams(vmem_limit_bytes=32 * 2**20),
        cost_estimate=pl.CostEstimate(flops=2 * n * nodes * nodes, bytes_accessed=4 * n * nodes + 2 * blocks * nodes * nodes, transcendentals=0),
        name="interpolate",
    )(ids, targets, traces, far, *sources)


def total_kernel(*refs):
    out = refs[-1]
    for s in range(out.shape[0]):
        total = refs[0][s]
        for ref in refs[1:-1]:
            total = total + ref[s].astype(jnp.float32)
        out[s] = total.astype(out.dtype)


def total(parts, dtype):
    return pl.pallas_call(
        total_kernel,
        out_shape=jax.ShapeDtypeStruct(parts[0].shape, dtype),
        compiler_params=pltpu.CompilerParams(vmem_limit_bytes=32 * 2**20),
        cost_estimate=pl.CostEstimate(flops=parts[0].size * len(parts), bytes_accessed=2 * parts[0].size * (len(parts) + 2), transcendentals=0),
        name="total",
    )(*parts)


def finish_kernel(chips, ids, weight_ref, *refs):
    out = refs[-1]
    slots, _, length, _ = refs[0].shape
    for turn in range(chips):
        at = pl.ds(pl.multiple_of(ids[turn * IDS + 1] * length, length), length)
        for s in range(slots):
            value = refs[turn][s].astype(jnp.float32) * weight_ref[s:s + 1, :][None]
            out[s, :, at, :] = value.astype(out.dtype)


def finish(ids, weight, pieces):
    slots, comp, length, nodes = pieces[0].shape
    chips = len(pieces)
    shape = (slots, comp, length * chips, nodes)
    whole = lambda s: pl.BlockSpec(s, lambda i, ids: (0,) * len(s))
    return pl.pallas_call(
        functools.partial(finish_kernel, chips),
        grid_spec=pltpu.PrefetchScalarGridSpec(
            num_scalar_prefetch=1,
            grid=(1,),
            in_specs=[whole(weight.shape)] + [whole(p.shape) for p in pieces],
            out_specs=whole(shape),
        ),
        out_shape=jax.ShapeDtypeStruct(shape, jnp.bfloat16),
        compiler_params=pltpu.CompilerParams(vmem_limit_bytes=32 * 2**20),
        name="finish",
    )(ids, weight, *pieces)


def plan(chips, boxes):
    ways = [[(0, 0)]]
    for r in range(1, chips):
        ways.append(sorted({((z ^ r) > z, abs((z ^ r) - z)) for z in range(chips)}))
    table = np.zeros((chips, CORES, boxes, chips, IDS), np.int32)
    for z in range(chips):
        for r in range(chips):
            way = ((z ^ r) > z, abs((z ^ r) - z))
            for c in range(CORES):
                for b in range(boxes):
                    table[z, c, b, r] = (c, z ^ r, b, ways[r].index(way))
    return ways, table.reshape(chips * CORES, boxes, chips * IDS)


def per_device(chips, boxes, traces, projection, owner_route, face_slot, face_weight):
    ways, table = plan(chips, boxes)
    matrices = projection[0]
    blocks, nodes, _ = matrices.shape
    slots = face_weight.shape[0]
    ids = jnp.asarray(table)[lax.axis_index("tm"), lax.axis_index("box")]

    def along(x, pairs):
        return lax.ppermute(x, "tm", [(a * CORES + c, b * CORES + c) for a, b in pairs for c in range(CORES)])

    arrived = {(0, 0): matrices}
    up, down = matrices, matrices
    for k in range(1, chips):
        up = along(up, [(z, z + 1) for z in range(k - 1, chips - 1)])
        down = along(down, [(z + 1, z) for z in range(chips - k)])
        arrived[(False, k)], arrived[(True, k)] = up, down

    targets = owner_route[0, :, 0] * slots + face_slot[0, :, 0]
    far = lax.ppermute(
        pick(ids, traces, chips, blocks * nodes), "tm", [(i, i ^ 1) for i in range(chips * CORES)]
    )
    pieces = []
    for r in range(chips):
        turn = [(z, z ^ r) for z in range(chips)]
        named = along(targets, turn) if r else targets
        parts = interpolate(r, ids, named, traces, far, [arrived[w] for w in ways[r]], boxes, slots)
        parts = [parts[0]] + [
            lax.ppermute(parts[d], "box", [(b, b ^ d) for b in range(boxes)]) for d in range(1, boxes)
        ]
        summed = total(parts, jnp.bfloat16 if r else jnp.float32)
        pieces.append(along(summed, turn) if r else summed)
    return finish(ids, face_weight, pieces)


def solution(mesh):
    chips, boxes = mesh.shape["tm"] // CORES, mesh.shape["box"]
    return jax.shard_map(
        functools.partial(per_device, chips, boxes),
        mesh=mesh,
        in_specs=(
            P(None, "tm", "box"),
            P("box", "tm", None, None),
            P("box", "tm", None),
            P("box", "tm", None),
            P(("tm", "box"), None),
        ),
        out_specs=P(("tm", "box"), None, None, None),
        check_vma=False,
    )
```

time: 271 us -> 104 us (0.38)
  local copies, waits for them, and re-layouts: 128 us -> 1.22 us
  waiting for transfers between devices: 116 us -> 55.2 us
  starting transfers between devices: 15.3 us -> 35.6 us
  Pallas kernels: 0 us -> 11.6 us
  matrix products: 9.08 us -> 0 us
    all_to_all x3 -> x0, waiting for transfers between devices: 116 us -> none  [the longest x1 71.3 us: per_device(): lax.all_to_all(traces, 'tm', split_axis=2, concat_axis=1, tiled=True)]
    unnamed x12, local copies, waits for them, and re-layouts: 92.7 us -> 0.02 us
    ppermute x0 -> x25, waiting for transfers between devices: none -> 55.2 us  [the longest x12 44.8 us: along(): lax.ppermute(x, 'tm', [(a * CORES + c, b * CORES + c) for a, b in pairs f...]
    ppermute x0 -> x25, starting transfers between devices: none -> 35.6 us  [the longest x12 18.8 us: along(): lax.ppermute(x, 'tm', [(a * CORES + c, b * CORES + c) for a, b in pairs f...]
    all_to_all x1 -> x0, local copies, waits for them, and re-layouts: 31 us -> none  [per_device(): lax.all_to_all(traces, 'tm', split_axis=2, concat_axis=1, tiled=True)]
    all_to_all x3 -> x0, starting transfers between devices: 15.3 us -> none  [the longest x1 6.46 us: per_device(): lax.all_to_all(traces, 'tm', split_axis=2, concat_axis=1, tiled=True)]
    pallas_call x0 -> x10, Pallas kernels: none -> 11.6 us  [the longest x4 5.06 us: interpolate(): pl.pallas_call(functools.partial(interpolate_kernel, turn, len(sources),...]
    dot_general x3 -> x0, matrix products: 9.08 us -> none  [the longest x1 5.81 us: per_device(): jnp.einsum('fks,kcsn->fcsn', placing, flat, preferred_element_type=jnp.fl...]
  transfers between devices with their start and end apart: 3 -> 25, of which waited for: 2 -> 12; matrix products, arithmetic and copies ran while one was open for 27% -> 0% of each run, Pallas kernels for 0% -> 5%
where the time goes in v1:
time: 104 us
  waiting for transfers between devices  55.2 us (53%)
  starting transfers between devices  35.6 us (34%)
  Pallas kernels  11.6 us (11%)
  local copies, waits for them, and re-layouts  1.22 us (1%)
    ppermute x12, waiting for transfers between devices, along(): lax.ppermute(x, 'tm', [(a * CORES + c, b * CORES + c) for a, b in pairs f...  44.8 us
    ppermute x12, starting transfers between devices, along(): lax.ppermute(x, 'tm', [(a * CORES + c, b * CORES + c) for a, b in pairs f...  18.8 us
    ppermute x12, starting transfers between devices, per_device(): lax.ppermute(parts[d], 'box', [(b, b ^ d) for b in range(boxes)])  16.3 us
    ppermute x12, waiting for transfers between devices, per_device(): lax.ppermute(parts[d], 'box', [(b, b ^ d) for b in range(boxes)])  10.4 us
    pallas_call x4, Pallas kernels, interpolate(): pl.pallas_call(functools.partial(interpolate_kernel, turn, len(sources),...  5.06 us
    pallas_call x1, Pallas kernels, pick(): pl.pallas_call(pick_kernel, grid_spec=pltpu.PrefetchScalarGridSpec(num_sc...  4.62 us
  transfers between devices with their start and end apart: 25, of which 12 were waited for; matrix products, arithmetic and copies ran while one was open for 0% of the time, Pallas kernels for 5%

profile of v1, /device:TPU:0, one launch (start us, length us, event | category | flops | bytes accessed | tf_op | source)
XLA Modules:
  0.0 103.8 jit_solution(11787241998127090556)
XLA Ops:
  0.0 1.2 %dynamic-slice_bitcast_fusion.ids = s32[16]{0:T(128)} fusion(s32[8,4,16]{2,1,0:T(4,128)} %constant.18.clone, s32[]{:T(128)S(6)} %select_n.6, s32[]{:T(128)S(6)} %select_n.7), kind=kLoop, calls=%fused_computation.1 | loop fusion | bytes 136 | tf_op jit(solution)/shard_map/squeeze | solution.py:162
  1.2 4.6 %pick.1 = bf16[6,16,8192]{2,1,0:T(8,128)(2,1)} custom-call(s32[16]{0:T(128)} %dynamic-slice_bitcast_fusion.ids, bf16[6,16,16384]{2,1,0:T(8,128)(2,1)} %own_ref.7), custom_call_target="tpu_custom_call" | custom-call | tf_op jit(solution)/shard_map/pick/pallas_call | solution.py:22
  5.8 0.5 collective-permute-start
  6.3 4.5 %collective-permute-start.5 = (bf16[16,128,128]{2,1,0:T(8,128)(2,1)}, bf16[16,128,128]{2,1,0:T(8,128)(2,1)S(1)}, u32[]{:S(2)}, u32[]{:S(2)}) collective-permute-start(bf16[16,128,128]{2,1,0:T(8,128)(2,1)} %bitcast.5), channel_id=1, source_target_pairs={{0,8},{4,12},{8,16},{12,20},{16,24},{20,28},{1,9},{5,13},{9,17},{1... | collective-permute-start | bytes 1572872 | tf_op jit(solution)/shard_map/ppermute | solution.py:165
  10.8 1.3 %collective-permute-start.6 = (bf16[16,128,128]{2,1,0:T(8,128)(2,1)}, bf16[16,128,128]{2,1,0:T(8,128)(2,1)S(1)}, u32[]{:S(2)}, u32[]{:S(2)}) collective-permute-start(bf16[16,128,128]{2,1,0:T(8,128)(2,1)} %bitcast.6), channel_id=1, source_target_pairs={{8,0},{12,4},{16,8},{20,12},{24,16},{28,20},{9,1},{13,5},{17,9},{2... | collective-permute-start | bytes 1572872 | tf_op jit(solution)/shard_map/ppermute | solution.py:165
  12.1 10.8 %collective-permute-done.5.rest_0_ = bf16[16,128,128]{2,1,0:T(8,128)(2,1)S(1)} collective-permute-done((bf16[16,128,128]{2,1,0:T(8,128)(2,1)}, bf16[16,128,128]{2,1,0:T(8,128)(2,1)S(1)}, u32[]{:S(2)}, u32[]{:S(2)}) %collective-permute-start.5) | collective-permute-done | bytes 524320 | tf_op jit(solution)/shard_map/ppermute | solution.py:165
  22.9 0.7 collective-permute-start.12
  23.6 3.4 %collective-permute-done.6.rest_1_.rest_2_ = bf16[16,128,128]{2,1,0:T(8,128)(2,1)S(1)} collective-permute-done((bf16[16,128,128]{2,1,0:T(8,128)(2,1)}, bf16[16,128,128]{2,1,0:T(8,128)(2,1)S(1)}, u32[]{:S(2)}, u32[]{:S(2)}) %collective-permute-start.6) | collective-permute-done | bytes 524320 | tf_op jit(solution)/shard_map/ppermute | solution.py:165
  27.0 1.3 %collective-permute-start.13 = (bf16[16,128,128]{2,1,0:T(8,128)(2,1)S(1)}, bf16[16,128,128]{2,1,0:T(8,128)(2,1)S(1)}, u32[]{:S(2)}, u32[]{:S(2)}) collective-permute-start(bf16[16,128,128]{2,1,0:T(8,128)(2,1)S(1)} %collective-permute-done.6.rest_1_.rest_2_), channel_id=1, source_target_pairs={{8,0},{12,4},{16,8},{20,12},{9,1},{13,5},{17,9},{21,13},{10,2},{14... | collective-permute-start | bytes 1572872 | tf_op jit(solution)/shard_map/ppermute | solution.py:165
  28.2 0.0 collective-permute-done.12.rest_0_
  28.2 0.7 collective-permute-start.19
  29.0 13.3 %collective-permute-done.13.rest_1_ = bf16[16,128,128]{2,1,0:T(8,128)(2,1)S(1)} collective-permute-done((bf16[16,128,128]{2,1,0:T(8,128)(2,1)S(1)}, bf16[16,128,128]{2,1,0:T(8,128)(2,1)S(1)}, u32[]{:S(2)}, u32[]{:S(2)}) %collective-permute-start.13) | collective-permute-done | bytes 524320 | tf_op jit(solution)/shard_map/ppermute | solution.py:165
  42.2 1.3 %collective-permute-start.20 = (bf16[16,128,128]{2,1,0:T(8,128)(2,1)S(1)}, bf16[16,128,128]{2,1,0:T(8,128)(2,1)S(1)}, u32[]{:S(2)}, u32[]{:S(2)}) collective-permute-start(bf16[16,128,128]{2,1,0:T(8,128)(2,1)S(1)} %collective-permute-done.13.rest_1_), channel_id=1, source_target_pairs={{8,0},{12,4},{9,1},{13,5},{10,2},{14,6},{11,3},{15,7}} | collective-permute-start | bytes 1572872 | tf_op jit(solution)/shard_map/ppermute | solution.py:165
  43.6 2.7 %collective-permute-start.4 = (s32[16]{0:T(128)S(1)}, s32[16]{0:T(128)S(1)}, u32[]{:S(2)}, u32[]{:S(2)}) collective-permute-start(s32[16]{0:T(128)S(1)} %add_bitcast_fusion.targets), channel_id=1, source_target_pairs={{0,8},{4,12},{8,0},{12,4},{16,24},{20,28},{24,16},{28,20},{1,9},{5... | collective-permute-start | bytes 200 | tf_op jit(solution)/shard_map/ppermute | solution.py:165
  46.3 0.0 collective-permute-start.11
  46.3 10.4 %collective-permute-done.4.targets = s32[16]{0:T(128)S(1)} collective-permute-done((s32[16]{0:T(128)S(1)}, s32[16]{0:T(128)S(1)}, u32[]{:S(2)}, u32[]{:S(2)}) %collective-permute-start.4) | collective-permute-done | bytes 96 | tf_op jit(solution)/shard_map/ppermute | solution.py:165
  56.7 0.7 collective-permute-start.18
  57.4 0.0 collective-permute-done.far_ref
  57.4 1.3 %interpolate.5 = (f32[4,6,32,128]{3,2,1,0:T(8,128)S(1)}, bf16[4,6,32,128]{3,2,1,0:T(8,128)(2,1)S(1)}, bf16[4,6,32,128]{3,2,1,0:T(8,128)(2,1)S(1)}, bf16[4,6,32,128]{3,2,1,0:T(8,128)(2,1)S(1)}) custom-call(s32[16]{0:T(128)S(1)} %copy-done.2, s32[16]{0:T(128)S(1)} %collective-permute-done.4.targets, bf16[6,16,16384]{2,1,0:T(8,128)(2,1)S(1)} %copy-done, ...), custom_call_target="tpu_custom_call" | custom-call | flops 100663296 | bytes 2097152 | tf_op jit(solution)/shard_map/interpolate/pallas_call | solution.py:70
  58.7 1.6 %collective-permute-start.7 = (bf16[4,6,32,128]{3,2,1,0:T(8,128)(2,1)S(1)}, bf16[4,6,32,128]{3,2,1,0:T(8,128)(2,1)S(1)}, u32[]{:S(2)}, u32[]{:S(2)}) collective-permute-start(bf16[4,6,32,128]{3,2,1,0:T(8,128)(2,1)S(1)} %get-tuple-element.26), channel_id=1, source_target_pairs={{0,1},{1,0},{2,3},{3,2},{4,5},{5,4},{6,7},{7,6},{8,9},{9,8},{10,11... | collective-permute-start | bytes 589832 | tf_op jit(solution)/shard_map/ppermute | solution.py:184
  60.2 1.5 %collective-permute-start.8 = (bf16[4,6,32,128]{3,2,1,0:T(8,128)(2,1)S(1)}, bf16[4,6,32,128]{3,2,1,0:T(8,128)(2,1)S(1)}, u32[]{:S(2)}, u32[]{:S(2)}) collective-permute-start(bf16[4,6,32,128]{3,2,1,0:T(8,128)(2,1)S(1)} %get-tuple-element.27), channel_id=1, source_target_pairs={{0,2},{1,3},{2,0},{3,1},{4,6},{5,7},{6,4},{7,5},{8,10},{9,11},{10,... | collective-permute-start | bytes 589832 | tf_op jit(solution)/shard_map/ppermute | solution.py:184
  61.7 1.3 %interpolate.6 = (f32[4,6,32,128]{3,2,1,0:T(8,128)S(1)}, bf16[4,6,32,128]{3,2,1,0:T(8,128)(2,1)S(1)}, bf16[4,6,32,128]{3,2,1,0:T(8,128)(2,1)S(1)}, bf16[4,6,32,128]{3,2,1,0:T(8,128)(2,1)S(1)}) custom-call(s32[16]{0:T(128)S(1)} %copy-done.2, s32[16]{0:T(128)S(1)} %collective-permute-done.11.targets, bf16[6,16,16384]{2,1,0:T(8,128)(2,1)S(1)} %copy-done, ...), custom_call_target="tpu_custom_call" | custom-call | flops 100663296 | bytes 2097152 | tf_op jit(solution)/shard_map/interpolate/pallas_call | solution.py:70
  63.0 1.5 %collective-permute-start.9 = (bf16[4,6,32,128]{3,2,1,0:T(8,128)(2,1)S(1)}, bf16[4,6,32,128]{3,2,1,0:T(8,128)(2,1)S(1)}, u32[]{:S(2)}, u32[]{:S(2)}) collective-permute-start(bf16[4,6,32,128]{3,2,1,0:T(8,128)(2,1)S(1)} %get-tuple-element.28), channel_id=1, source_target_pairs={{0,3},{1,2},{2,1},{3,0},{4,7},{5,6},{6,5},{7,4},{8,11},{9,10},{10,... | collective-permute-start | bytes 589832 | tf_op jit(solution)/shard_map/ppermute | solution.py:184
  64.5 0.6 collective-permute-start.14
  65.1 1.5 %collective-permute-start.15 = (bf16[4,6,32,128]{3,2,1,0:T(8,128)(2,1)S(1)}, bf16[4,6,32,128]{3,2,1,0:T(8,128)(2,1)S(1)}, u32[]{:S(2)}, u32[]{:S(2)}) collective-permute-start(bf16[4,6,32,128]{3,2,1,0:T(8,128)(2,1)S(1)} %get-tuple-element.31), channel_id=1, source_target_pairs={{0,2},{1,3},{2,0},{3,1},{4,6},{5,7},{6,4},{7,5},{8,10},{9,11},{10,... | collective-permute-start | bytes 589832 | tf_op jit(solution)/shard_map/ppermute | solution.py:184
  66.6 1.3 %interpolate.7 = (f32[4,6,32,128]{3,2,1,0:T(8,128)S(1)}, bf16[4,6,32,128]{3,2,1,0:T(8,128)(2,1)S(1)}, bf16[4,6,32,128]{3,2,1,0:T(8,128)(2,1)S(1)}, bf16[4,6,32,128]{3,2,1,0:T(8,128)(2,1)S(1)}) custom-call(s32[16]{0:T(128)S(1)} %copy-done.2, s32[16]{0:T(128)S(1)} %collective-permute-done.18.targets, bf16[6,16,16384]{2,1,0:T(8,128)(2,1)S(1)} %copy-done, ...), custom_call_target="tpu_custom_call" | custom-call | flops 100663296 | bytes 2097152 | tf_op jit(solution)/shard_map/interpolate/pallas_call | solution.py:70
  67.9 1.5 %collective-permute-start.16 = (bf16[4,6,32,128]{3,2,1,0:T(8,128)(2,1)S(1)}, bf16[4,6,32,128]{3,2,1,0:T(8,128)(2,1)S(1)}, u32[]{:S(2)}, u32[]{:S(2)}) collective-permute-start(bf16[4,6,32,128]{3,2,1,0:T(8,128)(2,1)S(1)} %get-tuple-element.32), channel_id=1, source_target_pairs={{0,3},{1,2},{2,1},{3,0},{4,7},{5,6},{6,5},{7,4},{8,11},{9,10},{10,... | collective-permute-start | bytes 589832 | tf_op jit(solution)/shard_map/ppermute | solution.py:184
  69.3 2.9 %collective-permute-done.8.refs_2_ = bf16[4,6,32,128]{3,2,1,0:T(8,128)(2,1)S(1)} collective-permute-done((bf16[4,6,32,128]{3,2,1,0:T(8,128)(2,1)S(1)}, bf16[4,6,32,128]{3,2,1,0:T(8,128)(2,1)S(1)}, u32[]{:S(2)}, u32[]{:S(2)}) %collective-permute-start.8) | collective-permute-done | bytes 196640 | tf_op jit(solution)/shard_map/ppermute | solution.py:184
  72.3 1.8 %collective-permute-start.22 = (bf16[4,6,32,128]{3,2,1,0:T(8,128)(2,1)S(1)}, bf16[4,6,32,128]{3,2,1,0:T(8,128)(2,1)S(1)}, u32[]{:S(2)}, u32[]{:S(2)}) collective-permute-start(bf16[4,6,32,128]{3,2,1,0:T(8,128)(2,1)S(1)} %get-tuple-element.35), channel_id=1, source_target_pairs={{0,2},{1,3},{2,0},{3,1},{4,6},{5,7},{6,4},{7,5},{8,10},{9,11},{10,... | collective-permute-start | bytes 589832 | tf_op jit(solution)/shard_map/ppermute | solution.py:184
  74.1 1.0 collective-permute-done.14.refs_1_
  75.1 2.3 %collective-permute-start.23 = (bf16[4,6,32,128]{3,2,1,0:T(8,128)(2,1)S(1)}, bf16[4,6,32,128]{3,2,1,0:T(8,128)(2,1)S(1)}, u32[]{:S(2)}, u32[]{:S(2)}) collective-permute-start(bf16[4,6,32,128]{3,2,1,0:T(8,128)(2,1)S(1)} %get-tuple-element.36), channel_id=1, source_target_pairs={{0,3},{1,2},{2,1},{3,0},{4,7},{5,6},{6,5},{7,4},{8,11},{9,10},{10,... | collective-permute-start | bytes 589832 | tf_op jit(solution)/shard_map/ppermute | solution.py:184
  77.3 1.3 %interpolate.4 = (f32[4,6,32,128]{3,2,1,0:T(8,128)S(1)}, bf16[4,6,32,128]{3,2,1,0:T(8,128)(2,1)S(1)}, bf16[4,6,32,128]{3,2,1,0:T(8,128)(2,1)S(1)}, bf16[4,6,32,128]{3,2,1,0:T(8,128)(2,1)S(1)}) custom-call(s32[16]{0:T(128)S(1)} %copy-done.2, s32[16]{0:T(128)S(1)} %add_bitcast_fusion.targets, bf16[6,16,16384]{2,1,0:T(8,128)(2,1)S(1)} %copy-done, ...), custom_call_target="tpu_custom_call" | custom-call | flops 100663296 | bytes 2097152 | tf_op jit(solution)/shard_map/interpolate/pallas_call | solution.py:70
  78.6 2.1 %collective-permute-done.15.refs_2_ = bf16[4,6,32,128]{3,2,1,0:T(8,128)(2,1)S(1)} collective-permute-done((bf16[4,6,32,128]{3,2,1,0:T(8,128)(2,1)S(1)}, bf16[4,6,32,128]{3,2,1,0:T(8,128)(2,1)S(1)}, u32[]{:S(2)}, u32[]{:S(2)}) %collective-permute-start.15) | collective-permute-done | bytes 196640 | tf_op jit(solution)/shard_map/ppermute | solution.py:184
  80.7 0.1 total.5
  80.8 1.8 %collective-permute-start.2 = (bf16[4,6,32,128]{3,2,1,0:T(8,128)(2,1)S(1)}, bf16[4,6,32,128]{3,2,1,0:T(8,128)(2,1)S(1)}, u32[]{:S(2)}, u32[]{:S(2)}) collective-permute-start(bf16[4,6,32,128]{3,2,1,0:T(8,128)(2,1)S(1)} %get-tuple-element.23), channel_id=1, source_target_pairs={{0,2},{1,3},{2,0},{3,1},{4,6},{5,7},{6,4},{7,5},{8,10},{9,11},{10,... | collective-permute-start | bytes 589832 | tf_op jit(solution)/shard_map/ppermute | solution.py:184
  82.7 0.1 total.6
  82.7 0.0 copy-start.3
  82.8 0.8 collective-permute-done.21.refs_1_
  83.5 2.3 %collective-permute-start.3 = (bf16[4,6,32,128]{3,2,1,0:T(8,128)(2,1)S(1)}, bf16[4,6,32,128]{3,2,1,0:T(8,128)(2,1)S(1)}, u32[]{:S(2)}, u32[]{:S(2)}) collective-permute-start(bf16[4,6,32,128]{3,2,1,0:T(8,128)(2,1)S(1)} %get-tuple-element.24), channel_id=1, source_target_pairs={{0,3},{1,2},{2,1},{3,0},{4,7},{5,6},{6,5},{7,4},{8,11},{9,10},{10,... | collective-permute-start | bytes 589832 | tf_op jit(solution)/shard_map/ppermute | solution.py:184
  85.8 3.3 %collective-permute-done.22.refs_2_ = bf16[4,6,32,128]{3,2,1,0:T(8,128)(2,1)S(1)} collective-permute-done((bf16[4,6,32,128]{3,2,1,0:T(8,128)(2,1)S(1)}, bf16[4,6,32,128]{3,2,1,0:T(8,128)(2,1)S(1)}, u32[]{:S(2)}, u32[]{:S(2)}) %collective-permute-start.22) | collective-permute-done | bytes 196640 | tf_op jit(solution)/shard_map/ppermute | solution.py:184
  89.1 3.8 %collective-permute-start.17 = (bf16[4,6,32,128]{3,2,1,0:T(8,128)(2,1)S(1)}, bf16[4,6,32,128]{3,2,1,0:T(8,128)(2,1)S(1)}, u32[]{:S(2)}, u32[]{:S(2)}) collective-permute-start(bf16[4,6,32,128]{3,2,1,0:T(8,128)(2,1)S(1)} %total.6), channel_id=1, source_target_pairs={{0,16},{4,20},{8,24},{12,28},{16,0},{20,4},{24,8},{28,12},{1,17},{... | collective-permute-start | bytes 589832 | tf_op jit(solution)/shard_map/ppermute | solution.py:165
  92.9 0.1 total.7
  93.0 1.9 %collective-permute-start.24 = (bf16[4,6,32,128]{3,2,1,0:T(8,128)(2,1)S(1)}, bf16[4,6,32,128]{3,2,1,0:T(8,128)(2,1)S(1)}, u32[]{:S(2)}, u32[]{:S(2)}) collective-permute-start(bf16[4,6,32,128]{3,2,1,0:T(8,128)(2,1)S(1)} %total.7), channel_id=1, source_target_pairs={{0,24},{4,28},{8,16},{12,20},{16,8},{20,12},{24,0},{28,4},{1,25},{... | collective-permute-start | bytes 589832 | tf_op jit(solution)/shard_map/ppermute | solution.py:165
  94.9 0.3 collective-permute-done.2.refs_2_
  95.2 0.1 total.4.refs_0_
  95.3 1.8 %collective-permute-done.10.refs_1_ = bf16[4,6,32,128]{3,2,1,0:T(8,128)(2,1)S(1)} collective-permute-done((bf16[4,6,32,128]{3,2,1,0:T(8,128)(2,1)S(1)}, bf16[4,6,32,128]{3,2,1,0:T(8,128)(2,1)S(1)}, u32[]{:S(2)}, u32[]{:S(2)}) %collective-permute-start.10) | collective-permute-done | bytes 196640 | tf_op jit(solution)/shard_map/ppermute | solution.py:165
  97.1 5.1 %collective-permute-done.17.refs_2_ = bf16[4,6,32,128]{3,2,1,0:T(8,128)(2,1)S(1)} collective-permute-done((bf16[4,6,32,128]{3,2,1,0:T(8,128)(2,1)S(1)}, bf16[4,6,32,128]{3,2,1,0:T(8,128)(2,1)S(1)}, u32[]{:S(2)}, u32[]{:S(2)}) %collective-permute-start.17) | collective-permute-done | bytes 196640 | tf_op jit(solution)/shard_map/ppermute | solution.py:165
  102.2 1.5 %finish.1 = bf16[4,6,128,128]{3,2,1,0:T(8,128)(2,1)} custom-call(s32[16]{0:T(128)S(1)} %copy-done.2, f32[4,128]{1,0:T(4,128)S(1)} %copy-done.3, f32[4,6,32,128]{3,2,1,0:T(8,128)S(1)} %total.4.refs_0_, bf16[4,6,32,128]{3,2,1,0:T(8,128)(2,1)S(1)} %collective-permute-done.10.refs_1_, bf16[4,6,32,128]{3,2,1,0:T(8,128)(2,1)S(1)} %collective-permute-done.17.refs_2_, ...), custom_call_target="tpu_custom_call" | custom-call | tf_op jit(solution)/shard_map/finish/pallas_call | solution.py:129
  (26 shorter events, 0.1 us)
Async XLA Ops:
  1.2 42.3 %copy-start.4 = (s32[1,16,1]{1,2,0:T(1,128)S(1)}, s32[1,16,1]{1,2,0:T(1,128)}, u32[]{:S(2)}) copy-start(s32[1,16,1]{1,2,0:T(1,128)} %param.9) | copy-start | bytes 196
  1.2 42.3 %copy-start.5 = (s32[1,16,1]{1,2,0:T(1,128)S(1)}, s32[1,16,1]{1,2,0:T(1,128)}, u32[]{:S(2)}) copy-start(s32[1,16,1]{1,2,0:T(1,128)} %param.8) | copy-start | bytes 196
  1.2 56.2 %copy-start = (bf16[6,16,16384]{2,1,0:T(8,128)(2,1)S(1)}, bf16[6,16,16384]{2,1,0:T(8,128)(2,1)}, u32[]{:S(2)}) copy-start(bf16[6,16,16384]{2,1,0:T(8,128)(2,1)} %own_ref.7) | copy-start | bytes 9437188
  1.2 56.2 %copy-start.2 = (s32[16]{0:T(128)S(1)}, s32[16]{0:T(128)}, u32[]{:S(2)}) copy-start(s32[16]{0:T(128)} %dynamic-slice_bitcast_fusion.ids) | copy-start | bytes 196
  5.8 51.5 %collective-permute-start = (bf16[6,16,8192]{2,1,0:T(8,128)(2,1)}, bf16[6,16,8192]{2,1,0:T(8,128)(2,1)S(1)}, u32[]{:S(2)}, u32[]{:S(2)}) collective-permute-start(bf16[6,16,8192]{2,1,0:T(8,128)(2,1)} %pick.1), channel_id=1, source_target_pairs={{0,4},{4,0},{8,12},{12,8},{16,20},{20,16},{24,28},{28,24},{1,5},{5... | collective-permute-start | bytes 4718600 | tf_op jit(solution)/shard_map/ppermute | solution.py:175
  6.3 16.6 %collective-permute-start.5 = (bf16[16,128,128]{2,1,0:T(8,128)(2,1)}, bf16[16,128,128]{2,1,0:T(8,128)(2,1)S(1)}, u32[]{:S(2)}, u32[]{:S(2)}) collective-permute-start(bf16[16,128,128]{2,1,0:T(8,128)(2,1)} %bitcast.5), channel_id=1, source_target_pairs={{0,8},{4,12},{8,16},{12,20},{16,24},{20,28},{1,9},{5,13},{9,17},{1... | collective-permute-start | bytes 1572872 | tf_op jit(solution)/shard_map/ppermute | solution.py:165
  10.8 16.2 %collective-permute-start.6 = (bf16[16,128,128]{2,1,0:T(8,128)(2,1)}, bf16[16,128,128]{2,1,0:T(8,128)(2,1)S(1)}, u32[]{:S(2)}, u32[]{:S(2)}) collective-permute-start(bf16[16,128,128]{2,1,0:T(8,128)(2,1)} %bitcast.6), channel_id=1, source_target_pairs={{8,0},{12,4},{16,8},{20,12},{24,16},{28,20},{9,1},{13,5},{17,9},{2... | collective-permute-start | bytes 1572872 | tf_op jit(solution)/shard_map/ppermute | solution.py:165
  22.9 5.3 %collective-permute-start.12 = (bf16[16,128,128]{2,1,0:T(8,128)(2,1)S(1)}, bf16[16,128,128]{2,1,0:T(8,128)(2,1)S(1)}, u32[]{:S(2)}, u32[]{:S(2)}) collective-permute-start(bf16[16,128,128]{2,1,0:T(8,128)(2,1)S(1)} %collective-permute-done.5.rest_0_), channel_id=1, source_target_pairs={{8,16},{12,20},{16,24},{20,28},{9,17},{13,21},{17,25},{21,29},{10,... | collective-permute-start | bytes 1572872 | tf_op jit(solution)/shard_map/ppermute | solution.py:165
  27.0 15.3 %collective-permute-start.13 = (bf16[16,128,128]{2,1,0:T(8,128)(2,1)S(1)}, bf16[16,128,128]{2,1,0:T(8,128)(2,1)S(1)}, u32[]{:S(2)}, u32[]{:S(2)}) collective-permute-start(bf16[16,128,128]{2,1,0:T(8,128)(2,1)S(1)} %collective-permute-done.6.rest_1_.rest_2_), channel_id=1, source_target_pairs={{8,0},{12,4},{16,8},{20,12},{9,1},{13,5},{17,9},{21,13},{10,2},{14... | collective-permute-start | bytes 1572872 | tf_op jit(solution)/shard_map/ppermute | solution.py:165
  28.2 36.2 %collective-permute-start.19 = (bf16[16,128,128]{2,1,0:T(8,128)(2,1)S(1)}, bf16[16,128,128]{2,1,0:T(8,128)(2,1)S(1)}, u32[]{:S(2)}, u32[]{:S(2)}) collective-permute-start(bf16[16,128,128]{2,1,0:T(8,128)(2,1)S(1)} %collective-permute-done.12.rest_0_), channel_id=1, source_target_pairs={{16,24},{20,28},{17,25},{21,29},{18,26},{22,30},{19,27},{23,31}} | collective-permute-start | bytes 1572872 | tf_op jit(solution)/shard_map/ppermute | solution.py:165
  42.2 22.8 %collective-permute-start.20 = (bf16[16,128,128]{2,1,0:T(8,128)(2,1)S(1)}, bf16[16,128,128]{2,1,0:T(8,128)(2,1)S(1)}, u32[]{:S(2)}, u32[]{:S(2)}) collective-permute-start(bf16[16,128,128]{2,1,0:T(8,128)(2,1)S(1)} %collective-permute-done.13.rest_1_), channel_id=1, source_target_pairs={{8,0},{12,4},{9,1},{13,5},{10,2},{14,6},{11,3},{15,7}} | collective-permute-start | bytes 1572872 | tf_op jit(solution)/shard_map/ppermute | solution.py:165
  43.6 13.1 %collective-permute-start.4 = (s32[16]{0:T(128)S(1)}, s32[16]{0:T(128)S(1)}, u32[]{:S(2)}, u32[]{:S(2)}) collective-permute-start(s32[16]{0:T(128)S(1)} %add_bitcast_fusion.targets), channel_id=1, source_target_pairs={{0,8},{4,12},{8,0},{12,4},{16,24},{20,28},{24,16},{28,20},{1,9},{5... | collective-permute-start | bytes 200 | tf_op jit(solution)/shard_map/ppermute | solution.py:165
  46.3 13.9 %collective-permute-start.11 = (s32[16]{0:T(128)S(1)}, s32[16]{0:T(128)S(1)}, u32[]{:S(2)}, u32[]{:S(2)}) collective-permute-start(s32[16]{0:T(128)S(1)} %add_bitcast_fusion.targets), channel_id=1, source_target_pairs={{0,16},{4,20},{8,24},{12,28},{16,0},{20,4},{24,8},{28,12},{1,17},{... | collective-permute-start | bytes 200 | tf_op jit(solution)/shard_map/ppermute | solution.py:165
  56.7 6.3 %collective-permute-start.18 = (s32[16]{0:T(128)S(1)}, s32[16]{0:T(128)S(1)}, u32[]{:S(2)}, u32[]{:S(2)}) collective-permute-start(s32[16]{0:T(128)S(1)} %add_bitcast_fusion.targets), channel_id=1, source_target_pairs={{0,24},{4,28},{8,16},{12,20},{16,8},{20,12},{24,0},{28,4},{1,25},{... | collective-permute-start | bytes 200 | tf_op jit(solution)/shard_map/ppermute | solution.py:165
  58.7 9.2 %collective-permute-start.7 = (bf16[4,6,32,128]{3,2,1,0:T(8,128)(2,1)S(1)}, bf16[4,6,32,128]{3,2,1,0:T(8,128)(2,1)S(1)}, u32[]{:S(2)}, u32[]{:S(2)}) collective-permute-start(bf16[4,6,32,128]{3,2,1,0:T(8,128)(2,1)S(1)} %get-tuple-element.26), channel_id=1, source_target_pairs={{0,1},{1,0},{2,3},{3,2},{4,5},{5,4},{6,7},{7,6},{8,9},{9,8},{10,11... | collective-permute-start | bytes 589832 | tf_op jit(solution)/shard_map/ppermute | solution.py:184
  60.2 12.1 %collective-permute-start.8 = (bf16[4,6,32,128]{3,2,1,0:T(8,128)(2,1)S(1)}, bf16[4,6,32,128]{3,2,1,0:T(8,128)(2,1)S(1)}, u32[]{:S(2)}, u32[]{:S(2)}) collective-permute-start(bf16[4,6,32,128]{3,2,1,0:T(8,128)(2,1)S(1)} %get-tuple-element.27), channel_id=1, source_target_pairs={{0,2},{1,3},{2,0},{3,1},{4,6},{5,7},{6,4},{7,5},{8,10},{9,11},{10,... | collective-permute-start | bytes 589832 | tf_op jit(solution)/shard_map/ppermute | solution.py:184
  63.0 9.3 %collective-permute-start.9 = (bf16[4,6,32,128]{3,2,1,0:T(8,128)(2,1)S(1)}, bf16[4,6,32,128]{3,2,1,0:T(8,128)(2,1)S(1)}, u32[]{:S(2)}, u32[]{:S(2)}) collective-permute-start(bf16[4,6,32,128]{3,2,1,0:T(8,128)(2,1)S(1)} %get-tuple-element.28), channel_id=1, source_target_pairs={{0,3},{1,2},{2,1},{3,0},{4,7},{5,6},{6,5},{7,4},{8,11},{9,10},{10,... | collective-permute-start | bytes 589832 | tf_op jit(solution)/shard_map/ppermute | solution.py:184
  64.5 10.6 %collective-permute-start.14 = (bf16[4,6,32,128]{3,2,1,0:T(8,128)(2,1)S(1)}, bf16[4,6,32,128]{3,2,1,0:T(8,128)(2,1)S(1)}, u32[]{:S(2)}, u32[]{:S(2)}) collective-permute-start(bf16[4,6,32,128]{3,2,1,0:T(8,128)(2,1)S(1)} %get-tuple-element.30), channel_id=1, source_target_pairs={{0,1},{1,0},{2,3},{3,2},{4,5},{5,4},{6,7},{7,6},{8,9},{9,8},{10,11... | collective-permute-start | bytes 589832 | tf_op jit(solution)/shard_map/ppermute | solution.py:184
  65.1 12.3 %copy-start.1 = (bf16[1,16,128,128]{3,2,1,0:T(8,128)(2,1)S(1)}, bf16[1,16,128,128]{3,2,1,0:T(8,128)(2,1)}, u32[]{:S(2)}) copy-start(bf16[1,16,128,128]{3,2,1,0:T(8,128)(2,1)} %param.7) | copy-start | bytes 1572868
  65.1 15.6 %collective-permute-start.15 = (bf16[4,6,32,128]{3,2,1,0:T(8,128)(2,1)S(1)}, bf16[4,6,32,128]{3,2,1,0:T(8,128)(2,1)S(1)}, u32[]{:S(2)}, u32[]{:S(2)}) collective-permute-start(bf16[4,6,32,128]{3,2,1,0:T(8,128)(2,1)S(1)} %get-tuple-element.31), channel_id=1, source_target_pairs={{0,2},{1,3},{2,0},{3,1},{4,6},{5,7},{6,4},{7,5},{8,10},{9,11},{10,... | collective-permute-start | bytes 589832 | tf_op jit(solution)/shard_map/ppermute | solution.py:184
  67.9 12.9 %collective-permute-start.16 = (bf16[4,6,32,128]{3,2,1,0:T(8,128)(2,1)S(1)}, bf16[4,6,32,128]{3,2,1,0:T(8,128)(2,1)S(1)}, u32[]{:S(2)}, u32[]{:S(2)}) collective-permute-start(bf16[4,6,32,128]{3,2,1,0:T(8,128)(2,1)S(1)} %get-tuple-element.32), channel_id=1, source_target_pairs={{0,3},{1,2},{2,1},{3,0},{4,7},{5,6},{6,5},{7,4},{8,11},{9,10},{10,... | collective-permute-start | bytes 589832 | tf_op jit(solution)/shard_map/ppermute | solution.py:184
  72.3 11.2 %collective-permute-start.21 = (bf16[4,6,32,128]{3,2,1,0:T(8,128)(2,1)S(1)}, bf16[4,6,32,128]{3,2,1,0:T(8,128)(2,1)S(1)}, u32[]{:S(2)}, u32[]{:S(2)}) collective-permute-start(bf16[4,6,32,128]{3,2,1,0:T(8,128)(2,1)S(1)} %get-tuple-element.34), channel_id=1, source_target_pairs={{0,1},{1,0},{2,3},{3,2},{4,5},{5,4},{6,7},{7,6},{8,9},{9,8},{10,11... | collective-permute-start | bytes 589832 | tf_op jit(solution)/shard_map/ppermute | solution.py:184
  72.3 16.8 %collective-permute-start.22 = (bf16[4,6,32,128]{3,2,1,0:T(8,128)(2,1)S(1)}, bf16[4,6,32,128]{3,2,1,0:T(8,128)(2,1)S(1)}, u32[]{:S(2)}, u32[]{:S(2)}) collective-permute-start(bf16[4,6,32,128]{3,2,1,0:T(8,128)(2,1)S(1)} %get-tuple-element.35), channel_id=1, source_target_pairs={{0,2},{1,3},{2,0},{3,1},{4,6},{5,7},{6,4},{7,5},{8,10},{9,11},{10,... | collective-permute-start | bytes 589832 | tf_op jit(solution)/shard_map/ppermute | solution.py:184
  75.1 14.1 %collective-permute-start.23 = (bf16[4,6,32,128]{3,2,1,0:T(8,128)(2,1)S(1)}, bf16[4,6,32,128]{3,2,1,0:T(8,128)(2,1)S(1)}, u32[]{:S(2)}, u32[]{:S(2)}) collective-permute-start(bf16[4,6,32,128]{3,2,1,0:T(8,128)(2,1)S(1)} %get-tuple-element.36), channel_id=1, source_target_pairs={{0,3},{1,2},{2,1},{3,0},{4,7},{5,6},{6,5},{7,4},{8,11},{9,10},{10,... | collective-permute-start | bytes 589832 | tf_op jit(solution)/shard_map/ppermute | solution.py:184
  80.7 12.3 %collective-permute-start.1 = (bf16[4,6,32,128]{3,2,1,0:T(8,128)(2,1)S(1)}, bf16[4,6,32,128]{3,2,1,0:T(8,128)(2,1)S(1)}, u32[]{:S(2)}, u32[]{:S(2)}) collective-permute-start(bf16[4,6,32,128]{3,2,1,0:T(8,128)(2,1)S(1)} %get-tuple-element.22), channel_id=1, source_target_pairs={{0,1},{1,0},{2,3},{3,2},{4,5},{5,4},{6,7},{7,6},{8,9},{9,8},{10,11... | collective-permute-start | bytes 589832 | tf_op jit(solution)/shard_map/ppermute | solution.py:184
  80.8 14.4 %collective-permute-start.2 = (bf16[4,6,32,128]{3,2,1,0:T(8,128)(2,1)S(1)}, bf16[4,6,32,128]{3,2,1,0:T(8,128)(2,1)S(1)}, u32[]{:S(2)}, u32[]{:S(2)}) collective-permute-start(bf16[4,6,32,128]{3,2,1,0:T(8,128)(2,1)S(1)} %get-tuple-element.23), channel_id=1, source_target_pairs={{0,2},{1,3},{2,0},{3,1},{4,6},{5,7},{6,4},{7,5},{8,10},{9,11},{10,... | collective-permute-start | bytes 589832 | tf_op jit(solution)/shard_map/ppermute | solution.py:184
  82.7 19.5 %copy-start.3 = (f32[4,128]{1,0:T(4,128)S(1)}, f32[4,128]{1,0:T(4,128)}, u32[]{:S(2)}) copy-start(f32[4,128]{1,0:T(4,128)} %weight_ref.1) | copy-start | bytes 6148
  83.5 11.7 %collective-permute-start.3 = (bf16[4,6,32,128]{3,2,1,0:T(8,128)(2,1)S(1)}, bf16[4,6,32,128]{3,2,1,0:T(8,128)(2,1)S(1)}, u32[]{:S(2)}, u32[]{:S(2)}) collective-permute-start(bf16[4,6,32,128]{3,2,1,0:T(8,128)(2,1)S(1)} %get-tuple-element.24), channel_id=1, source_target_pairs={{0,3},{1,2},{2,1},{3,0},{4,7},{5,6},{6,5},{7,4},{8,11},{9,10},{10,... | collective-permute-start | bytes 589832 | tf_op jit(solution)/shard_map/ppermute | solution.py:184
  89.1 8.0 %collective-permute-start.10 = (bf16[4,6,32,128]{3,2,1,0:T(8,128)(2,1)S(1)}, bf16[4,6,32,128]{3,2,1,0:T(8,128)(2,1)S(1)}, u32[]{:S(2)}, u32[]{:S(2)}) collective-permute-start(bf16[4,6,32,128]{3,2,1,0:T(8,128)(2,1)S(1)} %total.5), channel_id=1, source_target_pairs={{0,8},{4,12},{8,0},{12,4},{16,24},{20,28},{24,16},{28,20},{1,9},{5... | collective-permute-start | bytes 589832 | tf_op jit(solution)/shard_map/ppermute | solution.py:165
  89.1 13.1 %collective-permute-start.17 = (bf16[4,6,32,128]{3,2,1,0:T(8,128)(2,1)S(1)}, bf16[4,6,32,128]{3,2,1,0:T(8,128)(2,1)S(1)}, u32[]{:S(2)}, u32[]{:S(2)}) collective-permute-start(bf16[4,6,32,128]{3,2,1,0:T(8,128)(2,1)S(1)} %total.6), channel_id=1, source_target_pairs={{0,16},{4,20},{8,24},{12,28},{16,0},{20,4},{24,8},{28,12},{1,17},{... | collective-permute-start | bytes 589832 | tf_op jit(solution)/shard_map/ppermute | solution.py:165
  93.0 9.2 %collective-permute-start.24 = (bf16[4,6,32,128]{3,2,1,0:T(8,128)(2,1)S(1)}, bf16[4,6,32,128]{3,2,1,0:T(8,128)(2,1)S(1)}, u32[]{:S(2)}, u32[]{:S(2)}) collective-permute-start(bf16[4,6,32,128]{3,2,1,0:T(8,128)(2,1)S(1)} %total.7), channel_id=1, source_target_pairs={{0,24},{4,28},{8,16},{12,20},{16,8},{20,12},{24,0},{28,4},{1,25},{... | collective-permute-start | bytes 589832 | tf_op jit(solution)/shard_map/ppermute | solution.py:165

commit v2 on v0

v2 whole, which is shorter than its diff:
```python
import functools

import jax
import jax.numpy as jnp
from jax import lax
from jax.experimental import pallas as pl
from jax.experimental.pallas import tpu as pltpu
from jax.sharding import PartitionSpec as P

CORES = 2
TAIL = 16
LIMIT = pltpu.CompilerParams(vmem_limit_bytes=32 * 2**20)


def place():
    me = lax.axis_index("tm")
    return me // CORES, lax.rem(me, CORES), lax.axis_index("box")


def pack_kernel(slots, mats_ref, owner_ref, slot_ref, out_ref):
    rows, nodes = mats_ref.shape
    blocks = owner_ref.shape[1]
    out_ref[:rows, :] = mats_ref[...]
    target = (owner_ref[...] * slots + slot_ref[...]).astype(jnp.float32)
    row = jnp.concatenate([target, jnp.zeros((1, nodes - blocks), jnp.float32)], axis=1)
    out_ref[rows:, :] = jnp.broadcast_to(row, (TAIL, nodes)).astype(out_ref.dtype)


def pack(matrices, owners, slot_of, slots):
    rows, nodes = matrices.shape
    return pl.pallas_call(
        functools.partial(pack_kernel, slots),
        out_shape=jax.ShapeDtypeStruct((rows + TAIL, nodes), matrices.dtype),
        name="pack",
    )(matrices, owners, slot_of)


def interpolate_kernel(turn, boxes, blocks, own_hbm, far_hbm, mats_hbm, *rest):
    outs, (own, far, mats, acc, sems) = rest[:boxes], rest[boxes:]
    chip, core, box = place()
    comp, samples, width = own.shape
    nodes = mats.shape[1]
    slots = acc.shape[0] // boxes
    at = pl.ds(pl.multiple_of(((chip ^ turn) * CORES + core) * width, width), width)
    copies = [
        pltpu.make_async_copy(mats_hbm, mats, sems.at[0]),
        pltpu.make_async_copy(own_hbm.at[:, :, at], own, sems.at[1]),
        pltpu.make_async_copy(far_hbm.at[:, :, at], far, sems.at[2]),
    ]
    for copy in copies:
        copy.start()
    acc[...] = jnp.zeros_like(acc)
    for copy in copies:
        copy.wait()
    named = mats[blocks * nodes:, :].astype(jnp.float32)
    for j in range(blocks):
        target = named[0, j].astype(jnp.int32)
        for ref, half in ((own, core), (far, 1 - core)):
            x = ref[:, :, j * nodes:(j + 1) * nodes]
            if samples % 16:
                x = x.astype(jnp.float32).reshape(comp * samples, nodes).astype(x.dtype)
            else:
                x = x.reshape(comp * samples, nodes)
            y = jnp.dot(x, mats[j * nodes:(j + 1) * nodes, :], preferred_element_type=jnp.float32)
            acc[target, :, half] += y.reshape(comp, samples, nodes)
    for d, out in enumerate(outs):
        for s in range(slots):
            part = acc[(box ^ d) * slots + s]
            out[s] = part.reshape(comp, CORES * samples, nodes).astype(out.dtype)


def interpolate(turn, traces, far, mats, blocks, boxes, slots):
    nodes = mats.shape[1]
    comp, samples, _ = traces.shape
    width = blocks * nodes
    shape = (slots, comp, CORES * samples, nodes)
    return pl.pallas_call(
        functools.partial(interpolate_kernel, turn, boxes, blocks),
        in_specs=[pl.BlockSpec(memory_space=pl.ANY)] * 3,
        out_specs=[pl.BlockSpec(memory_space=pltpu.VMEM)] * boxes,
        scratch_shapes=[
            pltpu.VMEM((comp, samples, width), traces.dtype),
            pltpu.VMEM((comp, samples, width), traces.dtype),
            pltpu.VMEM(mats.shape, mats.dtype),
            pltpu.VMEM((boxes * slots, comp, CORES, samples, nodes), jnp.float32),
            pltpu.SemaphoreType.DMA((3,)),
        ],
        out_shape=[
            jax.ShapeDtypeStruct(shape, jnp.bfloat16 if d else jnp.float32) for d in range(boxes)
        ],
        compiler_params=LIMIT,
        name="interpolate",
    )(traces, far, mats)


def total_kernel(*refs):
    out = refs[-1]
    for s in range(out.shape[0]):
        value = refs[0][s]
        for ref in refs[1:-1]:
            value = value + ref[s].astype(jnp.float32)
        out[s] = value.astype(out.dtype)


def total(parts, dtype):
    return pl.pallas_call(
        total_kernel,
        out_shape=jax.ShapeDtypeStruct(parts[0].shape, dtype),
        compiler_params=LIMIT,
        name="total",
    )(*parts)


def finish_kernel(weight_ref, *refs):
    out = refs[-1]
    chip, _, _ = place()
    slots, _, length, _ = refs[0].shape
    for turn, ref in enumerate(refs[:-1]):
        at = pl.ds(pl.multiple_of((chip ^ turn) * length, length), length)
        for s in range(slots):
            value = ref[s].astype(jnp.float32) * weight_ref[s:s + 1, :][None]
            out[s, :, at, :] = value.astype(out.dtype)


def finish(weight, pieces):
    slots, comp, length, nodes = pieces[0].shape
    return pl.pallas_call(
        finish_kernel,
        out_shape=jax.ShapeDtypeStruct((slots, comp, length * len(pieces), nodes), jnp.bfloat16),
        compiler_params=LIMIT,
        name="finish",
    )(weight, *pieces)


def per_device(chips, boxes, traces, projection, owner_route, face_slot, face_weight):
    _, blocks, nodes, _ = projection.shape
    slots = face_weight.shape[0]

    def turned(x, r):
        pairs = [(z * CORES + c, (z ^ r) * CORES + c) for z in range(chips) for c in range(CORES)]
        return lax.ppermute(x, "tm", pairs)

    mats = pack(
        projection.reshape(blocks * nodes, nodes),
        owner_route.reshape(1, blocks), face_slot.reshape(1, blocks), slots,
    )
    far = lax.ppermute(traces, "tm", [(i, i ^ 1) for i in range(chips * CORES)])
    barrier = lax.optimization_barrier

    def crossed(r, mats):
        parts = interpolate(r, traces, far, mats, blocks, boxes, slots)
        return [parts[0]] + [
            lax.ppermute(parts[d], "box", [(b, b ^ d) for b in range(boxes)]) for d in range(1, boxes)
        ]

    pieces = {0: total(crossed(0, mats), jnp.float32)}
    first, arrived = turned(mats, 1), None
    for r in range(2, chips, 2):
        even = turned(mats, r)
        even, first, pieces[r - 2] = barrier((even, first, pieces[r - 2]))
        odd = turned(even, 1)
        parts = crossed(r, even)
        if r == 2:
            late = crossed(1, first)
        summed = total(parts, jnp.bfloat16)
        odd, summed = barrier((odd, summed))
        pieces[r] = turned(summed, r)
        parts = crossed(r + 1, odd)
        if r == 2:
            late[0], parts[0] = barrier((late[0], parts[0]))
            pieces[1] = turned(total(late, jnp.bfloat16), 1)
        pieces[r], parts[0] = barrier((pieces[r], parts[0]))
        pieces[r + 1] = turned(total(parts, jnp.bfloat16), r + 1)
    return finish(face_weight, [pieces[r] for r in range(chips)])


def solution(mesh):
    chips, boxes = mesh.shape["tm"] // CORES, mesh.shape["box"]
    return jax.shard_map(
        functools.partial(per_device, chips, boxes),
        mesh=mesh,
        in_specs=(
            P(None, "tm", "box"),
            P("box", "tm", None, None),
            P("box", "tm", None),
            P("box", "tm", None),
            P(("tm", "box"), None),
        ),
        out_specs=P(("tm", "box"), None, None, None),
        check_vma=False,
    )
```

time: 271 us -> 71.1 us (0.26)
  local copies, waits for them, and re-layouts: 128 us -> 2.94 us
  waiting for transfers between devices: 116 us -> 34.3 us
  starting transfers between devices: 15.3 us -> 27 us
  matrix products: 9.08 us -> 0 us
  Pallas kernels: 0 us -> 6.32 us
    all_to_all x3 -> x0, waiting for transfers between devices: 116 us -> none  [the longest x1 71.3 us: per_device(): lax.all_to_all(traces, 'tm', split_axis=2, concat_axis=1, tiled=True)]
    unnamed x12 -> x8, local copies, waits for them, and re-layouts: 92.7 us -> 2.94 us
    ppermute x0 -> x19, waiting for transfers between devices: none -> 34.3 us  [the longest x12 20.8 us: crossed(): lax.ppermute(parts[d], 'box', [(b, b ^ d) for b in range(boxes)])]
    all_to_all x1 -> x0, local copies, waits for them, and re-layouts: 31 us -> none  [per_device(): lax.all_to_all(traces, 'tm', split_axis=2, concat_axis=1, tiled=True)]
    ppermute x0 -> x19, starting transfers between devices: none -> 27 us  [the longest x12 15.5 us: crossed(): lax.ppermute(parts[d], 'box', [(b, b ^ d) for b in range(boxes)])]
    all_to_all x3 -> x0, starting transfers between devices: 15.3 us -> none  [the longest x1 6.46 us: per_device(): lax.all_to_all(traces, 'tm', split_axis=2, concat_axis=1, tiled=True)]
    dot_general x3 -> x0, matrix products: 9.08 us -> none  [the longest x1 5.81 us: per_device(): jnp.einsum('fks,kcsn->fcsn', placing, flat, preferred_element_type=jnp.fl...]
    pallas_call x0 -> x10, Pallas kernels: none -> 6.32 us  [the longest x4 3.05 us: interpolate(): pl.pallas_call(functools.partial(interpolate_kernel, turn, boxes, blocks)...]
  transfers between devices with their start and end apart: 3 -> 19, of which waited for: 2 -> 12; matrix products, arithmetic and copies ran while one was open for 27% -> 0% of each run, Pallas kernels for 0% -> 8%
where the time goes in v2:
time: 71.1 us; the launch traced here: 70.6 us
  waiting for transfers between devices  34.3 us (48%)
  starting transfers between devices  27 us (38%)
  Pallas kernels  6.32 us (9%)
  local copies, waits for them, and re-layouts  2.94 us (4%)
    ppermute x12, waiting for transfers between devices, crossed(): lax.ppermute(parts[d], 'box', [(b, b ^ d) for b in range(boxes)])  20.8 us
    ppermute x12, starting transfers between devices, crossed(): lax.ppermute(parts[d], 'box', [(b, b ^ d) for b in range(boxes)])  15.5 us
    ppermute x6, waiting for transfers between devices, turned(): return lax.ppermute(x, 'tm', pairs)  13.5 us
    ppermute x6, starting transfers between devices, turned(): return lax.ppermute(x, 'tm', pairs)  11 us
    pallas_call x4, Pallas kernels, interpolate(): pl.pallas_call(functools.partial(interpolate_kernel, turn, boxes, blocks)...  3.05 us
    unnamed x8, local copies, waits for them, and re-layouts  2.94 us
    pallas_call x1, Pallas kernels, pack(): pl.pallas_call(functools.partial(pack_kernel, slots), out_shape=jax.Shape...  1.89 us
  transfers between devices with their start and end apart: 19, of which 12 were waited for; matrix products, arithmetic and copies ran while one was open for 0% of the time, Pallas kernels for 8%

profile of v2, /device:TPU:0, one launch (start us, length us, event | category | flops | bytes accessed | tf_op | source)
XLA Modules:
  0.0 70.6 jit_solution(16569402006889910989)
XLA Ops:
  0.0 0.5 collective-permute-start.2
  0.5 1.9 %pack.1.mats_hbm = bf16[2064,128]{1,0:T(8,128)(2,1)} custom-call(bf16[2048,128]{1,0:T(8,128)(2,1)} %bitcast.3, s32[1,16]{1,0:T(1,128)} %bitcast.4, s32[1,16]{1,0:T(1,128)} %bitcast.5), custom_call_target="tpu_custom_call" | custom-call | tf_op jit(solution)/shard_map/pack/pallas_call | solution.py:31
  2.3 3.6 %collective-permute-start = (bf16[2064,128]{1,0:T(8,128)(2,1)}, bf16[2064,128]{1,0:T(8,128)(2,1)S(1)}, u32[]{:S(2)}, u32[]{:S(2)}) collective-permute-start(bf16[2064,128]{1,0:T(8,128)(2,1)} %pack.1.mats_hbm), channel_id=1, source_target_pairs={{0,16},{4,20},{8,24},{12,28},{16,0},{20,4},{24,8},{28,12},{1,17},{... | collective-permute-start | bytes 1585160 | tf_op jit(solution)/shard_map/ppermute | solution.py:141
  5.9 1.6 %collective-permute-start.1 = (bf16[2064,128]{1,0:T(8,128)(2,1)}, bf16[2064,128]{1,0:T(8,128)(2,1)S(1)}, u32[]{:S(2)}, u32[]{:S(2)}) collective-permute-start(bf16[2064,128]{1,0:T(8,128)(2,1)} %pack.1.mats_hbm), channel_id=1, source_target_pairs={{0,8},{4,12},{8,0},{12,4},{16,24},{20,28},{24,16},{28,20},{1,9},{5... | collective-permute-start | bytes 1585160 | tf_op jit(solution)/shard_map/ppermute | solution.py:141
  7.5 1.9 %copy-done = bf16[6,16,16384]{2,1,0:T(8,128)(2,1)S(1)} copy-done((bf16[6,16,16384]{2,1,0:T(8,128)(2,1)S(1)}, bf16[6,16,16384]{2,1,0:T(8,128)(2,1)}, u32[]{:S(2)}) %copy-start) | copy-done | bytes 3145752
  9.4 1.0 %copy-done.2 = bf16[2064,128]{1,0:T(8,128)(2,1)S(1)} copy-done((bf16[2064,128]{1,0:T(8,128)(2,1)S(1)}, bf16[2064,128]{1,0:T(8,128)(2,1)}, u32[]{:S(2)}) %copy-start.2) | copy-done | bytes 528408
  10.5 0.8 %interpolate.4 = (f32[4,6,32,128]{3,2,1,0:T(8,128)S(1)}, bf16[4,6,32,128]{3,2,1,0:T(8,128)(2,1)S(1)}, bf16[4,6,32,128]{3,2,1,0:T(8,128)(2,1)S(1)}, bf16[4,6,32,128]{3,2,1,0:T(8,128)(2,1)S(1)}) custom-call(bf16[6,16,16384]{2,1,0:T(8,128)(2,1)S(1)} %copy-done, bf16[6,16,16384]{2,1,0:T(8,128)(2,1)S(1)} %collective-permute-done.2.far_hbm, ...), custom_call_target="tpu_custom_call" | custom-call | tf_op jit(solution)/shard_map/interpolate/pallas_call | solution.py:77
  11.2 1.6 %collective-permute-start.3 = (bf16[4,6,32,128]{3,2,1,0:T(8,128)(2,1)S(1)}, bf16[4,6,32,128]{3,2,1,0:T(8,128)(2,1)S(1)}, u32[]{:S(2)}, u32[]{:S(2)}) collective-permute-start(bf16[4,6,32,128]{3,2,1,0:T(8,128)(2,1)S(1)} %get-tuple-element.31), channel_id=1, source_target_pairs={{0,1},{1,0},{2,3},{3,2},{4,5},{5,4},{6,7},{7,6},{8,9},{9,8},{10,11... | collective-permute-start | bytes 589832 | tf_op jit(solution)/shard_map/ppermute | solution.py:153
  12.8 1.5 %collective-permute-start.4 = (bf16[4,6,32,128]{3,2,1,0:T(8,128)(2,1)S(1)}, bf16[4,6,32,128]{3,2,1,0:T(8,128)(2,1)S(1)}, u32[]{:S(2)}, u32[]{:S(2)}) collective-permute-start(bf16[4,6,32,128]{3,2,1,0:T(8,128)(2,1)S(1)} %get-tuple-element.32), channel_id=1, source_target_pairs={{0,2},{1,3},{2,0},{3,1},{4,6},{5,7},{6,4},{7,5},{8,10},{9,11},{10,... | collective-permute-start | bytes 589832 | tf_op jit(solution)/shard_map/ppermute | solution.py:153
  14.3 0.5 collective-permute-start.5
  14.8 4.3 %collective-permute-done.3.refs_1_ = bf16[4,6,32,128]{3,2,1,0:T(8,128)(2,1)S(1)} collective-permute-done((bf16[4,6,32,128]{3,2,1,0:T(8,128)(2,1)S(1)}, bf16[4,6,32,128]{3,2,1,0:T(8,128)(2,1)S(1)}, u32[]{:S(2)}, u32[]{:S(2)}) %collective-permute-start.3) | collective-permute-done | bytes 196640 | tf_op jit(solution)/shard_map/ppermute | solution.py:153
  19.1 4.4 %collective-permute-done.4.refs_2_ = bf16[4,6,32,128]{3,2,1,0:T(8,128)(2,1)S(1)} collective-permute-done((bf16[4,6,32,128]{3,2,1,0:T(8,128)(2,1)S(1)}, bf16[4,6,32,128]{3,2,1,0:T(8,128)(2,1)S(1)}, u32[]{:S(2)}, u32[]{:S(2)}) %collective-permute-start.4) | collective-permute-done | bytes 196640 | tf_op jit(solution)/shard_map/ppermute | solution.py:153
  23.5 0.1 total.4.refs_0_
  23.6 6.7 %collective-permute-done.mats_hbm = bf16[2064,128]{1,0:T(8,128)(2,1)S(1)} collective-permute-done((bf16[2064,128]{1,0:T(8,128)(2,1)}, bf16[2064,128]{1,0:T(8,128)(2,1)S(1)}, u32[]{:S(2)}, u32[]{:S(2)}) %collective-permute-start) | collective-permute-done | bytes 528416 | tf_op jit(solution)/shard_map/ppermute | solution.py:141
  30.3 0.2 collective-permute-done.1.mats_hbm
  30.4 1.5 %collective-permute-start.6 = (bf16[2064,128]{1,0:T(8,128)(2,1)S(1)}, bf16[2064,128]{1,0:T(8,128)(2,1)S(1)}, u32[]{:S(2)}, u32[]{:S(2)}) collective-permute-start(bf16[2064,128]{1,0:T(8,128)(2,1)S(1)} %collective-permute-done.mats_hbm), channel_id=1, source_target_pairs={{0,8},{4,12},{8,0},{12,4},{16,24},{20,28},{24,16},{28,20},{1,9},{5... | collective-permute-start | bytes 1585160 | tf_op jit(solution)/shard_map/ppermute | solution.py:141
  31.9 0.8 %interpolate.6 = (f32[4,6,32,128]{3,2,1,0:T(8,128)S(1)}, bf16[4,6,32,128]{3,2,1,0:T(8,128)(2,1)S(1)}, bf16[4,6,32,128]{3,2,1,0:T(8,128)(2,1)S(1)}, bf16[4,6,32,128]{3,2,1,0:T(8,128)(2,1)S(1)}) custom-call(bf16[6,16,16384]{2,1,0:T(8,128)(2,1)S(1)} %copy-done.1, bf16[6,16,16384]{2,1,0:T(8,128)(2,1)S(1)} %collective-permute-done.2.far_hbm, ...), custom_call_target="tpu_custom_call" | custom-call | tf_op jit(solution)/shard_map/interpolate/pallas_call | solution.py:77
  32.7 1.6 %collective-permute-start.7 = (bf16[4,6,32,128]{3,2,1,0:T(8,128)(2,1)S(1)}, bf16[4,6,32,128]{3,2,1,0:T(8,128)(2,1)S(1)}, u32[]{:S(2)}, u32[]{:S(2)}) collective-permute-start(bf16[4,6,32,128]{3,2,1,0:T(8,128)(2,1)S(1)} %get-tuple-element.39), channel_id=1, source_target_pairs={{0,1},{1,0},{2,3},{3,2},{4,5},{5,4},{6,7},{7,6},{8,9},{9,8},{10,11... | collective-permute-start | bytes 589832 | tf_op jit(solution)/shard_map/ppermute | solution.py:153
  34.3 1.5 %collective-permute-start.8 = (bf16[4,6,32,128]{3,2,1,0:T(8,128)(2,1)S(1)}, bf16[4,6,32,128]{3,2,1,0:T(8,128)(2,1)S(1)}, u32[]{:S(2)}, u32[]{:S(2)}) collective-permute-start(bf16[4,6,32,128]{3,2,1,0:T(8,128)(2,1)S(1)} %get-tuple-element.40), channel_id=1, source_target_pairs={{0,2},{1,3},{2,0},{3,1},{4,6},{5,7},{6,4},{7,5},{8,10},{9,11},{10,... | collective-permute-start | bytes 589832 | tf_op jit(solution)/shard_map/ppermute | solution.py:153
  35.8 0.5 collective-permute-start.9
  36.3 0.8 %interpolate.5 = (f32[4,6,32,128]{3,2,1,0:T(8,128)S(1)}, bf16[4,6,32,128]{3,2,1,0:T(8,128)(2,1)S(1)}, bf16[4,6,32,128]{3,2,1,0:T(8,128)(2,1)S(1)}, bf16[4,6,32,128]{3,2,1,0:T(8,128)(2,1)S(1)}) custom-call(bf16[6,16,16384]{2,1,0:T(8,128)(2,1)S(1)} %copy-done.1, bf16[6,16,16384]{2,1,0:T(8,128)(2,1)S(1)} %collective-permute-done.2.far_hbm, ...), custom_call_target="tpu_custom_call" | custom-call | tf_op jit(solution)/shard_map/interpolate/pallas_call | solution.py:77
  37.0 1.6 %collective-permute-start.10 = (bf16[4,6,32,128]{3,2,1,0:T(8,128)(2,1)S(1)}, bf16[4,6,32,128]{3,2,1,0:T(8,128)(2,1)S(1)}, u32[]{:S(2)}, u32[]{:S(2)}) collective-permute-start(bf16[4,6,32,128]{3,2,1,0:T(8,128)(2,1)S(1)} %get-tuple-element.45), channel_id=1, source_target_pairs={{0,1},{1,0},{2,3},{3,2},{4,5},{5,4},{6,7},{7,6},{8,9},{9,8},{10,11... | collective-permute-start | bytes 589832 | tf_op jit(solution)/shard_map/ppermute | solution.py:153
  38.6 2.0 %collective-permute-done.7.refs_1_ = bf16[4,6,32,128]{3,2,1,0:T(8,128)(2,1)S(1)} collective-permute-done((bf16[4,6,32,128]{3,2,1,0:T(8,128)(2,1)S(1)}, bf16[4,6,32,128]{3,2,1,0:T(8,128)(2,1)S(1)}, u32[]{:S(2)}, u32[]{:S(2)}) %collective-permute-start.7) | collective-permute-done | bytes 196640 | tf_op jit(solution)/shard_map/ppermute | solution.py:153
  40.6 1.5 %collective-permute-start.11 = (bf16[4,6,32,128]{3,2,1,0:T(8,128)(2,1)S(1)}, bf16[4,6,32,128]{3,2,1,0:T(8,128)(2,1)S(1)}, u32[]{:S(2)}, u32[]{:S(2)}) collective-permute-start(bf16[4,6,32,128]{3,2,1,0:T(8,128)(2,1)S(1)} %get-tuple-element.46), channel_id=1, source_target_pairs={{0,2},{1,3},{2,0},{3,1},{4,6},{5,7},{6,4},{7,5},{8,10},{9,11},{10,... | collective-permute-start | bytes 589832 | tf_op jit(solution)/shard_map/ppermute | solution.py:153
  42.1 2.8 %collective-permute-done.8.refs_2_ = bf16[4,6,32,128]{3,2,1,0:T(8,128)(2,1)S(1)} collective-permute-done((bf16[4,6,32,128]{3,2,1,0:T(8,128)(2,1)S(1)}, bf16[4,6,32,128]{3,2,1,0:T(8,128)(2,1)S(1)}, u32[]{:S(2)}, u32[]{:S(2)}) %collective-permute-start.8) | collective-permute-done | bytes 196640 | tf_op jit(solution)/shard_map/ppermute | solution.py:153
  44.9 0.6 collective-permute-start.12
  45.5 0.3 collective-permute-done.9.refs_3_
  45.8 0.1 total.5
  45.9 0.0 copy-start.3
  45.9 0.0 collective-permute-done.6.mats_hbm
  45.9 2.3 %collective-permute-start.14 = (bf16[4,6,32,128]{3,2,1,0:T(8,128)(2,1)S(1)}, bf16[4,6,32,128]{3,2,1,0:T(8,128)(2,1)S(1)}, u32[]{:S(2)}, u32[]{:S(2)}) collective-permute-start(bf16[4,6,32,128]{3,2,1,0:T(8,128)(2,1)S(1)} %total.5), channel_id=1, source_target_pairs={{0,16},{4,20},{8,24},{12,28},{16,0},{20,4},{24,8},{28,12},{1,17},{... | collective-permute-start | bytes 589832 | tf_op jit(solution)/shard_map/ppermute | solution.py:141
  48.3 0.8 %interpolate.7 = (f32[4,6,32,128]{3,2,1,0:T(8,128)S(1)}, bf16[4,6,32,128]{3,2,1,0:T(8,128)(2,1)S(1)}, bf16[4,6,32,128]{3,2,1,0:T(8,128)(2,1)S(1)}, bf16[4,6,32,128]{3,2,1,0:T(8,128)(2,1)S(1)}) custom-call(bf16[6,16,16384]{2,1,0:T(8,128)(2,1)S(1)} %copy-done.1, bf16[6,16,16384]{2,1,0:T(8,128)(2,1)S(1)} %collective-permute-done.2.far_hbm, ...), custom_call_target="tpu_custom_call" | custom-call | tf_op jit(solution)/shard_map/interpolate/pallas_call | solution.py:77
  49.1 3.2 %collective-permute-start.15 = (bf16[4,6,32,128]{3,2,1,0:T(8,128)(2,1)S(1)}, bf16[4,6,32,128]{3,2,1,0:T(8,128)(2,1)S(1)}, u32[]{:S(2)}, u32[]{:S(2)}) collective-permute-start(bf16[4,6,32,128]{3,2,1,0:T(8,128)(2,1)S(1)} %get-tuple-element.52), channel_id=1, source_target_pairs={{0,1},{1,0},{2,3},{3,2},{4,5},{5,4},{6,7},{7,6},{8,9},{9,8},{10,11... | collective-permute-start | bytes 589832 | tf_op jit(solution)/shard_map/ppermute | solution.py:153
  52.2 0.0 collective-permute-done.10.refs_1_
  52.2 0.0 collective-permute-start.16
  52.2 0.0 collective-permute-done.11.refs_2_
  52.2 1.5 %collective-permute-start.17 = (bf16[4,6,32,128]{3,2,1,0:T(8,128)(2,1)S(1)}, bf16[4,6,32,128]{3,2,1,0:T(8,128)(2,1)S(1)}, u32[]{:S(2)}, u32[]{:S(2)}) collective-permute-start(bf16[4,6,32,128]{3,2,1,0:T(8,128)(2,1)S(1)} %get-tuple-element.54), channel_id=1, source_target_pairs={{0,3},{1,2},{2,1},{3,0},{4,7},{5,6},{6,5},{7,4},{8,11},{9,10},{10,... | collective-permute-start | bytes 589832 | tf_op jit(solution)/shard_map/ppermute | solution.py:153
  53.8 0.5 collective-permute-done.12.refs_3_
  54.3 0.1 total.6
  54.4 0.1 collective-permute-start.13
  54.5 0.9 %collective-permute-done.14.refs_2_ = bf16[4,6,32,128]{3,2,1,0:T(8,128)(2,1)S(1)} collective-permute-done((bf16[4,6,32,128]{3,2,1,0:T(8,128)(2,1)S(1)}, bf16[4,6,32,128]{3,2,1,0:T(8,128)(2,1)S(1)}, u32[]{:S(2)}, u32[]{:S(2)}) %collective-permute-start.14) | collective-permute-done | bytes 196640 | tf_op jit(solution)/shard_map/ppermute | solution.py:141
  55.4 2.6 %collective-permute-done.15.refs_1_ = bf16[4,6,32,128]{3,2,1,0:T(8,128)(2,1)S(1)} collective-permute-done((bf16[4,6,32,128]{3,2,1,0:T(8,128)(2,1)S(1)}, bf16[4,6,32,128]{3,2,1,0:T(8,128)(2,1)S(1)}, u32[]{:S(2)}, u32[]{:S(2)}) %collective-permute-start.15) | collective-permute-done | bytes 196640 | tf_op jit(solution)/shard_map/ppermute | solution.py:153
  58.1 3.8 %collective-permute-done.16.refs_2_ = bf16[4,6,32,128]{3,2,1,0:T(8,128)(2,1)S(1)} collective-permute-done((bf16[4,6,32,128]{3,2,1,0:T(8,128)(2,1)S(1)}, bf16[4,6,32,128]{3,2,1,0:T(8,128)(2,1)S(1)}, u32[]{:S(2)}, u32[]{:S(2)}) %collective-permute-start.16) | collective-permute-done | bytes 196640 | tf_op jit(solution)/shard_map/ppermute | solution.py:153
  61.9 0.1 total.7
  62.0 1.9 %collective-permute-start.18 = (bf16[4,6,32,128]{3,2,1,0:T(8,128)(2,1)S(1)}, bf16[4,6,32,128]{3,2,1,0:T(8,128)(2,1)S(1)}, u32[]{:S(2)}, u32[]{:S(2)}) collective-permute-start(bf16[4,6,32,128]{3,2,1,0:T(8,128)(2,1)S(1)} %total.7), channel_id=1, source_target_pairs={{0,24},{4,28},{8,16},{12,20},{16,8},{20,12},{24,0},{28,4},{1,25},{... | collective-permute-start | bytes 589832 | tf_op jit(solution)/shard_map/ppermute | solution.py:141
  63.9 0.0 collective-permute-done.13.refs_1_
  63.9 5.7 %collective-permute-done.18.refs_3_ = bf16[4,6,32,128]{3,2,1,0:T(8,128)(2,1)S(1)} collective-permute-done((bf16[4,6,32,128]{3,2,1,0:T(8,128)(2,1)S(1)}, bf16[4,6,32,128]{3,2,1,0:T(8,128)(2,1)S(1)}, u32[]{:S(2)}, u32[]{:S(2)}) %collective-permute-start.18) | collective-permute-done | bytes 196640 | tf_op jit(solution)/shard_map/ppermute | solution.py:141
  69.6 1.0 %finish.1 = bf16[4,6,128,128]{3,2,1,0:T(8,128)(2,1)} custom-call(f32[4,128]{1,0:T(4,128)S(1)} %copy-done.3, f32[4,6,32,128]{3,2,1,0:T(8,128)S(1)} %total.4.refs_0_, bf16[4,6,32,128]{3,2,1,0:T(8,128)(2,1)S(1)} %collective-permute-done.13.refs_1_, bf16[4,6,32,128]{3,2,1,0:T(8,128)(2,1)S(1)} %collective-permute-done.14.refs_2_, ...), custom_call_target="tpu_custom_call" | custom-call | tf_op jit(solution)/shard_map/finish/pallas_call | solution.py:127
  (8 shorter events, 0.0 us)
Async XLA Ops:
  0.0 7.5 %collective-permute-start.2 = (bf16[6,16,16384]{2,1,0:T(8,128)(2,1)}, bf16[6,16,16384]{2,1,0:T(8,128)(2,1)S(1)}, u32[]{:S(2)}, u32[]{:S(2)}) collective-permute-start(bf16[6,16,16384]{2,1,0:T(8,128)(2,1)} %own_hbm.7), channel_id=1, source_target_pairs={{0,4},{4,0},{8,12},{12,8},{16,20},{20,16},{24,28},{28,24},{1,5},{5... | collective-permute-start | bytes 9437192 | tf_op jit(solution)/shard_map/ppermute | solution.py:147
  2.3 27.9 %collective-permute-start = (bf16[2064,128]{1,0:T(8,128)(2,1)}, bf16[2064,128]{1,0:T(8,128)(2,1)S(1)}, u32[]{:S(2)}, u32[]{:S(2)}) collective-permute-start(bf16[2064,128]{1,0:T(8,128)(2,1)} %pack.1.mats_hbm), channel_id=1, source_target_pairs={{0,16},{4,20},{8,24},{12,28},{16,0},{20,4},{24,8},{28,12},{1,17},{... | collective-permute-start | bytes 1585160 | tf_op jit(solution)/shard_map/ppermute | solution.py:141
  5.9 24.5 %collective-permute-start.1 = (bf16[2064,128]{1,0:T(8,128)(2,1)}, bf16[2064,128]{1,0:T(8,128)(2,1)S(1)}, u32[]{:S(2)}, u32[]{:S(2)}) collective-permute-start(bf16[2064,128]{1,0:T(8,128)(2,1)} %pack.1.mats_hbm), channel_id=1, source_target_pairs={{0,8},{4,12},{8,0},{12,4},{16,24},{20,28},{24,16},{28,20},{1,9},{5... | collective-permute-start | bytes 1585160 | tf_op jit(solution)/shard_map/ppermute | solution.py:141
  7.5 1.9 %copy-start = (bf16[6,16,16384]{2,1,0:T(8,128)(2,1)S(1)}, bf16[6,16,16384]{2,1,0:T(8,128)(2,1)}, u32[]{:S(2)}) copy-start(bf16[6,16,16384]{2,1,0:T(8,128)(2,1)} %own_hbm.7) | copy-start | bytes 9437188
  9.4 1.0 %copy-start.2 = (bf16[2064,128]{1,0:T(8,128)(2,1)S(1)}, bf16[2064,128]{1,0:T(8,128)(2,1)}, u32[]{:S(2)}) copy-start(bf16[2064,128]{1,0:T(8,128)(2,1)} %pack.1.mats_hbm) | copy-start | bytes 1585156
  10.4 21.5 %copy-start.1 = (bf16[6,16,16384]{2,1,0:T(8,128)(2,1)S(1)}, bf16[6,16,16384]{2,1,0:T(8,128)(2,1)}, u32[]{:S(2)}) copy-start(bf16[6,16,16384]{2,1,0:T(8,128)(2,1)} %own_hbm.7) | copy-start | bytes 9437188
  11.2 7.8 %collective-permute-start.3 = (bf16[4,6,32,128]{3,2,1,0:T(8,128)(2,1)S(1)}, bf16[4,6,32,128]{3,2,1,0:T(8,128)(2,1)S(1)}, u32[]{:S(2)}, u32[]{:S(2)}) collective-permute-start(bf16[4,6,32,128]{3,2,1,0:T(8,128)(2,1)S(1)} %get-tuple-element.31), channel_id=1, source_target_pairs={{0,1},{1,0},{2,3},{3,2},{4,5},{5,4},{6,7},{7,6},{8,9},{9,8},{10,11... | collective-permute-start | bytes 589832 | tf_op jit(solution)/shard_map/ppermute | solution.py:153
  12.8 10.7 %collective-permute-start.4 = (bf16[4,6,32,128]{3,2,1,0:T(8,128)(2,1)S(1)}, bf16[4,6,32,128]{3,2,1,0:T(8,128)(2,1)S(1)}, u32[]{:S(2)}, u32[]{:S(2)}) collective-permute-start(bf16[4,6,32,128]{3,2,1,0:T(8,128)(2,1)S(1)} %get-tuple-element.32), channel_id=1, source_target_pairs={{0,2},{1,3},{2,0},{3,1},{4,6},{5,7},{6,4},{7,5},{8,10},{9,11},{10,... | collective-permute-start | bytes 589832 | tf_op jit(solution)/shard_map/ppermute | solution.py:153
  14.3 9.2 %collective-permute-start.5 = (bf16[4,6,32,128]{3,2,1,0:T(8,128)(2,1)S(1)}, bf16[4,6,32,128]{3,2,1,0:T(8,128)(2,1)S(1)}, u32[]{:S(2)}, u32[]{:S(2)}) collective-permute-start(bf16[4,6,32,128]{3,2,1,0:T(8,128)(2,1)S(1)} %get-tuple-element.33), channel_id=1, source_target_pairs={{0,3},{1,2},{2,1},{3,0},{4,7},{5,6},{6,5},{7,4},{8,11},{9,10},{10,... | collective-permute-start | bytes 589832 | tf_op jit(solution)/shard_map/ppermute | solution.py:153
  30.4 15.5 %collective-permute-start.6 = (bf16[2064,128]{1,0:T(8,128)(2,1)S(1)}, bf16[2064,128]{1,0:T(8,128)(2,1)S(1)}, u32[]{:S(2)}, u32[]{:S(2)}) collective-permute-start(bf16[2064,128]{1,0:T(8,128)(2,1)S(1)} %collective-permute-done.mats_hbm), channel_id=1, source_target_pairs={{0,8},{4,12},{8,0},{12,4},{16,24},{20,28},{24,16},{28,20},{1,9},{5... | collective-permute-start | bytes 1585160 | tf_op jit(solution)/shard_map/ppermute | solution.py:141
  32.7 7.9 %collective-permute-start.7 = (bf16[4,6,32,128]{3,2,1,0:T(8,128)(2,1)S(1)}, bf16[4,6,32,128]{3,2,1,0:T(8,128)(2,1)S(1)}, u32[]{:S(2)}, u32[]{:S(2)}) collective-permute-start(bf16[4,6,32,128]{3,2,1,0:T(8,128)(2,1)S(1)} %get-tuple-element.39), channel_id=1, source_target_pairs={{0,1},{1,0},{2,3},{3,2},{4,5},{5,4},{6,7},{7,6},{8,9},{9,8},{10,11... | collective-permute-start | bytes 589832 | tf_op jit(solution)/shard_map/ppermute | solution.py:153
  34.3 10.6 %collective-permute-start.8 = (bf16[4,6,32,128]{3,2,1,0:T(8,128)(2,1)S(1)}, bf16[4,6,32,128]{3,2,1,0:T(8,128)(2,1)S(1)}, u32[]{:S(2)}, u32[]{:S(2)}) collective-permute-start(bf16[4,6,32,128]{3,2,1,0:T(8,128)(2,1)S(1)} %get-tuple-element.40), channel_id=1, source_target_pairs={{0,2},{1,3},{2,0},{3,1},{4,6},{5,7},{6,4},{7,5},{8,10},{9,11},{10,... | collective-permute-start | bytes 589832 | tf_op jit(solution)/shard_map/ppermute | solution.py:153
  35.8 10.0 %collective-permute-start.9 = (bf16[4,6,32,128]{3,2,1,0:T(8,128)(2,1)S(1)}, bf16[4,6,32,128]{3,2,1,0:T(8,128)(2,1)S(1)}, u32[]{:S(2)}, u32[]{:S(2)}) collective-permute-start(bf16[4,6,32,128]{3,2,1,0:T(8,128)(2,1)S(1)} %get-tuple-element.41), channel_id=1, source_target_pairs={{0,3},{1,2},{2,1},{3,0},{4,7},{5,6},{6,5},{7,4},{8,11},{9,10},{10,... | collective-permute-start | bytes 589832 | tf_op jit(solution)/shard_map/ppermute | solution.py:153
  37.0 15.2 %collective-permute-start.10 = (bf16[4,6,32,128]{3,2,1,0:T(8,128)(2,1)S(1)}, bf16[4,6,32,128]{3,2,1,0:T(8,128)(2,1)S(1)}, u32[]{:S(2)}, u32[]{:S(2)}) collective-permute-start(bf16[4,6,32,128]{3,2,1,0:T(8,128)(2,1)S(1)} %get-tuple-element.45), channel_id=1, source_target_pairs={{0,1},{1,0},{2,3},{3,2},{4,5},{5,4},{6,7},{7,6},{8,9},{9,8},{10,11... | collective-permute-start | bytes 589832 | tf_op jit(solution)/shard_map/ppermute | solution.py:153
  40.6 11.6 %collective-permute-start.11 = (bf16[4,6,32,128]{3,2,1,0:T(8,128)(2,1)S(1)}, bf16[4,6,32,128]{3,2,1,0:T(8,128)(2,1)S(1)}, u32[]{:S(2)}, u32[]{:S(2)}) collective-permute-start(bf16[4,6,32,128]{3,2,1,0:T(8,128)(2,1)S(1)} %get-tuple-element.46), channel_id=1, source_target_pairs={{0,2},{1,3},{2,0},{3,1},{4,6},{5,7},{6,4},{7,5},{8,10},{9,11},{10,... | collective-permute-start | bytes 589832 | tf_op jit(solution)/shard_map/ppermute | solution.py:153
  44.9 9.4 %collective-permute-start.12 = (bf16[4,6,32,128]{3,2,1,0:T(8,128)(2,1)S(1)}, bf16[4,6,32,128]{3,2,1,0:T(8,128)(2,1)S(1)}, u32[]{:S(2)}, u32[]{:S(2)}) collective-permute-start(bf16[4,6,32,128]{3,2,1,0:T(8,128)(2,1)S(1)} %get-tuple-element.47), channel_id=1, source_target_pairs={{0,3},{1,2},{2,1},{3,0},{4,7},{5,6},{6,5},{7,4},{8,11},{9,10},{10,... | collective-permute-start | bytes 589832 | tf_op jit(solution)/shard_map/ppermute | solution.py:153
  45.9 23.7 %copy-start.3 = (f32[4,128]{1,0:T(4,128)S(1)}, f32[4,128]{1,0:T(4,128)}, u32[]{:S(2)}) copy-start(f32[4,128]{1,0:T(4,128)} %weight_ref.1) | copy-start | bytes 6148
  45.9 9.5 %collective-permute-start.14 = (bf16[4,6,32,128]{3,2,1,0:T(8,128)(2,1)S(1)}, bf16[4,6,32,128]{3,2,1,0:T(8,128)(2,1)S(1)}, u32[]{:S(2)}, u32[]{:S(2)}) collective-permute-start(bf16[4,6,32,128]{3,2,1,0:T(8,128)(2,1)S(1)} %total.5), channel_id=1, source_target_pairs={{0,16},{4,20},{8,24},{12,28},{16,0},{20,4},{24,8},{28,12},{1,17},{... | collective-permute-start | bytes 589832 | tf_op jit(solution)/shard_map/ppermute | solution.py:141
  49.1 9.0 %collective-permute-start.15 = (bf16[4,6,32,128]{3,2,1,0:T(8,128)(2,1)S(1)}, bf16[4,6,32,128]{3,2,1,0:T(8,128)(2,1)S(1)}, u32[]{:S(2)}, u32[]{:S(2)}) collective-permute-start(bf16[4,6,32,128]{3,2,1,0:T(8,128)(2,1)S(1)} %get-tuple-element.52), channel_id=1, source_target_pairs={{0,1},{1,0},{2,3},{3,2},{4,5},{5,4},{6,7},{7,6},{8,9},{9,8},{10,11... | collective-permute-start | bytes 589832 | tf_op jit(solution)/shard_map/ppermute | solution.py:153
  52.2 9.7 %collective-permute-start.16 = (bf16[4,6,32,128]{3,2,1,0:T(8,128)(2,1)S(1)}, bf16[4,6,32,128]{3,2,1,0:T(8,128)(2,1)S(1)}, u32[]{:S(2)}, u32[]{:S(2)}) collective-permute-start(bf16[4,6,32,128]{3,2,1,0:T(8,128)(2,1)S(1)} %get-tuple-element.53), channel_id=1, source_target_pairs={{0,2},{1,3},{2,0},{3,1},{4,6},{5,7},{6,4},{7,5},{8,10},{9,11},{10,... | collective-permute-start | bytes 589832 | tf_op jit(solution)/shard_map/ppermute | solution.py:153
  52.2 9.6 %collective-permute-start.17 = (bf16[4,6,32,128]{3,2,1,0:T(8,128)(2,1)S(1)}, bf16[4,6,32,128]{3,2,1,0:T(8,128)(2,1)S(1)}, u32[]{:S(2)}, u32[]{:S(2)}) collective-permute-start(bf16[4,6,32,128]{3,2,1,0:T(8,128)(2,1)S(1)} %get-tuple-element.54), channel_id=1, source_target_pairs={{0,3},{1,2},{2,1},{3,0},{4,7},{5,6},{6,5},{7,4},{8,11},{9,10},{10,... | collective-permute-start | bytes 589832 | tf_op jit(solution)/shard_map/ppermute | solution.py:153
  54.4 9.5 %collective-permute-start.13 = (bf16[4,6,32,128]{3,2,1,0:T(8,128)(2,1)S(1)}, bf16[4,6,32,128]{3,2,1,0:T(8,128)(2,1)S(1)}, u32[]{:S(2)}, u32[]{:S(2)}) collective-permute-start(bf16[4,6,32,128]{3,2,1,0:T(8,128)(2,1)S(1)} %total.6), channel_id=1, source_target_pairs={{0,8},{4,12},{8,0},{12,4},{16,24},{20,28},{24,16},{28,20},{1,9},{5... | collective-permute-start | bytes 589832 | tf_op jit(solution)/shard_map/ppermute | solution.py:141
  62.0 7.6 %collective-permute-start.18 = (bf16[4,6,32,128]{3,2,1,0:T(8,128)(2,1)S(1)}, bf16[4,6,32,128]{3,2,1,0:T(8,128)(2,1)S(1)}, u32[]{:S(2)}, u32[]{:S(2)}) collective-permute-start(bf16[4,6,32,128]{3,2,1,0:T(8,128)(2,1)S(1)} %total.7), channel_id=1, source_target_pairs={{0,24},{4,28},{8,16},{12,20},{16,8},{20,12},{24,0},{28,4},{1,25},{... | collective-permute-start | bytes 589832 | tf_op jit(solution)/shard_map/ppermute | solution.py:141

commit v3 on v2

v3 whole, which is shorter than its diff:
```python
import functools

import jax
import jax.numpy as jnp
from jax import lax
from jax.experimental import pallas as pl
from jax.experimental.pallas import tpu as pltpu
from jax.sharding import PartitionSpec as P

CORES = 2
LIMIT = pltpu.CompilerParams(vmem_limit_bytes=32 * 2**20)

ORDER = {('name', 1, 0): [('face', 0, 0)], ('name', 2, 0): [('face', 0, 0)], ('name', 3, 0): [('face', 0, 0)], ('mats', 3, 0): [('mats', 1, 0), ('name', 1, 0), ('name', 2, 0), ('sum', 0, 0)], ('face', 3, 0): [('sum', 2, 0)], ('home', 2, 0): [('mats', 3, 0)], ('sum', 1, 0): [('face', 3, 0)], ('sum', 3, 0): [('home', 2, 0)]}


def place():
    me = lax.axis_index("tm")
    return me // CORES, lax.rem(me, CORES), lax.axis_index("box")


def interpolate_kernel(turn, boxes, blocks, named, own_hbm, far_hbm, mats_hbm, *rest):
    outs, (own, far, mats, acc, sems) = rest[:boxes], rest[boxes:]
    chip, core, box = place()
    comp, samples, width = own.shape
    nodes = mats.shape[1]
    slots = acc.shape[0] // boxes
    at = pl.ds(pl.multiple_of(((chip ^ turn) * CORES + core) * width, width), width)
    copies = [
        pltpu.make_async_copy(mats_hbm, mats, sems.at[0]),
        pltpu.make_async_copy(own_hbm.at[:, :, at], own, sems.at[1]),
        pltpu.make_async_copy(far_hbm.at[:, :, at], far, sems.at[2]),
    ]
    for copy in copies:
        copy.start()
    acc[...] = jnp.zeros_like(acc)
    for copy in copies:
        copy.wait()
    named_row = named[...]
    for j in range(blocks):
        target = named_row[0, j]
        for ref, half in ((own, core), (far, 1 - core)):
            x = ref[:, :, j * nodes:(j + 1) * nodes]
            if samples % 16:
                x = x.astype(jnp.float32).reshape(comp * samples, nodes).astype(x.dtype)
            else:
                x = x.reshape(comp * samples, nodes)
            y = jnp.dot(x, mats[j * nodes:(j + 1) * nodes, :], preferred_element_type=jnp.float32)
            acc[target, :, half] += y.reshape(comp, samples, nodes)
    for d, out in enumerate(outs):
        for s in range(slots):
            part = acc[(box ^ d) * slots + s]
            out[s] = part.reshape(comp, CORES * samples, nodes).astype(out.dtype)


def interpolate(turn, named, traces, far, mats, blocks, boxes, slots):
    nodes = mats.shape[1]
    comp, samples, _ = traces.shape
    width = blocks * nodes
    shape = (slots, comp, CORES * samples, nodes)
    return pl.pallas_call(
        functools.partial(interpolate_kernel, turn, boxes, blocks),
        in_specs=[pl.BlockSpec(memory_space=pltpu.VMEM)] + [pl.BlockSpec(memory_space=pl.ANY)] * 3,
        out_specs=[pl.BlockSpec(memory_space=pltpu.VMEM)] * boxes,
        scratch_shapes=[
            pltpu.VMEM((comp, samples, width), traces.dtype),
            pltpu.VMEM((comp, samples, width), traces.dtype),
            pltpu.VMEM(mats.shape, mats.dtype),
            pltpu.VMEM((boxes * slots, comp, CORES, samples, nodes), jnp.float32),
            pltpu.SemaphoreType.DMA((3,)),
        ],
        out_shape=[
            jax.ShapeDtypeStruct(shape, jnp.bfloat16 if d else jnp.float32) for d in range(boxes)
        ],
        compiler_params=LIMIT,
        name="interpolate",
    )(named, traces, far, mats)


def total_kernel(*refs):
    out = refs[-1]
    for s in range(out.shape[0]):
        value = refs[0][s]
        for ref in refs[1:-1]:
            value = value + ref[s].astype(jnp.float32)
        out[s] = value.astype(out.dtype)


def total(parts, dtype):
    return pl.pallas_call(
        total_kernel,
        out_shape=jax.ShapeDtypeStruct(parts[0].shape, dtype),
        compiler_params=LIMIT,
        name="total",
    )(*parts)


def finish_kernel(turns, count, weight_ref, *refs):
    pieces, out, (scratch, sems) = refs[:count], refs[-3], refs[-2:]
    chip, _, _ = place()
    _, _, length, _ = pieces[0].shape
    copies, first = [], 0
    for i, (turn, piece) in enumerate(zip(turns, pieces)):
        number = piece.shape[0]
        first = 0 if i and turn != turns[i - 1] else first
        for s in range(number):
            value = piece[s].astype(jnp.float32) * weight_ref[first + s:first + s + 1, :][None]
            scratch[i, s] = value.astype(scratch.dtype)
        at = pl.ds(pl.multiple_of((chip ^ turn) * length, length), length)
        copies.append(pltpu.make_async_copy(
            scratch.at[i, :number], out.at[first:first + number, :, at, :], sems.at[i]
        ))
        copies[-1].start()
        first += number
    for copy in copies:
        copy.wait()


def finish(weight, turns, pieces, chips, earlier=None):
    slots, _ = weight.shape
    number, comp, length, nodes = pieces[0].shape
    whole = pl.BlockSpec(memory_space=pltpu.VMEM)
    rest = [] if earlier is None else [earlier]
    return pl.pallas_call(
        functools.partial(finish_kernel, turns, len(pieces)),
        in_specs=[whole] * (1 + len(pieces)) + [pl.BlockSpec(memory_space=pl.ANY)] * len(rest),
        out_specs=pl.BlockSpec(memory_space=pl.ANY),
        scratch_shapes=[
            pltpu.VMEM((len(pieces), number, comp, length, nodes), jnp.bfloat16),
            pltpu.SemaphoreType.DMA((len(pieces),)),
        ],
        out_shape=jax.ShapeDtypeStruct((slots, comp, length * chips, nodes), jnp.bfloat16),
        input_output_aliases={1 + len(pieces): 0} if rest else {},
        compiler_params=LIMIT,
        name="finish",
    )(weight, *pieces, *rest)


def per_device(chips, boxes, traces, projection, owner_route, face_slot, face_weight):
    _, blocks, nodes, _ = projection.shape
    slots = face_weight.shape[0]
    whole = projection.reshape(blocks * nodes, nodes)
    targets = owner_route.reshape(1, blocks) * slots + face_slot.reshape(1, blocks)
    made = {}

    def along(x, turn):
        pairs = [(z * CORES + c, (z ^ turn) * CORES + c) for z in range(chips) for c in range(CORES)]
        return lax.ppermute(x, "tm", pairs)

    def make(kind, turn=0, d=0):
        def wait(x):
            others = [get(*other) for other in ORDER.get((kind, turn, d), ())]
            others = [y[0] if isinstance(y, (list, tuple)) else y for y in others]
            return lax.optimization_barrier((x, *others))[0] if others else x

        if kind == "mats":
            if turn < 2:
                return along(wait(whole), turn) if turn else whole
            return along(wait(get("mats", turn - 1)), 1) if turn % 2 else along(wait(whole), turn)
        if kind == "name":
            return along(wait(targets), turn) if turn else targets
        if kind == "far":
            return lax.ppermute(wait(traces), "tm", [(j, j ^ 1) for j in range(chips * CORES)])
        if kind == "face":
            mats = wait(get("mats", turn))
            return interpolate(turn, get("name", turn), traces, get("far"), mats, blocks, boxes, slots)
        if kind == "cross":
            return lax.ppermute(wait(get("face", turn)[d]), "box", [(b, b ^ d) for b in range(boxes)])
        if kind == "sum":
            mine = wait(get("face", turn)[0])
            return total([mine] + [get("cross", turn, d) for d in range(1, boxes)], jnp.bfloat16 if turn else jnp.float32)
        if kind == "home":
            return along(wait(get("sum", turn)), turn) if turn else get("sum", 0)

    def get(kind, turn=0, d=0):
        key = (kind, turn, d)
        if key not in made:
            made[key] = make(*key)
        return made[key]

    last = chips - 1
    out = finish(face_weight, range(last), [get("home", r) for r in range(last)], chips)
    return finish(face_weight, [last], [get("home", last)], chips, out)


def solution(mesh):
    chips, boxes = mesh.shape["tm"] // CORES, mesh.shape["box"]
    return jax.shard_map(
        functools.partial(per_device, chips, boxes),
        mesh=mesh,
        in_specs=(
            P(None, "tm", "box"),
            P("box", "tm", None, None),
            P("box", "tm", None),
            P("box", "tm", None),
            P(("tm", "box"), None),
        ),
        out_specs=P(("tm", "box"), None, None, None),
        check_vma=False,
    )
```

time: 71.1 us -> 68.5 us (0.963)
  waiting for transfers between devices: 34.3 us -> 25.2 us
  starting transfers between devices: 27 us -> 34.4 us
  Pallas kernels: 6.32 us -> 4.98 us
    ppermute x19 -> x22, waiting for transfers between devices: 34.3 us -> 25.2 us  [the longest x12 17.5 us: make(): lax.ppermute(wait(get('face', turn)[d]), 'box', [(b, b ^ d) for b in rang...]
    ppermute x19 -> x22, starting transfers between devices: 27 us -> 34.4 us  [the longest x9 18.3 us: along(): return lax.ppermute(x, 'tm', pairs)]
    pallas_call x2, Pallas kernels: 2.91 us -> 1.58 us  [finish(): pl.pallas_call(functools.partial(finish_kernel, turns, len(pieces)), in_s...]
  transfers between devices with their start and end apart: 19 -> 22, of which waited for: 12 -> 13; matrix products, arithmetic and copies ran while one was open for 0% -> 1% of each run, Pallas kernels for 8% -> 6%
where the time goes in v3:
time: 68.5 us; the launch traced here: 68.3 us
  starting transfers between devices  34.4 us (50%)
  waiting for transfers between devices  25.2 us (37%)
  Pallas kernels  4.98 us (7%)
  local copies, waits for them, and re-layouts  2.94 us (4%)
    ppermute x9, starting transfers between devices, along(): return lax.ppermute(x, 'tm', pairs)  18.3 us
    ppermute x12, waiting for transfers between devices, make(): lax.ppermute(wait(get('face', turn)[d]), 'box', [(b, b ^ d) for b in rang...  17.5 us
    ppermute x12, starting transfers between devices, make(): lax.ppermute(wait(get('face', turn)[d]), 'box', [(b, b ^ d) for b in rang...  15.6 us
    ppermute x9, waiting for transfers between devices, along(): return lax.ppermute(x, 'tm', pairs)  7.64 us
    pallas_call x4, Pallas kernels, interpolate(): pl.pallas_call(functools.partial(interpolate_kernel, turn, boxes, blocks)...  3.01 us
    unnamed x8, local copies, waits for them, and re-layouts  2.94 us
    pallas_call x2, Pallas kernels, finish(): pl.pallas_call(functools.partial(finish_kernel, turns, len(pieces)), in_s...  1.58 us
  transfers between devices with their start and end apart: 22, of which 13 were waited for; matrix products, arithmetic and copies ran while one was open for 1% of the time, Pallas kernels for 6%

profile of v3, /device:TPU:0, one launch (start us, length us, event | category | flops | bytes accessed | tf_op | source)
XLA Modules:
  0.0 68.3 jit_solution(12561251155214496616)
XLA Ops:
  0.0 0.5 collective-permute-start
  0.5 3.6 %collective-permute-start.2 = (bf16[2048,128]{1,0:T(8,128)(2,1)}, bf16[2048,128]{1,0:T(8,128)(2,1)S(1)}, u32[]{:S(2)}, u32[]{:S(2)}) collective-permute-start(bf16[2048,128]{1,0:T(8,128)(2,1)} %bitcast.3), channel_id=1, source_target_pairs={{0,16},{4,20},{8,24},{12,28},{16,0},{20,4},{24,8},{28,12},{1,17},{... | collective-permute-start | bytes 1572872 | tf_op jit(solution)/shard_map/ppermute | solution.py:147
  4.0 1.6 %collective-permute-start.3 = (bf16[2048,128]{1,0:T(8,128)(2,1)}, bf16[2048,128]{1,0:T(8,128)(2,1)S(1)}, u32[]{:S(2)}, u32[]{:S(2)}) collective-permute-start(bf16[2048,128]{1,0:T(8,128)(2,1)} %bitcast.4), channel_id=1, source_target_pairs={{0,8},{4,12},{8,0},{12,4},{16,24},{20,28},{24,16},{28,20},{1,9},{5... | collective-permute-start | bytes 1572872 | tf_op jit(solution)/shard_map/ppermute | solution.py:147
  5.6 0.7 add_bitcast_fusion.named
  6.3 1.9 %copy-done = bf16[6,16,16384]{2,1,0:T(8,128)(2,1)S(1)} copy-done((bf16[6,16,16384]{2,1,0:T(8,128)(2,1)S(1)}, bf16[6,16,16384]{2,1,0:T(8,128)(2,1)}, u32[]{:S(2)}) %copy-start) | copy-done | bytes 3145752
  8.2 1.0 %copy-done.2 = bf16[1,16,128,128]{3,2,1,0:T(8,128)(2,1)S(1)} copy-done((bf16[1,16,128,128]{3,2,1,0:T(8,128)(2,1)S(1)}, bf16[1,16,128,128]{3,2,1,0:T(8,128)(2,1)}, u32[]{:S(2)}) %copy-start.2) | copy-done | bytes 524312
  9.2 0.8 %interpolate.4 = (f32[4,6,32,128]{3,2,1,0:T(8,128)S(1)}, bf16[4,6,32,128]{3,2,1,0:T(8,128)(2,1)S(1)}, bf16[4,6,32,128]{3,2,1,0:T(8,128)(2,1)S(1)}, bf16[4,6,32,128]{3,2,1,0:T(8,128)(2,1)S(1)}) custom-call(s32[1,16]{1,0:T(1,128)S(1)} %add_bitcast_fusion.named, bf16[6,16,16384]{2,1,0:T(8,128)(2,1)S(1)} %copy-done, ...), custom_call_target="tpu_custom_call" | custom-call | tf_op jit(solution)/shard_map/interpolate/pallas_call | solution.py:60
  10.0 2.6 %collective-permute-start.6 = (bf16[4,6,32,128]{3,2,1,0:T(8,128)(2,1)S(1)}, bf16[4,6,32,128]{3,2,1,0:T(8,128)(2,1)S(1)}, u32[]{:S(2)}, u32[]{:S(2)}) collective-permute-start(bf16[4,6,32,128]{3,2,1,0:T(8,128)(2,1)S(1)} %get-tuple-element.29), channel_id=1, source_target_pairs={{0,1},{1,0},{2,3},{3,2},{4,5},{5,4},{6,7},{7,6},{8,9},{9,8},{10,11... | collective-permute-start | bytes 589832 | tf_op jit(solution)/shard_map/ppermute | solution.py:167
  12.6 1.5 %collective-permute-start.7 = (bf16[4,6,32,128]{3,2,1,0:T(8,128)(2,1)S(1)}, bf16[4,6,32,128]{3,2,1,0:T(8,128)(2,1)S(1)}, u32[]{:S(2)}, u32[]{:S(2)}) collective-permute-start(bf16[4,6,32,128]{3,2,1,0:T(8,128)(2,1)S(1)} %get-tuple-element.30), channel_id=1, source_target_pairs={{0,2},{1,3},{2,0},{3,1},{4,6},{5,7},{6,4},{7,5},{8,10},{9,11},{10,... | collective-permute-start | bytes 589832 | tf_op jit(solution)/shard_map/ppermute | solution.py:167
  14.1 4.1 %collective-permute-done.6.refs_1_ = bf16[4,6,32,128]{3,2,1,0:T(8,128)(2,1)S(1)} collective-permute-done((bf16[4,6,32,128]{3,2,1,0:T(8,128)(2,1)S(1)}, bf16[4,6,32,128]{3,2,1,0:T(8,128)(2,1)S(1)}, u32[]{:S(2)}, u32[]{:S(2)}) %collective-permute-start.6) | collective-permute-done | bytes 196640 | tf_op jit(solution)/shard_map/ppermute | solution.py:167
  18.3 2.1 %collective-permute-start.4 = (s32[1,16]{1,0:T(1,128)S(1)}, s32[1,16]{1,0:T(1,128)S(1)}, u32[]{:S(2)}, u32[]{:S(2)}) collective-permute-start(s32[1,16]{1,0:T(1,128)S(1)} %add_bitcast_fusion.named), channel_id=1, source_target_pairs={{0,8},{4,12},{8,0},{12,4},{16,24},{20,28},{24,16},{28,20},{1,9},{5... | collective-permute-start | bytes 200 | tf_op jit(solution)/shard_map/ppermute | solution.py:147
  20.4 3.0 %collective-permute-done.7.refs_2_ = bf16[4,6,32,128]{3,2,1,0:T(8,128)(2,1)S(1)} collective-permute-done((bf16[4,6,32,128]{3,2,1,0:T(8,128)(2,1)S(1)}, bf16[4,6,32,128]{3,2,1,0:T(8,128)(2,1)S(1)}, u32[]{:S(2)}, u32[]{:S(2)}) %collective-permute-start.7) | collective-permute-done | bytes 196640 | tf_op jit(solution)/shard_map/ppermute | solution.py:167
  23.5 2.6 %collective-permute-start.5 = (s32[1,16]{1,0:T(1,128)S(1)}, s32[1,16]{1,0:T(1,128)S(1)}, u32[]{:S(2)}, u32[]{:S(2)}) collective-permute-start(s32[1,16]{1,0:T(1,128)S(1)} %add_bitcast_fusion.named), channel_id=1, source_target_pairs={{0,16},{4,20},{8,24},{12,28},{16,0},{20,4},{24,8},{28,12},{1,17},{... | collective-permute-start | bytes 200 | tf_op jit(solution)/shard_map/ppermute | solution.py:147
  26.0 0.1 total.4.refs_0_
  26.1 2.0 %collective-permute-done.2.mats_hbm = bf16[2048,128]{1,0:T(8,128)(2,1)S(1)} collective-permute-done((bf16[2048,128]{1,0:T(8,128)(2,1)}, bf16[2048,128]{1,0:T(8,128)(2,1)S(1)}, u32[]{:S(2)}, u32[]{:S(2)}) %collective-permute-start.2) | collective-permute-done | bytes 524320 | tf_op jit(solution)/shard_map/ppermute | solution.py:147
  28.2 0.2 collective-permute-done.3.mats_hbm
  28.4 0.1 collective-permute-done.4.named
  28.5 1.5 %collective-permute-start.9 = (bf16[2048,128]{1,0:T(8,128)(2,1)S(1)}, bf16[2048,128]{1,0:T(8,128)(2,1)S(1)}, u32[]{:S(2)}, u32[]{:S(2)}) collective-permute-start(bf16[2048,128]{1,0:T(8,128)(2,1)S(1)} %collective-permute-done.2.mats_hbm), channel_id=1, source_target_pairs={{0,8},{4,12},{8,0},{12,4},{16,24},{20,28},{24,16},{28,20},{1,9},{5... | collective-permute-start | bytes 1572872 | tf_op jit(solution)/shard_map/ppermute | solution.py:147
  29.9 0.8 %interpolate.5 = (f32[4,6,32,128]{3,2,1,0:T(8,128)S(1)}, bf16[4,6,32,128]{3,2,1,0:T(8,128)(2,1)S(1)}, bf16[4,6,32,128]{3,2,1,0:T(8,128)(2,1)S(1)}, bf16[4,6,32,128]{3,2,1,0:T(8,128)(2,1)S(1)}) custom-call(s32[1,16]{1,0:T(1,128)S(1)} %collective-permute-done.5.named, bf16[6,16,16384]{2,1,0:T(8,128)(2,1)S(1)} %copy-done.1, ...), custom_call_target="tpu_custom_call" | custom-call | tf_op jit(solution)/shard_map/interpolate/pallas_call | solution.py:60
  30.7 1.6 %collective-permute-start.10 = (bf16[4,6,32,128]{3,2,1,0:T(8,128)(2,1)S(1)}, bf16[4,6,32,128]{3,2,1,0:T(8,128)(2,1)S(1)}, u32[]{:S(2)}, u32[]{:S(2)}) collective-permute-start(bf16[4,6,32,128]{3,2,1,0:T(8,128)(2,1)S(1)} %get-tuple-element.34), channel_id=1, source_target_pairs={{0,1},{1,0},{2,3},{3,2},{4,5},{5,4},{6,7},{7,6},{8,9},{9,8},{10,11... | collective-permute-start | bytes 589832 | tf_op jit(solution)/shard_map/ppermute | solution.py:167
  32.3 1.5 %collective-permute-start.11 = (bf16[4,6,32,128]{3,2,1,0:T(8,128)(2,1)S(1)}, bf16[4,6,32,128]{3,2,1,0:T(8,128)(2,1)S(1)}, u32[]{:S(2)}, u32[]{:S(2)}) collective-permute-start(bf16[4,6,32,128]{3,2,1,0:T(8,128)(2,1)S(1)} %get-tuple-element.35), channel_id=1, source_target_pairs={{0,2},{1,3},{2,0},{3,1},{4,6},{5,7},{6,4},{7,5},{8,10},{9,11},{10,... | collective-permute-start | bytes 589832 | tf_op jit(solution)/shard_map/ppermute | solution.py:167
  33.8 0.5 collective-permute-start.12
  34.3 0.8 %interpolate.7 = (f32[4,6,32,128]{3,2,1,0:T(8,128)S(1)}, bf16[4,6,32,128]{3,2,1,0:T(8,128)(2,1)S(1)}, bf16[4,6,32,128]{3,2,1,0:T(8,128)(2,1)S(1)}, bf16[4,6,32,128]{3,2,1,0:T(8,128)(2,1)S(1)}) custom-call(s32[1,16]{1,0:T(1,128)S(1)} %collective-permute-done.4.named, bf16[6,16,16384]{2,1,0:T(8,128)(2,1)S(1)} %copy-done.1, ...), custom_call_target="tpu_custom_call" | custom-call | tf_op jit(solution)/shard_map/interpolate/pallas_call | solution.py:60
  35.0 1.6 %collective-permute-start.18 = (bf16[4,6,32,128]{3,2,1,0:T(8,128)(2,1)S(1)}, bf16[4,6,32,128]{3,2,1,0:T(8,128)(2,1)S(1)}, u32[]{:S(2)}, u32[]{:S(2)}) collective-permute-start(bf16[4,6,32,128]{3,2,1,0:T(8,128)(2,1)S(1)} %get-tuple-element.46), channel_id=1, source_target_pairs={{0,1},{1,0},{2,3},{3,2},{4,5},{5,4},{6,7},{7,6},{8,9},{9,8},{10,11... | collective-permute-start | bytes 589832 | tf_op jit(solution)/shard_map/ppermute | solution.py:167
  36.6 2.0 %collective-permute-done.10.refs_1_ = bf16[4,6,32,128]{3,2,1,0:T(8,128)(2,1)S(1)} collective-permute-done((bf16[4,6,32,128]{3,2,1,0:T(8,128)(2,1)S(1)}, bf16[4,6,32,128]{3,2,1,0:T(8,128)(2,1)S(1)}, u32[]{:S(2)}, u32[]{:S(2)}) %collective-permute-start.10) | collective-permute-done | bytes 196640 | tf_op jit(solution)/shard_map/ppermute | solution.py:167
  38.6 1.5 %collective-permute-start.19 = (bf16[4,6,32,128]{3,2,1,0:T(8,128)(2,1)S(1)}, bf16[4,6,32,128]{3,2,1,0:T(8,128)(2,1)S(1)}, u32[]{:S(2)}, u32[]{:S(2)}) collective-permute-start(bf16[4,6,32,128]{3,2,1,0:T(8,128)(2,1)S(1)} %get-tuple-element.47), channel_id=1, source_target_pairs={{0,2},{1,3},{2,0},{3,1},{4,6},{5,7},{6,4},{7,5},{8,10},{9,11},{10,... | collective-permute-start | bytes 589832 | tf_op jit(solution)/shard_map/ppermute | solution.py:167
  40.1 2.8 %collective-permute-done.11.refs_2_ = bf16[4,6,32,128]{3,2,1,0:T(8,128)(2,1)S(1)} collective-permute-done((bf16[4,6,32,128]{3,2,1,0:T(8,128)(2,1)S(1)}, bf16[4,6,32,128]{3,2,1,0:T(8,128)(2,1)S(1)}, u32[]{:S(2)}, u32[]{:S(2)}) %collective-permute-start.11) | collective-permute-done | bytes 196640 | tf_op jit(solution)/shard_map/ppermute | solution.py:167
  42.9 2.2 %collective-permute-start.1 = (s32[1,16]{1,0:T(1,128)S(1)}, s32[1,16]{1,0:T(1,128)S(1)}, u32[]{:S(2)}, u32[]{:S(2)}) collective-permute-start(s32[1,16]{1,0:T(1,128)S(1)} %add_bitcast_fusion.named), channel_id=1, source_target_pairs={{0,24},{4,28},{8,16},{12,20},{16,8},{20,12},{24,0},{28,4},{1,25},{... | collective-permute-start | bytes 200 | tf_op jit(solution)/shard_map/ppermute | solution.py:147
  45.2 0.6 collective-permute-start.20
  45.8 0.1 total.5
  45.9 1.8 %collective-permute-start.13 = (bf16[4,6,32,128]{3,2,1,0:T(8,128)(2,1)S(1)}, bf16[4,6,32,128]{3,2,1,0:T(8,128)(2,1)S(1)}, u32[]{:S(2)}, u32[]{:S(2)}) collective-permute-start(bf16[4,6,32,128]{3,2,1,0:T(8,128)(2,1)S(1)} %total.5), channel_id=1, source_target_pairs={{0,16},{4,20},{8,24},{12,28},{16,0},{20,4},{24,8},{28,12},{1,17},{... | collective-permute-start | bytes 589832 | tf_op jit(solution)/shard_map/ppermute | solution.py:147
  47.7 0.5 collective-permute-done.1.named
  48.3 0.8 %interpolate.6 = (f32[4,6,32,128]{3,2,1,0:T(8,128)S(1)}, bf16[4,6,32,128]{3,2,1,0:T(8,128)(2,1)S(1)}, bf16[4,6,32,128]{3,2,1,0:T(8,128)(2,1)S(1)}, bf16[4,6,32,128]{3,2,1,0:T(8,128)(2,1)S(1)}) custom-call(s32[1,16]{1,0:T(1,128)S(1)} %collective-permute-done.1.named, bf16[6,16,16384]{2,1,0:T(8,128)(2,1)S(1)} %copy-done.1, ...), custom_call_target="tpu_custom_call" | custom-call | tf_op jit(solution)/shard_map/interpolate/pallas_call | solution.py:60
  49.0 1.2 %collective-permute-start.14 = (bf16[4,6,32,128]{3,2,1,0:T(8,128)(2,1)S(1)}, bf16[4,6,32,128]{3,2,1,0:T(8,128)(2,1)S(1)}, u32[]{:S(2)}, u32[]{:S(2)}) collective-permute-start(bf16[4,6,32,128]{3,2,1,0:T(8,128)(2,1)S(1)} %get-tuple-element.41), channel_id=1, source_target_pairs={{0,1},{1,0},{2,3},{3,2},{4,5},{5,4},{6,7},{7,6},{8,9},{9,8},{10,11... | collective-permute-start | bytes 589832 | tf_op jit(solution)/shard_map/ppermute | solution.py:167
  50.2 1.6 %collective-permute-start.15 = (bf16[4,6,32,128]{3,2,1,0:T(8,128)(2,1)S(1)}, bf16[4,6,32,128]{3,2,1,0:T(8,128)(2,1)S(1)}, u32[]{:S(2)}, u32[]{:S(2)}) collective-permute-start(bf16[4,6,32,128]{3,2,1,0:T(8,128)(2,1)S(1)} %get-tuple-element.42), channel_id=1, source_target_pairs={{0,2},{1,3},{2,0},{3,1},{4,6},{5,7},{6,4},{7,5},{8,10},{9,11},{10,... | collective-permute-start | bytes 589832 | tf_op jit(solution)/shard_map/ppermute | solution.py:167
  51.8 1.4 %collective-permute-start.16 = (bf16[4,6,32,128]{3,2,1,0:T(8,128)(2,1)S(1)}, bf16[4,6,32,128]{3,2,1,0:T(8,128)(2,1)S(1)}, u32[]{:S(2)}, u32[]{:S(2)}) collective-permute-start(bf16[4,6,32,128]{3,2,1,0:T(8,128)(2,1)S(1)} %get-tuple-element.43), channel_id=1, source_target_pairs={{0,3},{1,2},{2,1},{3,0},{4,7},{5,6},{6,5},{7,4},{8,11},{9,10},{10,... | collective-permute-start | bytes 589832 | tf_op jit(solution)/shard_map/ppermute | solution.py:167
  53.3 0.5 collective-permute-done.20.refs_3_
  53.7 0.1 total.7
  53.9 0.8 %collective-permute-start.21 = (bf16[4,6,32,128]{3,2,1,0:T(8,128)(2,1)S(1)}, bf16[4,6,32,128]{3,2,1,0:T(8,128)(2,1)S(1)}, u32[]{:S(2)}, u32[]{:S(2)}) collective-permute-start(bf16[4,6,32,128]{3,2,1,0:T(8,128)(2,1)S(1)} %total.7), channel_id=1, source_target_pairs={{0,8},{4,12},{8,0},{12,4},{16,24},{20,28},{24,16},{28,20},{1,9},{5... | collective-permute-start | bytes 589832 | tf_op jit(solution)/shard_map/ppermute | solution.py:147
  54.7 0.0 collective-permute-done.13.refs_2_
  54.7 2.0 %collective-permute-done.14.refs_1_ = bf16[4,6,32,128]{3,2,1,0:T(8,128)(2,1)S(1)} collective-permute-done((bf16[4,6,32,128]{3,2,1,0:T(8,128)(2,1)S(1)}, bf16[4,6,32,128]{3,2,1,0:T(8,128)(2,1)S(1)}, u32[]{:S(2)}, u32[]{:S(2)}) %collective-permute-start.14) | collective-permute-done | bytes 196640 | tf_op jit(solution)/shard_map/ppermute | solution.py:167
  56.8 1.5 %collective-permute-done.15.refs_2_ = bf16[4,6,32,128]{3,2,1,0:T(8,128)(2,1)S(1)} collective-permute-done((bf16[4,6,32,128]{3,2,1,0:T(8,128)(2,1)S(1)}, bf16[4,6,32,128]{3,2,1,0:T(8,128)(2,1)S(1)}, u32[]{:S(2)}, u32[]{:S(2)}) %collective-permute-start.15) | collective-permute-done | bytes 196640 | tf_op jit(solution)/shard_map/ppermute | solution.py:167
  58.3 1.5 %collective-permute-done.16.refs_3_ = bf16[4,6,32,128]{3,2,1,0:T(8,128)(2,1)S(1)} collective-permute-done((bf16[4,6,32,128]{3,2,1,0:T(8,128)(2,1)S(1)}, bf16[4,6,32,128]{3,2,1,0:T(8,128)(2,1)S(1)}, u32[]{:S(2)}, u32[]{:S(2)}) %collective-permute-start.16) | collective-permute-done | bytes 196640 | tf_op jit(solution)/shard_map/ppermute | solution.py:167
  59.8 0.1 total.6
  59.9 2.0 %collective-permute-start.17 = (bf16[4,6,32,128]{3,2,1,0:T(8,128)(2,1)S(1)}, bf16[4,6,32,128]{3,2,1,0:T(8,128)(2,1)S(1)}, u32[]{:S(2)}, u32[]{:S(2)}) collective-permute-start(bf16[4,6,32,128]{3,2,1,0:T(8,128)(2,1)S(1)} %total.6), channel_id=1, source_target_pairs={{0,24},{4,28},{8,16},{12,20},{16,8},{20,12},{24,0},{28,4},{1,25},{... | collective-permute-start | bytes 589832 | tf_op jit(solution)/shard_map/ppermute | solution.py:147
  61.9 0.9 %finish.2.refs_1_ = bf16[4,6,128,128]{3,2,1,0:T(8,128)(2,1)} custom-call(f32[4,128]{1,0:T(4,128)S(1)} %copy-done.3, f32[4,6,32,128]{3,2,1,0:T(8,128)S(1)} %total.4.refs_0_, bf16[4,6,32,128]{3,2,1,0:T(8,128)(2,1)S(1)} %collective-permute-done.21.refs_1_, bf16[4,6,32,128]{3,2,1,0:T(8,128)(2,1)S(1)} %collective-permute-done.13.refs_2_), custom_call_target="tpu_custom_call" | custom-call | tf_op jit(solution)/shard_map/finish/pallas_call | solution.py:123
  62.8 4.7 %collective-permute-done.17.refs_0_ = bf16[4,6,32,128]{3,2,1,0:T(8,128)(2,1)S(1)} collective-permute-done((bf16[4,6,32,128]{3,2,1,0:T(8,128)(2,1)S(1)}, bf16[4,6,32,128]{3,2,1,0:T(8,128)(2,1)S(1)}, u32[]{:S(2)}, u32[]{:S(2)}) %collective-permute-start.17) | collective-permute-done | bytes 196640 | tf_op jit(solution)/shard_map/ppermute | solution.py:147
  67.5 0.7 %finish.3 = bf16[4,6,128,128]{3,2,1,0:T(8,128)(2,1)} custom-call(f32[4,128]{1,0:T(4,128)S(1)} %copy-done.3, bf16[4,6,32,128]{3,2,1,0:T(8,128)(2,1)S(1)} %collective-permute-done.17.refs_0_, bf16[4,6,128,128]{3,2,1,0:T(8,128)(2,1)} %finish.2.refs_1_), custom_call_target="tpu_custom_call", output_to_operand_aliasing={{}: (2, {})} | custom-call | tf_op jit(solution)/shard_map/finish/pallas_call | solution.py:123
  (15 shorter events, 0.1 us)
Async XLA Ops:
  0.0 6.3 %collective-permute-start = (bf16[6,16,16384]{2,1,0:T(8,128)(2,1)}, bf16[6,16,16384]{2,1,0:T(8,128)(2,1)S(1)}, u32[]{:S(2)}, u32[]{:S(2)}) collective-permute-start(bf16[6,16,16384]{2,1,0:T(8,128)(2,1)} %own_hbm.7), channel_id=1, source_target_pairs={{0,4},{4,0},{8,12},{12,8},{16,20},{20,16},{24,28},{28,24},{1,5},{5... | collective-permute-start | bytes 9437192 | tf_op jit(solution)/shard_map/ppermute | solution.py:162
  0.5 27.7 %collective-permute-start.2 = (bf16[2048,128]{1,0:T(8,128)(2,1)}, bf16[2048,128]{1,0:T(8,128)(2,1)S(1)}, u32[]{:S(2)}, u32[]{:S(2)}) collective-permute-start(bf16[2048,128]{1,0:T(8,128)(2,1)} %bitcast.3), channel_id=1, source_target_pairs={{0,16},{4,20},{8,24},{12,28},{16,0},{20,4},{24,8},{28,12},{1,17},{... | collective-permute-start | bytes 1572872 | tf_op jit(solution)/shard_map/ppermute | solution.py:147
  4.0 24.4 %collective-permute-start.3 = (bf16[2048,128]{1,0:T(8,128)(2,1)}, bf16[2048,128]{1,0:T(8,128)(2,1)S(1)}, u32[]{:S(2)}, u32[]{:S(2)}) collective-permute-start(bf16[2048,128]{1,0:T(8,128)(2,1)} %bitcast.4), channel_id=1, source_target_pairs={{0,8},{4,12},{8,0},{12,4},{16,24},{20,28},{24,16},{28,20},{1,9},{5... | collective-permute-start | bytes 1572872 | tf_op jit(solution)/shard_map/ppermute | solution.py:147
  6.3 1.9 %copy-start = (bf16[6,16,16384]{2,1,0:T(8,128)(2,1)S(1)}, bf16[6,16,16384]{2,1,0:T(8,128)(2,1)}, u32[]{:S(2)}) copy-start(bf16[6,16,16384]{2,1,0:T(8,128)(2,1)} %own_hbm.7) | copy-start | bytes 9437188
  8.2 1.0 %copy-start.2 = (bf16[1,16,128,128]{3,2,1,0:T(8,128)(2,1)S(1)}, bf16[1,16,128,128]{3,2,1,0:T(8,128)(2,1)}, u32[]{:S(2)}) copy-start(bf16[1,16,128,128]{3,2,1,0:T(8,128)(2,1)} %param.6) | copy-start | bytes 1572868
  9.2 20.7 %copy-start.1 = (bf16[6,16,16384]{2,1,0:T(8,128)(2,1)S(1)}, bf16[6,16,16384]{2,1,0:T(8,128)(2,1)}, u32[]{:S(2)}) copy-start(bf16[6,16,16384]{2,1,0:T(8,128)(2,1)} %own_hbm.7) | copy-start | bytes 9437188
  10.0 8.3 %collective-permute-start.6 = (bf16[4,6,32,128]{3,2,1,0:T(8,128)(2,1)S(1)}, bf16[4,6,32,128]{3,2,1,0:T(8,128)(2,1)S(1)}, u32[]{:S(2)}, u32[]{:S(2)}) collective-permute-start(bf16[4,6,32,128]{3,2,1,0:T(8,128)(2,1)S(1)} %get-tuple-element.29), channel_id=1, source_target_pairs={{0,1},{1,0},{2,3},{3,2},{4,5},{5,4},{6,7},{7,6},{8,9},{9,8},{10,11... | collective-permute-start | bytes 589832 | tf_op jit(solution)/shard_map/ppermute | solution.py:167
  12.6 10.9 %collective-permute-start.7 = (bf16[4,6,32,128]{3,2,1,0:T(8,128)(2,1)S(1)}, bf16[4,6,32,128]{3,2,1,0:T(8,128)(2,1)S(1)}, u32[]{:S(2)}, u32[]{:S(2)}) collective-permute-start(bf16[4,6,32,128]{3,2,1,0:T(8,128)(2,1)S(1)} %get-tuple-element.30), channel_id=1, source_target_pairs={{0,2},{1,3},{2,0},{3,1},{4,6},{5,7},{6,4},{7,5},{8,10},{9,11},{10,... | collective-permute-start | bytes 589832 | tf_op jit(solution)/shard_map/ppermute | solution.py:167
  14.1 12.0 %collective-permute-start.8 = (bf16[4,6,32,128]{3,2,1,0:T(8,128)(2,1)S(1)}, bf16[4,6,32,128]{3,2,1,0:T(8,128)(2,1)S(1)}, u32[]{:S(2)}, u32[]{:S(2)}) collective-permute-start(bf16[4,6,32,128]{3,2,1,0:T(8,128)(2,1)S(1)} %get-tuple-element.31), channel_id=1, source_target_pairs={{0,3},{1,2},{2,1},{3,0},{4,7},{5,6},{6,5},{7,4},{8,11},{9,10},{10,... | collective-permute-start | bytes 589832 | tf_op jit(solution)/shard_map/ppermute | solution.py:167
  18.3 10.2 %collective-permute-start.4 = (s32[1,16]{1,0:T(1,128)S(1)}, s32[1,16]{1,0:T(1,128)S(1)}, u32[]{:S(2)}, u32[]{:S(2)}) collective-permute-start(s32[1,16]{1,0:T(1,128)S(1)} %add_bitcast_fusion.named), channel_id=1, source_target_pairs={{0,8},{4,12},{8,0},{12,4},{16,24},{20,28},{24,16},{28,20},{1,9},{5... | collective-permute-start | bytes 200 | tf_op jit(solution)/shard_map/ppermute | solution.py:147
  23.5 5.0 %collective-permute-start.5 = (s32[1,16]{1,0:T(1,128)S(1)}, s32[1,16]{1,0:T(1,128)S(1)}, u32[]{:S(2)}, u32[]{:S(2)}) collective-permute-start(s32[1,16]{1,0:T(1,128)S(1)} %add_bitcast_fusion.named), channel_id=1, source_target_pairs={{0,16},{4,20},{8,24},{12,28},{16,0},{20,4},{24,8},{28,12},{1,17},{... | collective-permute-start | bytes 200 | tf_op jit(solution)/shard_map/ppermute | solution.py:147
  28.5 17.4 %collective-permute-start.9 = (bf16[2048,128]{1,0:T(8,128)(2,1)S(1)}, bf16[2048,128]{1,0:T(8,128)(2,1)S(1)}, u32[]{:S(2)}, u32[]{:S(2)}) collective-permute-start(bf16[2048,128]{1,0:T(8,128)(2,1)S(1)} %collective-permute-done.2.mats_hbm), channel_id=1, source_target_pairs={{0,8},{4,12},{8,0},{12,4},{16,24},{20,28},{24,16},{28,20},{1,9},{5... | collective-permute-start | bytes 1572872 | tf_op jit(solution)/shard_map/ppermute | solution.py:147
  30.7 7.9 %collective-permute-start.10 = (bf16[4,6,32,128]{3,2,1,0:T(8,128)(2,1)S(1)}, bf16[4,6,32,128]{3,2,1,0:T(8,128)(2,1)S(1)}, u32[]{:S(2)}, u32[]{:S(2)}) collective-permute-start(bf16[4,6,32,128]{3,2,1,0:T(8,128)(2,1)S(1)} %get-tuple-element.34), channel_id=1, source_target_pairs={{0,1},{1,0},{2,3},{3,2},{4,5},{5,4},{6,7},{7,6},{8,9},{9,8},{10,11... | collective-permute-start | bytes 589832 | tf_op jit(solution)/shard_map/ppermute | solution.py:167
  32.3 10.7 %collective-permute-start.11 = (bf16[4,6,32,128]{3,2,1,0:T(8,128)(2,1)S(1)}, bf16[4,6,32,128]{3,2,1,0:T(8,128)(2,1)S(1)}, u32[]{:S(2)}, u32[]{:S(2)}) collective-permute-start(bf16[4,6,32,128]{3,2,1,0:T(8,128)(2,1)S(1)} %get-tuple-element.35), channel_id=1, source_target_pairs={{0,2},{1,3},{2,0},{3,1},{4,6},{5,7},{6,4},{7,5},{8,10},{9,11},{10,... | collective-permute-start | bytes 589832 | tf_op jit(solution)/shard_map/ppermute | solution.py:167
  33.8 11.4 %collective-permute-start.12 = (bf16[4,6,32,128]{3,2,1,0:T(8,128)(2,1)S(1)}, bf16[4,6,32,128]{3,2,1,0:T(8,128)(2,1)S(1)}, u32[]{:S(2)}, u32[]{:S(2)}) collective-permute-start(bf16[4,6,32,128]{3,2,1,0:T(8,128)(2,1)S(1)} %get-tuple-element.36), channel_id=1, source_target_pairs={{0,3},{1,2},{2,1},{3,0},{4,7},{5,6},{6,5},{7,4},{8,11},{9,10},{10,... | collective-permute-start | bytes 589832 | tf_op jit(solution)/shard_map/ppermute | solution.py:167
  35.0 15.2 %collective-permute-start.18 = (bf16[4,6,32,128]{3,2,1,0:T(8,128)(2,1)S(1)}, bf16[4,6,32,128]{3,2,1,0:T(8,128)(2,1)S(1)}, u32[]{:S(2)}, u32[]{:S(2)}) collective-permute-start(bf16[4,6,32,128]{3,2,1,0:T(8,128)(2,1)S(1)} %get-tuple-element.46), channel_id=1, source_target_pairs={{0,1},{1,0},{2,3},{3,2},{4,5},{5,4},{6,7},{7,6},{8,9},{9,8},{10,11... | collective-permute-start | bytes 589832 | tf_op jit(solution)/shard_map/ppermute | solution.py:167
  38.6 13.2 %collective-permute-start.19 = (bf16[4,6,32,128]{3,2,1,0:T(8,128)(2,1)S(1)}, bf16[4,6,32,128]{3,2,1,0:T(8,128)(2,1)S(1)}, u32[]{:S(2)}, u32[]{:S(2)}) collective-permute-start(bf16[4,6,32,128]{3,2,1,0:T(8,128)(2,1)S(1)} %get-tuple-element.47), channel_id=1, source_target_pairs={{0,2},{1,3},{2,0},{3,1},{4,6},{5,7},{6,4},{7,5},{8,10},{9,11},{10,... | collective-permute-start | bytes 589832 | tf_op jit(solution)/shard_map/ppermute | solution.py:167
  42.9 5.3 %collective-permute-start.1 = (s32[1,16]{1,0:T(1,128)S(1)}, s32[1,16]{1,0:T(1,128)S(1)}, u32[]{:S(2)}, u32[]{:S(2)}) collective-permute-start(s32[1,16]{1,0:T(1,128)S(1)} %add_bitcast_fusion.named), channel_id=1, source_target_pairs={{0,24},{4,28},{8,16},{12,20},{16,8},{20,12},{24,0},{28,4},{1,25},{... | collective-permute-start | bytes 200 | tf_op jit(solution)/shard_map/ppermute | solution.py:147
  45.2 8.6 %collective-permute-start.20 = (bf16[4,6,32,128]{3,2,1,0:T(8,128)(2,1)S(1)}, bf16[4,6,32,128]{3,2,1,0:T(8,128)(2,1)S(1)}, u32[]{:S(2)}, u32[]{:S(2)}) collective-permute-start(bf16[4,6,32,128]{3,2,1,0:T(8,128)(2,1)S(1)} %get-tuple-element.48), channel_id=1, source_target_pairs={{0,3},{1,2},{2,1},{3,0},{4,7},{5,6},{6,5},{7,4},{8,11},{9,10},{10,... | collective-permute-start | bytes 589832 | tf_op jit(solution)/shard_map/ppermute | solution.py:167
  45.9 16.1 %copy-start.3 = (f32[4,128]{1,0:T(4,128)S(1)}, f32[4,128]{1,0:T(4,128)}, u32[]{:S(2)}) copy-start(f32[4,128]{1,0:T(4,128)} %weight_ref.3) | copy-start | bytes 6148
  45.9 8.8 %collective-permute-start.13 = (bf16[4,6,32,128]{3,2,1,0:T(8,128)(2,1)S(1)}, bf16[4,6,32,128]{3,2,1,0:T(8,128)(2,1)S(1)}, u32[]{:S(2)}, u32[]{:S(2)}) collective-permute-start(bf16[4,6,32,128]{3,2,1,0:T(8,128)(2,1)S(1)} %total.5), channel_id=1, source_target_pairs={{0,16},{4,20},{8,24},{12,28},{16,0},{20,4},{24,8},{28,12},{1,17},{... | collective-permute-start | bytes 589832 | tf_op jit(solution)/shard_map/ppermute | solution.py:147
  49.0 7.7 %collective-permute-start.14 = (bf16[4,6,32,128]{3,2,1,0:T(8,128)(2,1)S(1)}, bf16[4,6,32,128]{3,2,1,0:T(8,128)(2,1)S(1)}, u32[]{:S(2)}, u32[]{:S(2)}) collective-permute-start(bf16[4,6,32,128]{3,2,1,0:T(8,128)(2,1)S(1)} %get-tuple-element.41), channel_id=1, source_target_pairs={{0,1},{1,0},{2,3},{3,2},{4,5},{5,4},{6,7},{7,6},{8,9},{9,8},{10,11... | collective-permute-start | bytes 589832 | tf_op jit(solution)/shard_map/ppermute | solution.py:167
  50.2 8.1 %collective-permute-start.15 = (bf16[4,6,32,128]{3,2,1,0:T(8,128)(2,1)S(1)}, bf16[4,6,32,128]{3,2,1,0:T(8,128)(2,1)S(1)}, u32[]{:S(2)}, u32[]{:S(2)}) collective-permute-start(bf16[4,6,32,128]{3,2,1,0:T(8,128)(2,1)S(1)} %get-tuple-element.42), channel_id=1, source_target_pairs={{0,2},{1,3},{2,0},{3,1},{4,6},{5,7},{6,4},{7,5},{8,10},{9,11},{10,... | collective-permute-start | bytes 589832 | tf_op jit(solution)/shard_map/ppermute | solution.py:167
  51.8 8.0 %collective-permute-start.16 = (bf16[4,6,32,128]{3,2,1,0:T(8,128)(2,1)S(1)}, bf16[4,6,32,128]{3,2,1,0:T(8,128)(2,1)S(1)}, u32[]{:S(2)}, u32[]{:S(2)}) collective-permute-start(bf16[4,6,32,128]{3,2,1,0:T(8,128)(2,1)S(1)} %get-tuple-element.43), channel_id=1, source_target_pairs={{0,3},{1,2},{2,1},{3,0},{4,7},{5,6},{6,5},{7,4},{8,11},{9,10},{10,... | collective-permute-start | bytes 589832 | tf_op jit(solution)/shard_map/ppermute | solution.py:167
  53.9 8.1 %collective-permute-start.21 = (bf16[4,6,32,128]{3,2,1,0:T(8,128)(2,1)S(1)}, bf16[4,6,32,128]{3,2,1,0:T(8,128)(2,1)S(1)}, u32[]{:S(2)}, u32[]{:S(2)}) collective-permute-start(bf16[4,6,32,128]{3,2,1,0:T(8,128)(2,1)S(1)} %total.7), channel_id=1, source_target_pairs={{0,8},{4,12},{8,0},{12,4},{16,24},{20,28},{24,16},{28,20},{1,9},{5... | collective-permute-start | bytes 589832 | tf_op jit(solution)/shard_map/ppermute | solution.py:147
  59.9 7.6 %collective-permute-start.17 = (bf16[4,6,32,128]{3,2,1,0:T(8,128)(2,1)S(1)}, bf16[4,6,32,128]{3,2,1,0:T(8,128)(2,1)S(1)}, u32[]{:S(2)}, u32[]{:S(2)}) collective-permute-start(bf16[4,6,32,128]{3,2,1,0:T(8,128)(2,1)S(1)} %total.6), channel_id=1, source_target_pairs={{0,24},{4,28},{8,16},{12,20},{16,8},{20,12},{24,0},{28,4},{1,25},{... | collective-permute-start | bytes 589832 | tf_op jit(solution)/shard_map/ppermute | solution.py:147

commit v4 on v3

--- a/solution.py
+++ b/solution.py
@@ -10,7 +10,7 @@
 CORES = 2
 LIMIT = pltpu.CompilerParams(vmem_limit_bytes=32 * 2**20)
 
-ORDER = {('name', 1, 0): [('face', 0, 0)], ('name', 2, 0): [('face', 0, 0)], ('name', 3, 0): [('face', 0, 0)], ('mats', 3, 0): [('mats', 1, 0), ('name', 1, 0), ('name', 2, 0), ('sum', 0, 0)], ('face', 3, 0): [('sum', 2, 0)], ('home', 2, 0): [('mats', 3, 0)], ('sum', 1, 0): [('face', 3, 0)], ('sum', 3, 0): [('home', 2, 0)]}
+ORDER = {('name', 1, 0): [('face', 0, 0)], ('name', 2, 0): [('face', 0, 0)], ('name', 3, 0): [('face', 0, 0)], ('mats', 3, 0): [('mats', 1, 0), ('name', 1, 0), ('name', 2, 0), ('sum', 0, 0)], ('home', 2, 0): [('mats', 3, 0)], ('sum', 3, 0): [('home', 2, 0)]}
 
 
 def place():

time: 68.5 us -> 68.1 us (level)
    ppermute x12, waiting for transfers between devices: 17.5 us -> 16.7 us  [make(): lax.ppermute(wait(get('face', turn)[d]), 'box', [(b, b ^ d) for b in rang...]
  transfers between devices with their start and end apart: 22 -> 22, of which waited for: 13 -> 12; matrix products, arithmetic and copies ran while one was open for 1% -> 1% of each run, Pallas kernels for 6% -> 6%
where the time goes in v4:
time: 68.1 us; the launch traced here: 67.9 us
  starting transfers between devices  34.3 us (50%)
  waiting for transfers between devices  24.9 us (37%)
  Pallas kernels  4.98 us (7%)
  local copies, waits for them, and re-layouts  2.94 us (4%)
    ppermute x9, starting transfers between devices, along(): return lax.ppermute(x, 'tm', pairs)  18.4 us
    ppermute x12, waiting for transfers between devices, make(): lax.ppermute(wait(get('face', turn)[d]), 'box', [(b, b ^ d) for b in rang...  16.7 us
    ppermute x12, starting transfers between devices, make(): lax.ppermute(wait(get('face', turn)[d]), 'box', [(b, b ^ d) for b in rang...  15.5 us
    ppermute x9, waiting for transfers between devices, along(): return lax.ppermute(x, 'tm', pairs)  8.18 us
    pallas_call x4, Pallas kernels, interpolate(): pl.pallas_call(functools.partial(interpolate_kernel, turn, boxes, blocks)...  3.01 us
    unnamed x8, local copies, waits for them, and re-layouts  2.94 us
    pallas_call x2, Pallas kernels, finish(): pl.pallas_call(functools.partial(finish_kernel, turns, len(pieces)), in_s...  1.58 us
  transfers between devices with their start and end apart: 22, of which 12 were waited for; matrix products, arithmetic and copies ran while one was open for 1% of the time, Pallas kernels for 6%

profile of v4, /device:TPU:0, one launch (start us, length us, event | category | flops | bytes accessed | tf_op | source)
XLA Modules:
  0.0 67.9 jit_solution(1387117198723066149)
XLA Ops:
  0.0 0.5 collective-permute-start
  0.5 2.6 %collective-permute-start.3 = (bf16[2048,128]{1,0:T(8,128)(2,1)}, bf16[2048,128]{1,0:T(8,128)(2,1)S(1)}, u32[]{:S(2)}, u32[]{:S(2)}) collective-permute-start(bf16[2048,128]{1,0:T(8,128)(2,1)} %bitcast.3), channel_id=1, source_target_pairs={{0,8},{4,12},{8,0},{12,4},{16,24},{20,28},{24,16},{28,20},{1,9},{5... | collective-permute-start | bytes 1572872 | tf_op jit(solution)/shard_map/ppermute | solution.py:147
  3.0 2.6 %collective-permute-start.2 = (bf16[2048,128]{1,0:T(8,128)(2,1)}, bf16[2048,128]{1,0:T(8,128)(2,1)S(1)}, u32[]{:S(2)}, u32[]{:S(2)}) collective-permute-start(bf16[2048,128]{1,0:T(8,128)(2,1)} %bitcast.4), channel_id=1, source_target_pairs={{0,16},{4,20},{8,24},{12,28},{16,0},{20,4},{24,8},{28,12},{1,17},{... | collective-permute-start | bytes 1572872 | tf_op jit(solution)/shard_map/ppermute | solution.py:147
  5.6 0.7 add_bitcast_fusion.named
  6.3 1.9 %copy-done = bf16[6,16,16384]{2,1,0:T(8,128)(2,1)S(1)} copy-done((bf16[6,16,16384]{2,1,0:T(8,128)(2,1)S(1)}, bf16[6,16,16384]{2,1,0:T(8,128)(2,1)}, u32[]{:S(2)}) %copy-start) | copy-done | bytes 3145752
  8.2 1.0 %copy-done.2 = bf16[1,16,128,128]{3,2,1,0:T(8,128)(2,1)S(1)} copy-done((bf16[1,16,128,128]{3,2,1,0:T(8,128)(2,1)S(1)}, bf16[1,16,128,128]{3,2,1,0:T(8,128)(2,1)}, u32[]{:S(2)}) %copy-start.2) | copy-done | bytes 524312
  9.2 0.8 %interpolate.4 = (f32[4,6,32,128]{3,2,1,0:T(8,128)S(1)}, bf16[4,6,32,128]{3,2,1,0:T(8,128)(2,1)S(1)}, bf16[4,6,32,128]{3,2,1,0:T(8,128)(2,1)S(1)}, bf16[4,6,32,128]{3,2,1,0:T(8,128)(2,1)S(1)}) custom-call(s32[1,16]{1,0:T(1,128)S(1)} %add_bitcast_fusion.named, bf16[6,16,16384]{2,1,0:T(8,128)(2,1)S(1)} %copy-done, ...), custom_call_target="tpu_custom_call" | custom-call | tf_op jit(solution)/shard_map/interpolate/pallas_call | solution.py:60
  10.0 2.6 %collective-permute-start.6 = (bf16[4,6,32,128]{3,2,1,0:T(8,128)(2,1)S(1)}, bf16[4,6,32,128]{3,2,1,0:T(8,128)(2,1)S(1)}, u32[]{:S(2)}, u32[]{:S(2)}) collective-permute-start(bf16[4,6,32,128]{3,2,1,0:T(8,128)(2,1)S(1)} %get-tuple-element.27), channel_id=1, source_target_pairs={{0,1},{1,0},{2,3},{3,2},{4,5},{5,4},{6,7},{7,6},{8,9},{9,8},{10,11... | collective-permute-start | bytes 589832 | tf_op jit(solution)/shard_map/ppermute | solution.py:167
  12.6 1.5 %collective-permute-start.7 = (bf16[4,6,32,128]{3,2,1,0:T(8,128)(2,1)S(1)}, bf16[4,6,32,128]{3,2,1,0:T(8,128)(2,1)S(1)}, u32[]{:S(2)}, u32[]{:S(2)}) collective-permute-start(bf16[4,6,32,128]{3,2,1,0:T(8,128)(2,1)S(1)} %get-tuple-element.28), channel_id=1, source_target_pairs={{0,2},{1,3},{2,0},{3,1},{4,6},{5,7},{6,4},{7,5},{8,10},{9,11},{10,... | collective-permute-start | bytes 589832 | tf_op jit(solution)/shard_map/ppermute | solution.py:167
  14.1 0.0 collective-permute-start.8
  14.1 4.1 %collective-permute-done.6.refs_1_ = bf16[4,6,32,128]{3,2,1,0:T(8,128)(2,1)S(1)} collective-permute-done((bf16[4,6,32,128]{3,2,1,0:T(8,128)(2,1)S(1)}, bf16[4,6,32,128]{3,2,1,0:T(8,128)(2,1)S(1)}, u32[]{:S(2)}, u32[]{:S(2)}) %collective-permute-start.6) | collective-permute-done | bytes 196640 | tf_op jit(solution)/shard_map/ppermute | solution.py:167
  18.3 2.1 %collective-permute-start.4 = (s32[1,16]{1,0:T(1,128)S(1)}, s32[1,16]{1,0:T(1,128)S(1)}, u32[]{:S(2)}, u32[]{:S(2)}) collective-permute-start(s32[1,16]{1,0:T(1,128)S(1)} %add_bitcast_fusion.named), channel_id=1, source_target_pairs={{0,8},{4,12},{8,0},{12,4},{16,24},{20,28},{24,16},{28,20},{1,9},{5... | collective-permute-start | bytes 200 | tf_op jit(solution)/shard_map/ppermute | solution.py:147
  20.4 3.0 %collective-permute-done.7.refs_2_ = bf16[4,6,32,128]{3,2,1,0:T(8,128)(2,1)S(1)} collective-permute-done((bf16[4,6,32,128]{3,2,1,0:T(8,128)(2,1)S(1)}, bf16[4,6,32,128]{3,2,1,0:T(8,128)(2,1)S(1)}, u32[]{:S(2)}, u32[]{:S(2)}) %collective-permute-start.7) | collective-permute-done | bytes 196640 | tf_op jit(solution)/shard_map/ppermute | solution.py:167
  23.5 2.6 %collective-permute-start.5 = (s32[1,16]{1,0:T(1,128)S(1)}, s32[1,16]{1,0:T(1,128)S(1)}, u32[]{:S(2)}, u32[]{:S(2)}) collective-permute-start(s32[1,16]{1,0:T(1,128)S(1)} %add_bitcast_fusion.named), channel_id=1, source_target_pairs={{0,16},{4,20},{8,24},{12,28},{16,0},{20,4},{24,8},{28,12},{1,17},{... | collective-permute-start | bytes 200 | tf_op jit(solution)/shard_map/ppermute | solution.py:147
  26.0 0.1 total.4.refs_0_
  26.1 0.8 %collective-permute-done.3.mats_hbm = bf16[2048,128]{1,0:T(8,128)(2,1)S(1)} collective-permute-done((bf16[2048,128]{1,0:T(8,128)(2,1)}, bf16[2048,128]{1,0:T(8,128)(2,1)S(1)}, u32[]{:S(2)}, u32[]{:S(2)}) %collective-permute-start.3) | collective-permute-done | bytes 524320 | tf_op jit(solution)/shard_map/ppermute | solution.py:147
  26.9 2.6 %collective-permute-done.2.mats_hbm = bf16[2048,128]{1,0:T(8,128)(2,1)S(1)} collective-permute-done((bf16[2048,128]{1,0:T(8,128)(2,1)}, bf16[2048,128]{1,0:T(8,128)(2,1)S(1)}, u32[]{:S(2)}, u32[]{:S(2)}) %collective-permute-start.2) | collective-permute-done | bytes 524320 | tf_op jit(solution)/shard_map/ppermute | solution.py:147
  29.5 0.1 collective-permute-done.5.named
  29.6 0.4 collective-permute-start.9
  30.0 0.8 %interpolate.6 = (f32[4,6,32,128]{3,2,1,0:T(8,128)S(1)}, bf16[4,6,32,128]{3,2,1,0:T(8,128)(2,1)S(1)}, bf16[4,6,32,128]{3,2,1,0:T(8,128)(2,1)S(1)}, bf16[4,6,32,128]{3,2,1,0:T(8,128)(2,1)S(1)}) custom-call(s32[1,16]{1,0:T(1,128)S(1)} %collective-permute-done.5.named, bf16[6,16,16384]{2,1,0:T(8,128)(2,1)S(1)} %copy-done.1, ...), custom_call_target="tpu_custom_call" | custom-call | tf_op jit(solution)/shard_map/interpolate/pallas_call | solution.py:60
  30.8 1.6 %collective-permute-start.10 = (bf16[4,6,32,128]{3,2,1,0:T(8,128)(2,1)S(1)}, bf16[4,6,32,128]{3,2,1,0:T(8,128)(2,1)S(1)}, u32[]{:S(2)}, u32[]{:S(2)}) collective-permute-start(bf16[4,6,32,128]{3,2,1,0:T(8,128)(2,1)S(1)} %get-tuple-element.33), channel_id=1, source_target_pairs={{0,1},{1,0},{2,3},{3,2},{4,5},{5,4},{6,7},{7,6},{8,9},{9,8},{10,11... | collective-permute-start | bytes 589832 | tf_op jit(solution)/shard_map/ppermute | solution.py:167
  32.3 1.5 %collective-permute-start.11 = (bf16[4,6,32,128]{3,2,1,0:T(8,128)(2,1)S(1)}, bf16[4,6,32,128]{3,2,1,0:T(8,128)(2,1)S(1)}, u32[]{:S(2)}, u32[]{:S(2)}) collective-permute-start(bf16[4,6,32,128]{3,2,1,0:T(8,128)(2,1)S(1)} %get-tuple-element.34), channel_id=1, source_target_pairs={{0,2},{1,3},{2,0},{3,1},{4,6},{5,7},{6,4},{7,5},{8,10},{9,11},{10,... | collective-permute-start | bytes 589832 | tf_op jit(solution)/shard_map/ppermute | solution.py:167
  33.8 0.5 collective-permute-start.12
  34.3 0.8 %interpolate.7 = (f32[4,6,32,128]{3,2,1,0:T(8,128)S(1)}, bf16[4,6,32,128]{3,2,1,0:T(8,128)(2,1)S(1)}, bf16[4,6,32,128]{3,2,1,0:T(8,128)(2,1)S(1)}, bf16[4,6,32,128]{3,2,1,0:T(8,128)(2,1)S(1)}) custom-call(s32[1,16]{1,0:T(1,128)S(1)} %collective-permute-done.4.named, bf16[6,16,16384]{2,1,0:T(8,128)(2,1)S(1)} %copy-done.1, ...), custom_call_target="tpu_custom_call" | custom-call | tf_op jit(solution)/shard_map/interpolate/pallas_call | solution.py:60
  35.1 1.6 %collective-permute-start.18 = (bf16[4,6,32,128]{3,2,1,0:T(8,128)(2,1)S(1)}, bf16[4,6,32,128]{3,2,1,0:T(8,128)(2,1)S(1)}, u32[]{:S(2)}, u32[]{:S(2)}) collective-permute-start(bf16[4,6,32,128]{3,2,1,0:T(8,128)(2,1)S(1)} %get-tuple-element.42), channel_id=1, source_target_pairs={{0,1},{1,0},{2,3},{3,2},{4,5},{5,4},{6,7},{7,6},{8,9},{9,8},{10,11... | collective-permute-start | bytes 589832 | tf_op jit(solution)/shard_map/ppermute | solution.py:167
  36.6 2.0 %collective-permute-done.10.refs_1_ = bf16[4,6,32,128]{3,2,1,0:T(8,128)(2,1)S(1)} collective-permute-done((bf16[4,6,32,128]{3,2,1,0:T(8,128)(2,1)S(1)}, bf16[4,6,32,128]{3,2,1,0:T(8,128)(2,1)S(1)}, u32[]{:S(2)}, u32[]{:S(2)}) %collective-permute-start.10) | collective-permute-done | bytes 196640 | tf_op jit(solution)/shard_map/ppermute | solution.py:167
  38.6 1.5 %collective-permute-start.19 = (bf16[4,6,32,128]{3,2,1,0:T(8,128)(2,1)S(1)}, bf16[4,6,32,128]{3,2,1,0:T(8,128)(2,1)S(1)}, u32[]{:S(2)}, u32[]{:S(2)}) collective-permute-start(bf16[4,6,32,128]{3,2,1,0:T(8,128)(2,1)S(1)} %get-tuple-element.43), channel_id=1, source_target_pairs={{0,2},{1,3},{2,0},{3,1},{4,6},{5,7},{6,4},{7,5},{8,10},{9,11},{10,... | collective-permute-start | bytes 589832 | tf_op jit(solution)/shard_map/ppermute | solution.py:167
  40.2 2.8 %collective-permute-done.11.refs_2_ = bf16[4,6,32,128]{3,2,1,0:T(8,128)(2,1)S(1)} collective-permute-done((bf16[4,6,32,128]{3,2,1,0:T(8,128)(2,1)S(1)}, bf16[4,6,32,128]{3,2,1,0:T(8,128)(2,1)S(1)}, u32[]{:S(2)}, u32[]{:S(2)}) %collective-permute-start.11) | collective-permute-done | bytes 196640 | tf_op jit(solution)/shard_map/ppermute | solution.py:167
  42.9 2.1 %collective-permute-start.1 = (s32[1,16]{1,0:T(1,128)S(1)}, s32[1,16]{1,0:T(1,128)S(1)}, u32[]{:S(2)}, u32[]{:S(2)}) collective-permute-start(s32[1,16]{1,0:T(1,128)S(1)} %add_bitcast_fusion.named), channel_id=1, source_target_pairs={{0,24},{4,28},{8,16},{12,20},{16,8},{20,12},{24,0},{28,4},{1,25},{... | collective-permute-start | bytes 200 | tf_op jit(solution)/shard_map/ppermute | solution.py:147
  45.0 0.6 collective-permute-start.20
  45.6 0.1 total.5
  45.7 0.0 copy-start.3
  45.7 2.3 %collective-permute-start.13 = (bf16[4,6,32,128]{3,2,1,0:T(8,128)(2,1)S(1)}, bf16[4,6,32,128]{3,2,1,0:T(8,128)(2,1)S(1)}, u32[]{:S(2)}, u32[]{:S(2)}) collective-permute-start(bf16[4,6,32,128]{3,2,1,0:T(8,128)(2,1)S(1)} %total.5), channel_id=1, source_target_pairs={{0,16},{4,20},{8,24},{12,28},{16,0},{20,4},{24,8},{28,12},{1,17},{... | collective-permute-start | bytes 589832 | tf_op jit(solution)/shard_map/ppermute | solution.py:147
  48.0 0.3 collective-permute-done.1.named
  48.4 0.8 %interpolate.5 = (f32[4,6,32,128]{3,2,1,0:T(8,128)S(1)}, bf16[4,6,32,128]{3,2,1,0:T(8,128)(2,1)S(1)}, bf16[4,6,32,128]{3,2,1,0:T(8,128)(2,1)S(1)}, bf16[4,6,32,128]{3,2,1,0:T(8,128)(2,1)S(1)}) custom-call(s32[1,16]{1,0:T(1,128)S(1)} %collective-permute-done.1.named, bf16[6,16,16384]{2,1,0:T(8,128)(2,1)S(1)} %copy-done.1, ...), custom_call_target="tpu_custom_call" | custom-call | tf_op jit(solution)/shard_map/interpolate/pallas_call | solution.py:60
  49.1 1.9 %collective-permute-start.14 = (bf16[4,6,32,128]{3,2,1,0:T(8,128)(2,1)S(1)}, bf16[4,6,32,128]{3,2,1,0:T(8,128)(2,1)S(1)}, u32[]{:S(2)}, u32[]{:S(2)}) collective-permute-start(bf16[4,6,32,128]{3,2,1,0:T(8,128)(2,1)S(1)} %get-tuple-element.38), channel_id=1, source_target_pairs={{0,1},{1,0},{2,3},{3,2},{4,5},{5,4},{6,7},{7,6},{8,9},{9,8},{10,11... | collective-permute-start | bytes 589832 | tf_op jit(solution)/shard_map/ppermute | solution.py:167
  51.0 0.8 %collective-permute-start.15 = (bf16[4,6,32,128]{3,2,1,0:T(8,128)(2,1)S(1)}, bf16[4,6,32,128]{3,2,1,0:T(8,128)(2,1)S(1)}, u32[]{:S(2)}, u32[]{:S(2)}) collective-permute-start(bf16[4,6,32,128]{3,2,1,0:T(8,128)(2,1)S(1)} %get-tuple-element.39), channel_id=1, source_target_pairs={{0,2},{1,3},{2,0},{3,1},{4,6},{5,7},{6,4},{7,5},{8,10},{9,11},{10,... | collective-permute-start | bytes 589832 | tf_op jit(solution)/shard_map/ppermute | solution.py:167
  51.8 1.4 %collective-permute-start.16 = (bf16[4,6,32,128]{3,2,1,0:T(8,128)(2,1)S(1)}, bf16[4,6,32,128]{3,2,1,0:T(8,128)(2,1)S(1)}, u32[]{:S(2)}, u32[]{:S(2)}) collective-permute-start(bf16[4,6,32,128]{3,2,1,0:T(8,128)(2,1)S(1)} %get-tuple-element.40), channel_id=1, source_target_pairs={{0,3},{1,2},{2,1},{3,0},{4,7},{5,6},{6,5},{7,4},{8,11},{9,10},{10,... | collective-permute-start | bytes 589832 | tf_op jit(solution)/shard_map/ppermute | solution.py:167
  53.2 0.6 collective-permute-done.20.refs_3_
  53.9 0.1 total.7
  54.0 1.4 %collective-permute-start.21 = (bf16[4,6,32,128]{3,2,1,0:T(8,128)(2,1)S(1)}, bf16[4,6,32,128]{3,2,1,0:T(8,128)(2,1)S(1)}, u32[]{:S(2)}, u32[]{:S(2)}) collective-permute-start(bf16[4,6,32,128]{3,2,1,0:T(8,128)(2,1)S(1)} %total.7), channel_id=1, source_target_pairs={{0,8},{4,12},{8,0},{12,4},{16,24},{20,28},{24,16},{28,20},{1,9},{5... | collective-permute-start | bytes 589832 | tf_op jit(solution)/shard_map/ppermute | solution.py:147
  55.3 1.6 %collective-permute-done.14.refs_1_ = bf16[4,6,32,128]{3,2,1,0:T(8,128)(2,1)S(1)} collective-permute-done((bf16[4,6,32,128]{3,2,1,0:T(8,128)(2,1)S(1)}, bf16[4,6,32,128]{3,2,1,0:T(8,128)(2,1)S(1)}, u32[]{:S(2)}, u32[]{:S(2)}) %collective-permute-start.14) | collective-permute-done | bytes 196640 | tf_op jit(solution)/shard_map/ppermute | solution.py:167
  56.9 2.5 %collective-permute-done.15.refs_2_ = bf16[4,6,32,128]{3,2,1,0:T(8,128)(2,1)S(1)} collective-permute-done((bf16[4,6,32,128]{3,2,1,0:T(8,128)(2,1)S(1)}, bf16[4,6,32,128]{3,2,1,0:T(8,128)(2,1)S(1)}, u32[]{:S(2)}, u32[]{:S(2)}) %collective-permute-start.15) | collective-permute-done | bytes 196640 | tf_op jit(solution)/shard_map/ppermute | solution.py:167
  59.5 0.1 total.6
  59.6 2.3 %collective-permute-start.17 = (bf16[4,6,32,128]{3,2,1,0:T(8,128)(2,1)S(1)}, bf16[4,6,32,128]{3,2,1,0:T(8,128)(2,1)S(1)}, u32[]{:S(2)}, u32[]{:S(2)}) collective-permute-start(bf16[4,6,32,128]{3,2,1,0:T(8,128)(2,1)S(1)} %total.6), channel_id=1, source_target_pairs={{0,24},{4,28},{8,16},{12,20},{16,8},{20,12},{24,0},{28,4},{1,25},{... | collective-permute-start | bytes 589832 | tf_op jit(solution)/shard_map/ppermute | solution.py:147
  61.9 0.9 %finish.2.refs_1_ = bf16[4,6,128,128]{3,2,1,0:T(8,128)(2,1)} custom-call(f32[4,128]{1,0:T(4,128)S(1)} %copy-done.3, f32[4,6,32,128]{3,2,1,0:T(8,128)S(1)} %total.4.refs_0_, bf16[4,6,32,128]{3,2,1,0:T(8,128)(2,1)S(1)} %collective-permute-done.21.refs_1_, bf16[4,6,32,128]{3,2,1,0:T(8,128)(2,1)S(1)} %collective-permute-done.13.refs_2_), custom_call_target="tpu_custom_call" | custom-call | tf_op jit(solution)/shard_map/finish/pallas_call | solution.py:123
  62.8 4.4 %collective-permute-done.17.refs_0_ = bf16[4,6,32,128]{3,2,1,0:T(8,128)(2,1)S(1)} collective-permute-done((bf16[4,6,32,128]{3,2,1,0:T(8,128)(2,1)S(1)}, bf16[4,6,32,128]{3,2,1,0:T(8,128)(2,1)S(1)}, u32[]{:S(2)}, u32[]{:S(2)}) %collective-permute-start.17) | collective-permute-done | bytes 196640 | tf_op jit(solution)/shard_map/ppermute | solution.py:147
  67.2 0.7 %finish.3 = bf16[4,6,128,128]{3,2,1,0:T(8,128)(2,1)} custom-call(f32[4,128]{1,0:T(4,128)S(1)} %copy-done.3, bf16[4,6,32,128]{3,2,1,0:T(8,128)(2,1)S(1)} %collective-permute-done.17.refs_0_, bf16[4,6,128,128]{3,2,1,0:T(8,128)(2,1)} %finish.2.refs_1_), custom_call_target="tpu_custom_call", output_to_operand_aliasing={{}: (2, {})} | custom-call | tf_op jit(solution)/shard_map/finish/pallas_call | solution.py:123
  (15 shorter events, 0.0 us)
Async XLA Ops:
  0.0 6.3 %collective-permute-start = (bf16[6,16,16384]{2,1,0:T(8,128)(2,1)}, bf16[6,16,16384]{2,1,0:T(8,128)(2,1)S(1)}, u32[]{:S(2)}, u32[]{:S(2)}) collective-permute-start(bf16[6,16,16384]{2,1,0:T(8,128)(2,1)} %own_hbm.7), channel_id=1, source_target_pairs={{0,4},{4,0},{8,12},{12,8},{16,20},{20,16},{24,28},{28,24},{1,5},{5... | collective-permute-start | bytes 9437192 | tf_op jit(solution)/shard_map/ppermute | solution.py:162
  0.5 26.5 %collective-permute-start.3 = (bf16[2048,128]{1,0:T(8,128)(2,1)}, bf16[2048,128]{1,0:T(8,128)(2,1)S(1)}, u32[]{:S(2)}, u32[]{:S(2)}) collective-permute-start(bf16[2048,128]{1,0:T(8,128)(2,1)} %bitcast.3), channel_id=1, source_target_pairs={{0,8},{4,12},{8,0},{12,4},{16,24},{20,28},{24,16},{28,20},{1,9},{5... | collective-permute-start | bytes 1572872 | tf_op jit(solution)/shard_map/ppermute | solution.py:147
  3.0 26.5 %collective-permute-start.2 = (bf16[2048,128]{1,0:T(8,128)(2,1)}, bf16[2048,128]{1,0:T(8,128)(2,1)S(1)}, u32[]{:S(2)}, u32[]{:S(2)}) collective-permute-start(bf16[2048,128]{1,0:T(8,128)(2,1)} %bitcast.4), channel_id=1, source_target_pairs={{0,16},{4,20},{8,24},{12,28},{16,0},{20,4},{24,8},{28,12},{1,17},{... | collective-permute-start | bytes 1572872 | tf_op jit(solution)/shard_map/ppermute | solution.py:147
  6.3 1.9 %copy-start = (bf16[6,16,16384]{2,1,0:T(8,128)(2,1)S(1)}, bf16[6,16,16384]{2,1,0:T(8,128)(2,1)}, u32[]{:S(2)}) copy-start(bf16[6,16,16384]{2,1,0:T(8,128)(2,1)} %own_hbm.7) | copy-start | bytes 9437188
  8.2 1.0 %copy-start.2 = (bf16[1,16,128,128]{3,2,1,0:T(8,128)(2,1)S(1)}, bf16[1,16,128,128]{3,2,1,0:T(8,128)(2,1)}, u32[]{:S(2)}) copy-start(bf16[1,16,128,128]{3,2,1,0:T(8,128)(2,1)} %param.6) | copy-start | bytes 1572868
  9.2 20.8 %copy-start.1 = (bf16[6,16,16384]{2,1,0:T(8,128)(2,1)S(1)}, bf16[6,16,16384]{2,1,0:T(8,128)(2,1)}, u32[]{:S(2)}) copy-start(bf16[6,16,16384]{2,1,0:T(8,128)(2,1)} %own_hbm.7) | copy-start | bytes 9437188
  10.0 8.3 %collective-permute-start.6 = (bf16[4,6,32,128]{3,2,1,0:T(8,128)(2,1)S(1)}, bf16[4,6,32,128]{3,2,1,0:T(8,128)(2,1)S(1)}, u32[]{:S(2)}, u32[]{:S(2)}) collective-permute-start(bf16[4,6,32,128]{3,2,1,0:T(8,128)(2,1)S(1)} %get-tuple-element.27), channel_id=1, source_target_pairs={{0,1},{1,0},{2,3},{3,2},{4,5},{5,4},{6,7},{7,6},{8,9},{9,8},{10,11... | collective-permute-start | bytes 589832 | tf_op jit(solution)/shard_map/ppermute | solution.py:167
  12.6 10.9 %collective-permute-start.7 = (bf16[4,6,32,128]{3,2,1,0:T(8,128)(2,1)S(1)}, bf16[4,6,32,128]{3,2,1,0:T(8,128)(2,1)S(1)}, u32[]{:S(2)}, u32[]{:S(2)}) collective-permute-start(bf16[4,6,32,128]{3,2,1,0:T(8,128)(2,1)S(1)} %get-tuple-element.28), channel_id=1, source_target_pairs={{0,2},{1,3},{2,0},{3,1},{4,6},{5,7},{6,4},{7,5},{8,10},{9,11},{10,... | collective-permute-start | bytes 589832 | tf_op jit(solution)/shard_map/ppermute | solution.py:167
  14.1 12.0 %collective-permute-start.8 = (bf16[4,6,32,128]{3,2,1,0:T(8,128)(2,1)S(1)}, bf16[4,6,32,128]{3,2,1,0:T(8,128)(2,1)S(1)}, u32[]{:S(2)}, u32[]{:S(2)}) collective-permute-start(bf16[4,6,32,128]{3,2,1,0:T(8,128)(2,1)S(1)} %get-tuple-element.29), channel_id=1, source_target_pairs={{0,3},{1,2},{2,1},{3,0},{4,7},{5,6},{6,5},{7,4},{8,11},{9,10},{10,... | collective-permute-start | bytes 589832 | tf_op jit(solution)/shard_map/ppermute | solution.py:167
  18.3 11.3 %collective-permute-start.4 = (s32[1,16]{1,0:T(1,128)S(1)}, s32[1,16]{1,0:T(1,128)S(1)}, u32[]{:S(2)}, u32[]{:S(2)}) collective-permute-start(s32[1,16]{1,0:T(1,128)S(1)} %add_bitcast_fusion.named), channel_id=1, source_target_pairs={{0,8},{4,12},{8,0},{12,4},{16,24},{20,28},{24,16},{28,20},{1,9},{5... | collective-permute-start | bytes 200 | tf_op jit(solution)/shard_map/ppermute | solution.py:147
  23.5 6.1 %collective-permute-start.5 = (s32[1,16]{1,0:T(1,128)S(1)}, s32[1,16]{1,0:T(1,128)S(1)}, u32[]{:S(2)}, u32[]{:S(2)}) collective-permute-start(s32[1,16]{1,0:T(1,128)S(1)} %add_bitcast_fusion.named), channel_id=1, source_target_pairs={{0,16},{4,20},{8,24},{12,28},{16,0},{20,4},{24,8},{28,12},{1,17},{... | collective-permute-start | bytes 200 | tf_op jit(solution)/shard_map/ppermute | solution.py:147
  29.6 16.2 %collective-permute-start.9 = (bf16[2048,128]{1,0:T(8,128)(2,1)S(1)}, bf16[2048,128]{1,0:T(8,128)(2,1)S(1)}, u32[]{:S(2)}, u32[]{:S(2)}) collective-permute-start(bf16[2048,128]{1,0:T(8,128)(2,1)S(1)} %collective-permute-done.2.mats_hbm), channel_id=1, source_target_pairs={{0,8},{4,12},{8,0},{12,4},{16,24},{20,28},{24,16},{28,20},{1,9},{5... | collective-permute-start | bytes 1572872 | tf_op jit(solution)/shard_map/ppermute | solution.py:147
  30.8 7.9 %collective-permute-start.10 = (bf16[4,6,32,128]{3,2,1,0:T(8,128)(2,1)S(1)}, bf16[4,6,32,128]{3,2,1,0:T(8,128)(2,1)S(1)}, u32[]{:S(2)}, u32[]{:S(2)}) collective-permute-start(bf16[4,6,32,128]{3,2,1,0:T(8,128)(2,1)S(1)} %get-tuple-element.33), channel_id=1, source_target_pairs={{0,1},{1,0},{2,3},{3,2},{4,5},{5,4},{6,7},{7,6},{8,9},{9,8},{10,11... | collective-permute-start | bytes 589832 | tf_op jit(solution)/shard_map/ppermute | solution.py:167
  32.3 10.6 %collective-permute-start.11 = (bf16[4,6,32,128]{3,2,1,0:T(8,128)(2,1)S(1)}, bf16[4,6,32,128]{3,2,1,0:T(8,128)(2,1)S(1)}, u32[]{:S(2)}, u32[]{:S(2)}) collective-permute-start(bf16[4,6,32,128]{3,2,1,0:T(8,128)(2,1)S(1)} %get-tuple-element.34), channel_id=1, source_target_pairs={{0,2},{1,3},{2,0},{3,1},{4,6},{5,7},{6,4},{7,5},{8,10},{9,11},{10,... | collective-permute-start | bytes 589832 | tf_op jit(solution)/shard_map/ppermute | solution.py:167
  33.8 11.2 %collective-permute-start.12 = (bf16[4,6,32,128]{3,2,1,0:T(8,128)(2,1)S(1)}, bf16[4,6,32,128]{3,2,1,0:T(8,128)(2,1)S(1)}, u32[]{:S(2)}, u32[]{:S(2)}) collective-permute-start(bf16[4,6,32,128]{3,2,1,0:T(8,128)(2,1)S(1)} %get-tuple-element.35), channel_id=1, source_target_pairs={{0,3},{1,2},{2,1},{3,0},{4,7},{5,6},{6,5},{7,4},{8,11},{9,10},{10,... | collective-permute-start | bytes 589832 | tf_op jit(solution)/shard_map/ppermute | solution.py:167
  35.1 16.0 %collective-permute-start.18 = (bf16[4,6,32,128]{3,2,1,0:T(8,128)(2,1)S(1)}, bf16[4,6,32,128]{3,2,1,0:T(8,128)(2,1)S(1)}, u32[]{:S(2)}, u32[]{:S(2)}) collective-permute-start(bf16[4,6,32,128]{3,2,1,0:T(8,128)(2,1)S(1)} %get-tuple-element.42), channel_id=1, source_target_pairs={{0,1},{1,0},{2,3},{3,2},{4,5},{5,4},{6,7},{7,6},{8,9},{9,8},{10,11... | collective-permute-start | bytes 589832 | tf_op jit(solution)/shard_map/ppermute | solution.py:167
  38.6 13.2 %collective-permute-start.19 = (bf16[4,6,32,128]{3,2,1,0:T(8,128)(2,1)S(1)}, bf16[4,6,32,128]{3,2,1,0:T(8,128)(2,1)S(1)}, u32[]{:S(2)}, u32[]{:S(2)}) collective-permute-start(bf16[4,6,32,128]{3,2,1,0:T(8,128)(2,1)S(1)} %get-tuple-element.43), channel_id=1, source_target_pairs={{0,2},{1,3},{2,0},{3,1},{4,6},{5,7},{6,4},{7,5},{8,10},{9,11},{10,... | collective-permute-start | bytes 589832 | tf_op jit(solution)/shard_map/ppermute | solution.py:167
  42.9 5.4 %collective-permute-start.1 = (s32[1,16]{1,0:T(1,128)S(1)}, s32[1,16]{1,0:T(1,128)S(1)}, u32[]{:S(2)}, u32[]{:S(2)}) collective-permute-start(s32[1,16]{1,0:T(1,128)S(1)} %add_bitcast_fusion.named), channel_id=1, source_target_pairs={{0,24},{4,28},{8,16},{12,20},{16,8},{20,12},{24,0},{28,4},{1,25},{... | collective-permute-start | bytes 200 | tf_op jit(solution)/shard_map/ppermute | solution.py:147
  45.0 8.8 %collective-permute-start.20 = (bf16[4,6,32,128]{3,2,1,0:T(8,128)(2,1)S(1)}, bf16[4,6,32,128]{3,2,1,0:T(8,128)(2,1)S(1)}, u32[]{:S(2)}, u32[]{:S(2)}) collective-permute-start(bf16[4,6,32,128]{3,2,1,0:T(8,128)(2,1)S(1)} %get-tuple-element.44), channel_id=1, source_target_pairs={{0,3},{1,2},{2,1},{3,0},{4,7},{5,6},{6,5},{7,4},{8,11},{9,10},{10,... | collective-permute-start | bytes 589832 | tf_op jit(solution)/shard_map/ppermute | solution.py:167
  45.7 16.2 %copy-start.3 = (f32[4,128]{1,0:T(4,128)S(1)}, f32[4,128]{1,0:T(4,128)}, u32[]{:S(2)}) copy-start(f32[4,128]{1,0:T(4,128)} %weight_ref.3) | copy-start | bytes 6148
  45.7 9.6 %collective-permute-start.13 = (bf16[4,6,32,128]{3,2,1,0:T(8,128)(2,1)S(1)}, bf16[4,6,32,128]{3,2,1,0:T(8,128)(2,1)S(1)}, u32[]{:S(2)}, u32[]{:S(2)}) collective-permute-start(bf16[4,6,32,128]{3,2,1,0:T(8,128)(2,1)S(1)} %total.5), channel_id=1, source_target_pairs={{0,16},{4,20},{8,24},{12,28},{16,0},{20,4},{24,8},{28,12},{1,17},{... | collective-permute-start | bytes 589832 | tf_op jit(solution)/shard_map/ppermute | solution.py:147
  49.1 7.8 %collective-permute-start.14 = (bf16[4,6,32,128]{3,2,1,0:T(8,128)(2,1)S(1)}, bf16[4,6,32,128]{3,2,1,0:T(8,128)(2,1)S(1)}, u32[]{:S(2)}, u32[]{:S(2)}) collective-permute-start(bf16[4,6,32,128]{3,2,1,0:T(8,128)(2,1)S(1)} %get-tuple-element.38), channel_id=1, source_target_pairs={{0,1},{1,0},{2,3},{3,2},{4,5},{5,4},{6,7},{7,6},{8,9},{9,8},{10,11... | collective-permute-start | bytes 589832 | tf_op jit(solution)/shard_map/ppermute | solution.py:167
  51.0 8.4 %collective-permute-start.15 = (bf16[4,6,32,128]{3,2,1,0:T(8,128)(2,1)S(1)}, bf16[4,6,32,128]{3,2,1,0:T(8,128)(2,1)S(1)}, u32[]{:S(2)}, u32[]{:S(2)}) collective-permute-start(bf16[4,6,32,128]{3,2,1,0:T(8,128)(2,1)S(1)} %get-tuple-element.39), channel_id=1, source_target_pairs={{0,2},{1,3},{2,0},{3,1},{4,6},{5,7},{6,4},{7,5},{8,10},{9,11},{10,... | collective-permute-start | bytes 589832 | tf_op jit(solution)/shard_map/ppermute | solution.py:167
  51.8 7.7 %collective-permute-start.16 = (bf16[4,6,32,128]{3,2,1,0:T(8,128)(2,1)S(1)}, bf16[4,6,32,128]{3,2,1,0:T(8,128)(2,1)S(1)}, u32[]{:S(2)}, u32[]{:S(2)}) collective-permute-start(bf16[4,6,32,128]{3,2,1,0:T(8,128)(2,1)S(1)} %get-tuple-element.40), channel_id=1, source_target_pairs={{0,3},{1,2},{2,1},{3,0},{4,7},{5,6},{6,5},{7,4},{8,11},{9,10},{10,... | collective-permute-start | bytes 589832 | tf_op jit(solution)/shard_map/ppermute | solution.py:167
  54.0 7.9 %collective-permute-start.21 = (bf16[4,6,32,128]{3,2,1,0:T(8,128)(2,1)S(1)}, bf16[4,6,32,128]{3,2,1,0:T(8,128)(2,1)S(1)}, u32[]{:S(2)}, u32[]{:S(2)}) collective-permute-start(bf16[4,6,32,128]{3,2,1,0:T(8,128)(2,1)S(1)} %total.7), channel_id=1, source_target_pairs={{0,8},{4,12},{8,0},{12,4},{16,24},{20,28},{24,16},{28,20},{1,9},{5... | collective-permute-start | bytes 589832 | tf_op jit(solution)/shard_map/ppermute | solution.py:147
  59.6 7.6 %collective-permute-start.17 = (bf16[4,6,32,128]{3,2,1,0:T(8,128)(2,1)S(1)}, bf16[4,6,32,128]{3,2,1,0:T(8,128)(2,1)S(1)}, u32[]{:S(2)}, u32[]{:S(2)}) collective-permute-start(bf16[4,6,32,128]{3,2,1,0:T(8,128)(2,1)S(1)} %total.6), channel_id=1, source_target_pairs={{0,24},{4,28},{8,16},{12,20},{16,8},{20,12},{24,0},{28,4},{1,25},{... | collective-permute-start | bytes 589832 | tf_op jit(solution)/shard_map/ppermute | solution.py:147

commit v5 on v4

--- a/solution.py
+++ b/solution.py
@@ -18,28 +18,20 @@
     return me // CORES, lax.rem(me, CORES), lax.axis_index("box")
 
 
-def interpolate_kernel(turn, boxes, blocks, named, own_hbm, far_hbm, mats_hbm, *rest):
-    outs, (own, far, mats, acc, sems) = rest[:boxes], rest[boxes:]
+def interpolate_kernel(turn, boxes, blocks, named, traces, far, mats, *rest):
+    outs, acc = rest[:boxes], rest[boxes]
     chip, core, box = place()
-    comp, samples, width = own.shape
+    comp, samples, _ = traces.shape
     nodes = mats.shape[1]
     slots = acc.shape[0] // boxes
-    at = pl.ds(pl.multiple_of(((chip ^ turn) * CORES + core) * width, width), width)
-    copies = [
-        pltpu.make_async_copy(mats_hbm, mats, sems.at[0]),
-        pltpu.make_async_copy(own_hbm.at[:, :, at], own, sems.at[1]),
-        pltpu.make_async_copy(far_hbm.at[:, :, at], far, sems.at[2]),
-    ]
-    for copy in copies:
-        copy.start()
+    start = ((chip ^ turn) * CORES + core) * blocks * nodes
     acc[...] = jnp.zeros_like(acc)
-    for copy in copies:
-        copy.wait()
     named_row = named[...]
     for j in range(blocks):
         target = named_row[0, j]
-        for ref, half in ((own, core), (far, 1 - core)):
-            x = ref[:, :, j * nodes:(j + 1) * nodes]
+        at = pl.ds(pl.multiple_of(start + j * nodes, nodes), nodes)
+        for ref, half in ((traces, core), (far, 1 - core)):
+            x = ref[:, :, at]
             if samples % 16:
                 x = x.astype(jnp.float32).reshape(comp * samples, nodes).astype(x.dtype)
             else:
@@ -55,19 +47,12 @@
 def interpolate(turn, named, traces, far, mats, blocks, boxes, slots):
     nodes = mats.shape[1]
     comp, samples, _ = traces.shape
-    width = blocks * nodes
     shape = (slots, comp, CORES * samples, nodes)
     return pl.pallas_call(
         functools.partial(interpolate_kernel, turn, boxes, blocks),
-        in_specs=[pl.BlockSpec(memory_space=pltpu.VMEM)] + [pl.BlockSpec(memory_space=pl.ANY)] * 3,
+        in_specs=[pl.BlockSpec(memory_space=pltpu.VMEM)] * 4,
         out_specs=[pl.BlockSpec(memory_space=pltpu.VMEM)] * boxes,
-        scratch_shapes=[
-            pltpu.VMEM((comp, samples, width), traces.dtype),
-            pltpu.VMEM((comp, samples, width), traces.dtype),
-            pltpu.VMEM(mats.shape, mats.dtype),
-            pltpu.VMEM((boxes * slots, comp, CORES, samples, nodes), jnp.float32),
-            pltpu.SemaphoreType.DMA((3,)),
-        ],
+        scratch_shapes=[pltpu.VMEM((boxes * slots, comp, CORES, samples, nodes), jnp.float32)],
         out_shape=[
             jax.ShapeDtypeStruct(shape, jnp.bfloat16 if d else jnp.float32) for d in range(boxes)
         ],

time: 68.1 us -> 68 us (level)
  transfers between devices with their start and end apart: 22 -> 22, of which waited for: 12 -> 12; matrix products, arithmetic and copies ran while one was open for 1% -> 1% of each run, Pallas kernels for 6% -> 5%
where the time goes in v5:
time: 68 us; the launch traced here: 67.8 us
  starting transfers between devices  34.2 us (50%)
  waiting for transfers between devices  25.5 us (38%)
  Pallas kernels  4.42 us (6%)
  local copies, waits for them, and re-layouts  2.94 us (4%)
    ppermute x9, starting transfers between devices, along(): return lax.ppermute(x, 'tm', pairs)  18.3 us
    ppermute x12, waiting for transfers between devices, make(): lax.ppermute(wait(get('face', turn)[d]), 'box', [(b, b ^ d) for b in rang...  17 us
    ppermute x12, starting transfers between devices, make(): lax.ppermute(wait(get('face', turn)[d]), 'box', [(b, b ^ d) for b in rang...  15.5 us
    ppermute x9, waiting for transfers between devices, along(): return lax.ppermute(x, 'tm', pairs)  8.46 us
    unnamed x8, local copies, waits for them, and re-layouts  2.94 us
    pallas_call x4, Pallas kernels, interpolate(): pl.pallas_call(functools.partial(interpolate_kernel, turn, boxes, blocks)...  2.45 us
    pallas_call x2, Pallas kernels, finish(): pl.pallas_call(functools.partial(finish_kernel, turns, len(pieces)), in_s...  1.58 us
  transfers between devices with their start and end apart: 22, of which 12 were waited for; matrix products, arithmetic and copies ran while one was open for 1% of the time, Pallas kernels for 5%

profile of v5, /device:TPU:0, one launch (start us, length us, event | category | flops | bytes accessed | tf_op | source)
XLA Modules:
  0.0 67.8 jit_solution(12731991426441154225)
XLA Ops:
  0.0 0.5 collective-permute-start
  0.5 2.6 %collective-permute-start.3 = (bf16[2048,128]{1,0:T(8,128)(2,1)}, bf16[2048,128]{1,0:T(8,128)(2,1)S(1)}, u32[]{:S(2)}, u32[]{:S(2)}) collective-permute-start(bf16[2048,128]{1,0:T(8,128)(2,1)} %bitcast.3), channel_id=1, source_target_pairs={{0,8},{4,12},{8,0},{12,4},{16,24},{20,28},{24,16},{28,20},{1,9},{5... | collective-permute-start | bytes 1572872 | tf_op jit(solution)/shard_map/ppermute | solution.py:132
  3.0 2.6 %collective-permute-start.2 = (bf16[2048,128]{1,0:T(8,128)(2,1)}, bf16[2048,128]{1,0:T(8,128)(2,1)S(1)}, u32[]{:S(2)}, u32[]{:S(2)}) collective-permute-start(bf16[2048,128]{1,0:T(8,128)(2,1)} %bitcast.4), channel_id=1, source_target_pairs={{0,16},{4,20},{8,24},{12,28},{16,0},{20,4},{24,8},{28,12},{1,17},{... | collective-permute-start | bytes 1572872 | tf_op jit(solution)/shard_map/ppermute | solution.py:132
  5.6 0.7 add_bitcast_fusion.named
  6.3 1.9 %copy-done = bf16[6,16,16384]{2,1,0:T(8,128)(2,1)S(1)} copy-done((bf16[6,16,16384]{2,1,0:T(8,128)(2,1)S(1)}, bf16[6,16,16384]{2,1,0:T(8,128)(2,1)}, u32[]{:S(2)}) %copy-start) | copy-done | bytes 3145752
  8.2 1.0 %copy-done.2 = bf16[1,16,128,128]{3,2,1,0:T(8,128)(2,1)S(1)} copy-done((bf16[1,16,128,128]{3,2,1,0:T(8,128)(2,1)S(1)}, bf16[1,16,128,128]{3,2,1,0:T(8,128)(2,1)}, u32[]{:S(2)}) %copy-start.2) | copy-done | bytes 524312
  9.2 0.6 interpolate.4
  9.8 2.6 %collective-permute-start.6 = (bf16[4,6,32,128]{3,2,1,0:T(8,128)(2,1)S(1)}, bf16[4,6,32,128]{3,2,1,0:T(8,128)(2,1)S(1)}, u32[]{:S(2)}, u32[]{:S(2)}) collective-permute-start(bf16[4,6,32,128]{3,2,1,0:T(8,128)(2,1)S(1)} %get-tuple-element.27), channel_id=1, source_target_pairs={{0,1},{1,0},{2,3},{3,2},{4,5},{5,4},{6,7},{7,6},{8,9},{9,8},{10,11... | collective-permute-start | bytes 589832 | tf_op jit(solution)/shard_map/ppermute | solution.py:152
  12.4 1.5 %collective-permute-start.7 = (bf16[4,6,32,128]{3,2,1,0:T(8,128)(2,1)S(1)}, bf16[4,6,32,128]{3,2,1,0:T(8,128)(2,1)S(1)}, u32[]{:S(2)}, u32[]{:S(2)}) collective-permute-start(bf16[4,6,32,128]{3,2,1,0:T(8,128)(2,1)S(1)} %get-tuple-element.28), channel_id=1, source_target_pairs={{0,2},{1,3},{2,0},{3,1},{4,6},{5,7},{6,4},{7,5},{8,10},{9,11},{10,... | collective-permute-start | bytes 589832 | tf_op jit(solution)/shard_map/ppermute | solution.py:152
  13.9 0.0 collective-permute-start.8
  14.0 4.1 %collective-permute-done.6.refs_1_ = bf16[4,6,32,128]{3,2,1,0:T(8,128)(2,1)S(1)} collective-permute-done((bf16[4,6,32,128]{3,2,1,0:T(8,128)(2,1)S(1)}, bf16[4,6,32,128]{3,2,1,0:T(8,128)(2,1)S(1)}, u32[]{:S(2)}, u32[]{:S(2)}) %collective-permute-start.6) | collective-permute-done | bytes 196640 | tf_op jit(solution)/shard_map/ppermute | solution.py:152
  18.1 2.1 %collective-permute-start.4 = (s32[1,16]{1,0:T(1,128)S(1)}, s32[1,16]{1,0:T(1,128)S(1)}, u32[]{:S(2)}, u32[]{:S(2)}) collective-permute-start(s32[1,16]{1,0:T(1,128)S(1)} %add_bitcast_fusion.named), channel_id=1, source_target_pairs={{0,8},{4,12},{8,0},{12,4},{16,24},{20,28},{24,16},{28,20},{1,9},{5... | collective-permute-start | bytes 200 | tf_op jit(solution)/shard_map/ppermute | solution.py:132
  20.3 3.0 %collective-permute-done.7.refs_2_ = bf16[4,6,32,128]{3,2,1,0:T(8,128)(2,1)S(1)} collective-permute-done((bf16[4,6,32,128]{3,2,1,0:T(8,128)(2,1)S(1)}, bf16[4,6,32,128]{3,2,1,0:T(8,128)(2,1)S(1)}, u32[]{:S(2)}, u32[]{:S(2)}) %collective-permute-start.7) | collective-permute-done | bytes 196640 | tf_op jit(solution)/shard_map/ppermute | solution.py:152
  23.3 2.6 %collective-permute-start.5 = (s32[1,16]{1,0:T(1,128)S(1)}, s32[1,16]{1,0:T(1,128)S(1)}, u32[]{:S(2)}, u32[]{:S(2)}) collective-permute-start(s32[1,16]{1,0:T(1,128)S(1)} %add_bitcast_fusion.named), channel_id=1, source_target_pairs={{0,16},{4,20},{8,24},{12,28},{16,0},{20,4},{24,8},{28,12},{1,17},{... | collective-permute-start | bytes 200 | tf_op jit(solution)/shard_map/ppermute | solution.py:132
  25.9 0.1 total.4.refs_0_
  26.0 0.9 %collective-permute-done.3.mats = bf16[2048,128]{1,0:T(8,128)(2,1)S(1)} collective-permute-done((bf16[2048,128]{1,0:T(8,128)(2,1)}, bf16[2048,128]{1,0:T(8,128)(2,1)S(1)}, u32[]{:S(2)}, u32[]{:S(2)}) %collective-permute-start.3) | collective-permute-done | bytes 524320 | tf_op jit(solution)/shard_map/ppermute | solution.py:132
  26.9 2.6 %collective-permute-done.2.mats = bf16[2048,128]{1,0:T(8,128)(2,1)S(1)} collective-permute-done((bf16[2048,128]{1,0:T(8,128)(2,1)}, bf16[2048,128]{1,0:T(8,128)(2,1)S(1)}, u32[]{:S(2)}, u32[]{:S(2)}) %collective-permute-start.2) | collective-permute-done | bytes 524320 | tf_op jit(solution)/shard_map/ppermute | solution.py:132
  29.5 0.1 collective-permute-done.5.named
  29.6 0.4 collective-permute-start.9
  30.0 0.6 interpolate.6
  30.6 1.6 %collective-permute-start.10 = (bf16[4,6,32,128]{3,2,1,0:T(8,128)(2,1)S(1)}, bf16[4,6,32,128]{3,2,1,0:T(8,128)(2,1)S(1)}, u32[]{:S(2)}, u32[]{:S(2)}) collective-permute-start(bf16[4,6,32,128]{3,2,1,0:T(8,128)(2,1)S(1)} %get-tuple-element.33), channel_id=1, source_target_pairs={{0,1},{1,0},{2,3},{3,2},{4,5},{5,4},{6,7},{7,6},{8,9},{9,8},{10,11... | collective-permute-start | bytes 589832 | tf_op jit(solution)/shard_map/ppermute | solution.py:152
  32.2 1.5 %collective-permute-start.11 = (bf16[4,6,32,128]{3,2,1,0:T(8,128)(2,1)S(1)}, bf16[4,6,32,128]{3,2,1,0:T(8,128)(2,1)S(1)}, u32[]{:S(2)}, u32[]{:S(2)}) collective-permute-start(bf16[4,6,32,128]{3,2,1,0:T(8,128)(2,1)S(1)} %get-tuple-element.34), channel_id=1, source_target_pairs={{0,2},{1,3},{2,0},{3,1},{4,6},{5,7},{6,4},{7,5},{8,10},{9,11},{10,... | collective-permute-start | bytes 589832 | tf_op jit(solution)/shard_map/ppermute | solution.py:152
  33.7 0.5 collective-permute-start.12
  34.2 0.6 interpolate.7
  34.8 1.6 %collective-permute-start.18 = (bf16[4,6,32,128]{3,2,1,0:T(8,128)(2,1)S(1)}, bf16[4,6,32,128]{3,2,1,0:T(8,128)(2,1)S(1)}, u32[]{:S(2)}, u32[]{:S(2)}) collective-permute-start(bf16[4,6,32,128]{3,2,1,0:T(8,128)(2,1)S(1)} %get-tuple-element.42), channel_id=1, source_target_pairs={{0,1},{1,0},{2,3},{3,2},{4,5},{5,4},{6,7},{7,6},{8,9},{9,8},{10,11... | collective-permute-start | bytes 589832 | tf_op jit(solution)/shard_map/ppermute | solution.py:152
  36.3 2.2 %collective-permute-done.10.refs_1_ = bf16[4,6,32,128]{3,2,1,0:T(8,128)(2,1)S(1)} collective-permute-done((bf16[4,6,32,128]{3,2,1,0:T(8,128)(2,1)S(1)}, bf16[4,6,32,128]{3,2,1,0:T(8,128)(2,1)S(1)}, u32[]{:S(2)}, u32[]{:S(2)}) %collective-permute-start.10) | collective-permute-done | bytes 196640 | tf_op jit(solution)/shard_map/ppermute | solution.py:152
  38.5 1.5 %collective-permute-start.19 = (bf16[4,6,32,128]{3,2,1,0:T(8,128)(2,1)S(1)}, bf16[4,6,32,128]{3,2,1,0:T(8,128)(2,1)S(1)}, u32[]{:S(2)}, u32[]{:S(2)}) collective-permute-start(bf16[4,6,32,128]{3,2,1,0:T(8,128)(2,1)S(1)} %get-tuple-element.43), channel_id=1, source_target_pairs={{0,2},{1,3},{2,0},{3,1},{4,6},{5,7},{6,4},{7,5},{8,10},{9,11},{10,... | collective-permute-start | bytes 589832 | tf_op jit(solution)/shard_map/ppermute | solution.py:152
  40.0 2.8 %collective-permute-done.11.refs_2_ = bf16[4,6,32,128]{3,2,1,0:T(8,128)(2,1)S(1)} collective-permute-done((bf16[4,6,32,128]{3,2,1,0:T(8,128)(2,1)S(1)}, bf16[4,6,32,128]{3,2,1,0:T(8,128)(2,1)S(1)}, u32[]{:S(2)}, u32[]{:S(2)}) %collective-permute-start.11) | collective-permute-done | bytes 196640 | tf_op jit(solution)/shard_map/ppermute | solution.py:152
  42.8 2.1 %collective-permute-start.1 = (s32[1,16]{1,0:T(1,128)S(1)}, s32[1,16]{1,0:T(1,128)S(1)}, u32[]{:S(2)}, u32[]{:S(2)}) collective-permute-start(s32[1,16]{1,0:T(1,128)S(1)} %add_bitcast_fusion.named), channel_id=1, source_target_pairs={{0,24},{4,28},{8,16},{12,20},{16,8},{20,12},{24,0},{28,4},{1,25},{... | collective-permute-start | bytes 200 | tf_op jit(solution)/shard_map/ppermute | solution.py:132
  44.9 0.6 collective-permute-start.20
  45.5 0.1 total.5
  45.6 0.0 copy-start.3
  45.6 2.3 %collective-permute-start.13 = (bf16[4,6,32,128]{3,2,1,0:T(8,128)(2,1)S(1)}, bf16[4,6,32,128]{3,2,1,0:T(8,128)(2,1)S(1)}, u32[]{:S(2)}, u32[]{:S(2)}) collective-permute-start(bf16[4,6,32,128]{3,2,1,0:T(8,128)(2,1)S(1)} %total.5), channel_id=1, source_target_pairs={{0,16},{4,20},{8,24},{12,28},{16,0},{20,4},{24,8},{28,12},{1,17},{... | collective-permute-start | bytes 589832 | tf_op jit(solution)/shard_map/ppermute | solution.py:132
  47.9 0.3 collective-permute-done.1.named
  48.2 0.6 interpolate.5
  48.8 1.9 %collective-permute-start.14 = (bf16[4,6,32,128]{3,2,1,0:T(8,128)(2,1)S(1)}, bf16[4,6,32,128]{3,2,1,0:T(8,128)(2,1)S(1)}, u32[]{:S(2)}, u32[]{:S(2)}) collective-permute-start(bf16[4,6,32,128]{3,2,1,0:T(8,128)(2,1)S(1)} %get-tuple-element.38), channel_id=1, source_target_pairs={{0,1},{1,0},{2,3},{3,2},{4,5},{5,4},{6,7},{7,6},{8,9},{9,8},{10,11... | collective-permute-start | bytes 589832 | tf_op jit(solution)/shard_map/ppermute | solution.py:152
  50.7 0.8 %collective-permute-start.15 = (bf16[4,6,32,128]{3,2,1,0:T(8,128)(2,1)S(1)}, bf16[4,6,32,128]{3,2,1,0:T(8,128)(2,1)S(1)}, u32[]{:S(2)}, u32[]{:S(2)}) collective-permute-start(bf16[4,6,32,128]{3,2,1,0:T(8,128)(2,1)S(1)} %get-tuple-element.39), channel_id=1, source_target_pairs={{0,2},{1,3},{2,0},{3,1},{4,6},{5,7},{6,4},{7,5},{8,10},{9,11},{10,... | collective-permute-start | bytes 589832 | tf_op jit(solution)/shard_map/ppermute | solution.py:152
  51.5 1.4 %collective-permute-start.16 = (bf16[4,6,32,128]{3,2,1,0:T(8,128)(2,1)S(1)}, bf16[4,6,32,128]{3,2,1,0:T(8,128)(2,1)S(1)}, u32[]{:S(2)}, u32[]{:S(2)}) collective-permute-start(bf16[4,6,32,128]{3,2,1,0:T(8,128)(2,1)S(1)} %get-tuple-element.40), channel_id=1, source_target_pairs={{0,3},{1,2},{2,1},{3,0},{4,7},{5,6},{6,5},{7,4},{8,11},{9,10},{10,... | collective-permute-start | bytes 589832 | tf_op jit(solution)/shard_map/ppermute | solution.py:152
  53.0 0.8 %collective-permute-done.20.refs_3_ = bf16[4,6,32,128]{3,2,1,0:T(8,128)(2,1)S(1)} collective-permute-done((bf16[4,6,32,128]{3,2,1,0:T(8,128)(2,1)S(1)}, bf16[4,6,32,128]{3,2,1,0:T(8,128)(2,1)S(1)}, u32[]{:S(2)}, u32[]{:S(2)}) %collective-permute-start.20) | collective-permute-done | bytes 196640 | tf_op jit(solution)/shard_map/ppermute | solution.py:152
  53.7 0.1 total.7
  53.8 1.4 %collective-permute-start.21 = (bf16[4,6,32,128]{3,2,1,0:T(8,128)(2,1)S(1)}, bf16[4,6,32,128]{3,2,1,0:T(8,128)(2,1)S(1)}, u32[]{:S(2)}, u32[]{:S(2)}) collective-permute-start(bf16[4,6,32,128]{3,2,1,0:T(8,128)(2,1)S(1)} %total.7), channel_id=1, source_target_pairs={{0,8},{4,12},{8,0},{12,4},{16,24},{20,28},{24,16},{28,20},{1,9},{5... | collective-permute-start | bytes 589832 | tf_op jit(solution)/shard_map/ppermute | solution.py:132
  55.2 1.6 %collective-permute-done.14.refs_1_ = bf16[4,6,32,128]{3,2,1,0:T(8,128)(2,1)S(1)} collective-permute-done((bf16[4,6,32,128]{3,2,1,0:T(8,128)(2,1)S(1)}, bf16[4,6,32,128]{3,2,1,0:T(8,128)(2,1)S(1)}, u32[]{:S(2)}, u32[]{:S(2)}) %collective-permute-start.14) | collective-permute-done | bytes 196640 | tf_op jit(solution)/shard_map/ppermute | solution.py:152
  56.8 2.5 %collective-permute-done.15.refs_2_ = bf16[4,6,32,128]{3,2,1,0:T(8,128)(2,1)S(1)} collective-permute-done((bf16[4,6,32,128]{3,2,1,0:T(8,128)(2,1)S(1)}, bf16[4,6,32,128]{3,2,1,0:T(8,128)(2,1)S(1)}, u32[]{:S(2)}, u32[]{:S(2)}) %collective-permute-start.15) | collective-permute-done | bytes 196640 | tf_op jit(solution)/shard_map/ppermute | solution.py:152
  59.3 0.1 total.6
  59.4 2.2 %collective-permute-start.17 = (bf16[4,6,32,128]{3,2,1,0:T(8,128)(2,1)S(1)}, bf16[4,6,32,128]{3,2,1,0:T(8,128)(2,1)S(1)}, u32[]{:S(2)}, u32[]{:S(2)}) collective-permute-start(bf16[4,6,32,128]{3,2,1,0:T(8,128)(2,1)S(1)} %total.6), channel_id=1, source_target_pairs={{0,24},{4,28},{8,16},{12,20},{16,8},{20,12},{24,0},{28,4},{1,25},{... | collective-permute-start | bytes 589832 | tf_op jit(solution)/shard_map/ppermute | solution.py:132
  61.6 0.9 %finish.2.refs_1_ = bf16[4,6,128,128]{3,2,1,0:T(8,128)(2,1)} custom-call(f32[4,128]{1,0:T(4,128)S(1)} %copy-done.3, f32[4,6,32,128]{3,2,1,0:T(8,128)S(1)} %total.4.refs_0_, bf16[4,6,32,128]{3,2,1,0:T(8,128)(2,1)S(1)} %collective-permute-done.21.refs_1_, bf16[4,6,32,128]{3,2,1,0:T(8,128)(2,1)S(1)} %collective-permute-done.13.refs_2_), custom_call_target="tpu_custom_call" | custom-call | tf_op jit(solution)/shard_map/finish/pallas_call | solution.py:108
  62.5 4.6 %collective-permute-done.17.refs_0_ = bf16[4,6,32,128]{3,2,1,0:T(8,128)(2,1)S(1)} collective-permute-done((bf16[4,6,32,128]{3,2,1,0:T(8,128)(2,1)S(1)}, bf16[4,6,32,128]{3,2,1,0:T(8,128)(2,1)S(1)}, u32[]{:S(2)}, u32[]{:S(2)}) %collective-permute-start.17) | collective-permute-done | bytes 196640 | tf_op jit(solution)/shard_map/ppermute | solution.py:132
  67.1 0.7 %finish.3 = bf16[4,6,128,128]{3,2,1,0:T(8,128)(2,1)} custom-call(f32[4,128]{1,0:T(4,128)S(1)} %copy-done.3, bf16[4,6,32,128]{3,2,1,0:T(8,128)(2,1)S(1)} %collective-permute-done.17.refs_0_, bf16[4,6,128,128]{3,2,1,0:T(8,128)(2,1)} %finish.2.refs_1_), custom_call_target="tpu_custom_call", output_to_operand_aliasing={{}: (2, {})} | custom-call | tf_op jit(solution)/shard_map/finish/pallas_call | solution.py:108
  (15 shorter events, 0.0 us)
Async XLA Ops:
  0.0 6.3 %collective-permute-start = (bf16[6,16,16384]{2,1,0:T(8,128)(2,1)}, bf16[6,16,16384]{2,1,0:T(8,128)(2,1)S(1)}, u32[]{:S(2)}, u32[]{:S(2)}) collective-permute-start(bf16[6,16,16384]{2,1,0:T(8,128)(2,1)} %traces.7), channel_id=1, source_target_pairs={{0,4},{4,0},{8,12},{12,8},{16,20},{20,16},{24,28},{28,24},{1,5},{5... | collective-permute-start | bytes 9437192 | tf_op jit(solution)/shard_map/ppermute | solution.py:147
  0.5 26.5 %collective-permute-start.3 = (bf16[2048,128]{1,0:T(8,128)(2,1)}, bf16[2048,128]{1,0:T(8,128)(2,1)S(1)}, u32[]{:S(2)}, u32[]{:S(2)}) collective-permute-start(bf16[2048,128]{1,0:T(8,128)(2,1)} %bitcast.3), channel_id=1, source_target_pairs={{0,8},{4,12},{8,0},{12,4},{16,24},{20,28},{24,16},{28,20},{1,9},{5... | collective-permute-start | bytes 1572872 | tf_op jit(solution)/shard_map/ppermute | solution.py:132
  3.0 26.5 %collective-permute-start.2 = (bf16[2048,128]{1,0:T(8,128)(2,1)}, bf16[2048,128]{1,0:T(8,128)(2,1)S(1)}, u32[]{:S(2)}, u32[]{:S(2)}) collective-permute-start(bf16[2048,128]{1,0:T(8,128)(2,1)} %bitcast.4), channel_id=1, source_target_pairs={{0,16},{4,20},{8,24},{12,28},{16,0},{20,4},{24,8},{28,12},{1,17},{... | collective-permute-start | bytes 1572872 | tf_op jit(solution)/shard_map/ppermute | solution.py:132
  6.3 1.9 %copy-start = (bf16[6,16,16384]{2,1,0:T(8,128)(2,1)S(1)}, bf16[6,16,16384]{2,1,0:T(8,128)(2,1)}, u32[]{:S(2)}) copy-start(bf16[6,16,16384]{2,1,0:T(8,128)(2,1)} %traces.7) | copy-start | bytes 9437188
  8.2 1.0 %copy-start.2 = (bf16[1,16,128,128]{3,2,1,0:T(8,128)(2,1)S(1)}, bf16[1,16,128,128]{3,2,1,0:T(8,128)(2,1)}, u32[]{:S(2)}) copy-start(bf16[1,16,128,128]{3,2,1,0:T(8,128)(2,1)} %param.6) | copy-start | bytes 1572868
  9.2 20.8 %copy-start.1 = (bf16[6,16,16384]{2,1,0:T(8,128)(2,1)S(1)}, bf16[6,16,16384]{2,1,0:T(8,128)(2,1)}, u32[]{:S(2)}) copy-start(bf16[6,16,16384]{2,1,0:T(8,128)(2,1)} %traces.7) | copy-start | bytes 9437188
  9.8 8.3 %collective-permute-start.6 = (bf16[4,6,32,128]{3,2,1,0:T(8,128)(2,1)S(1)}, bf16[4,6,32,128]{3,2,1,0:T(8,128)(2,1)S(1)}, u32[]{:S(2)}, u32[]{:S(2)}) collective-permute-start(bf16[4,6,32,128]{3,2,1,0:T(8,128)(2,1)S(1)} %get-tuple-element.27), channel_id=1, source_target_pairs={{0,1},{1,0},{2,3},{3,2},{4,5},{5,4},{6,7},{7,6},{8,9},{9,8},{10,11... | collective-permute-start | bytes 589832 | tf_op jit(solution)/shard_map/ppermute | solution.py:152
  12.4 10.9 %collective-permute-start.7 = (bf16[4,6,32,128]{3,2,1,0:T(8,128)(2,1)S(1)}, bf16[4,6,32,128]{3,2,1,0:T(8,128)(2,1)S(1)}, u32[]{:S(2)}, u32[]{:S(2)}) collective-permute-start(bf16[4,6,32,128]{3,2,1,0:T(8,128)(2,1)S(1)} %get-tuple-element.28), channel_id=1, source_target_pairs={{0,2},{1,3},{2,0},{3,1},{4,6},{5,7},{6,4},{7,5},{8,10},{9,11},{10,... | collective-permute-start | bytes 589832 | tf_op jit(solution)/shard_map/ppermute | solution.py:152
  13.9 11.9 %collective-permute-start.8 = (bf16[4,6,32,128]{3,2,1,0:T(8,128)(2,1)S(1)}, bf16[4,6,32,128]{3,2,1,0:T(8,128)(2,1)S(1)}, u32[]{:S(2)}, u32[]{:S(2)}) collective-permute-start(bf16[4,6,32,128]{3,2,1,0:T(8,128)(2,1)S(1)} %get-tuple-element.29), channel_id=1, source_target_pairs={{0,3},{1,2},{2,1},{3,0},{4,7},{5,6},{6,5},{7,4},{8,11},{9,10},{10,... | collective-permute-start | bytes 589832 | tf_op jit(solution)/shard_map/ppermute | solution.py:152
  18.1 11.4 %collective-permute-start.4 = (s32[1,16]{1,0:T(1,128)S(1)}, s32[1,16]{1,0:T(1,128)S(1)}, u32[]{:S(2)}, u32[]{:S(2)}) collective-permute-start(s32[1,16]{1,0:T(1,128)S(1)} %add_bitcast_fusion.named), channel_id=1, source_target_pairs={{0,8},{4,12},{8,0},{12,4},{16,24},{20,28},{24,16},{28,20},{1,9},{5... | collective-permute-start | bytes 200 | tf_op jit(solution)/shard_map/ppermute | solution.py:132
  23.3 6.3 %collective-permute-start.5 = (s32[1,16]{1,0:T(1,128)S(1)}, s32[1,16]{1,0:T(1,128)S(1)}, u32[]{:S(2)}, u32[]{:S(2)}) collective-permute-start(s32[1,16]{1,0:T(1,128)S(1)} %add_bitcast_fusion.named), channel_id=1, source_target_pairs={{0,16},{4,20},{8,24},{12,28},{16,0},{20,4},{24,8},{28,12},{1,17},{... | collective-permute-start | bytes 200 | tf_op jit(solution)/shard_map/ppermute | solution.py:132
  29.6 16.0 %collective-permute-start.9 = (bf16[2048,128]{1,0:T(8,128)(2,1)S(1)}, bf16[2048,128]{1,0:T(8,128)(2,1)S(1)}, u32[]{:S(2)}, u32[]{:S(2)}) collective-permute-start(bf16[2048,128]{1,0:T(8,128)(2,1)S(1)} %collective-permute-done.2.mats), channel_id=1, source_target_pairs={{0,8},{4,12},{8,0},{12,4},{16,24},{20,28},{24,16},{28,20},{1,9},{5... | collective-permute-start | bytes 1572872 | tf_op jit(solution)/shard_map/ppermute | solution.py:132
  30.6 7.9 %collective-permute-start.10 = (bf16[4,6,32,128]{3,2,1,0:T(8,128)(2,1)S(1)}, bf16[4,6,32,128]{3,2,1,0:T(8,128)(2,1)S(1)}, u32[]{:S(2)}, u32[]{:S(2)}) collective-permute-start(bf16[4,6,32,128]{3,2,1,0:T(8,128)(2,1)S(1)} %get-tuple-element.33), channel_id=1, source_target_pairs={{0,1},{1,0},{2,3},{3,2},{4,5},{5,4},{6,7},{7,6},{8,9},{9,8},{10,11... | collective-permute-start | bytes 589832 | tf_op jit(solution)/shard_map/ppermute | solution.py:152
  32.2 10.6 %collective-permute-start.11 = (bf16[4,6,32,128]{3,2,1,0:T(8,128)(2,1)S(1)}, bf16[4,6,32,128]{3,2,1,0:T(8,128)(2,1)S(1)}, u32[]{:S(2)}, u32[]{:S(2)}) collective-permute-start(bf16[4,6,32,128]{3,2,1,0:T(8,128)(2,1)S(1)} %get-tuple-element.34), channel_id=1, source_target_pairs={{0,2},{1,3},{2,0},{3,1},{4,6},{5,7},{6,4},{7,5},{8,10},{9,11},{10,... | collective-permute-start | bytes 589832 | tf_op jit(solution)/shard_map/ppermute | solution.py:152
  33.7 11.2 %collective-permute-start.12 = (bf16[4,6,32,128]{3,2,1,0:T(8,128)(2,1)S(1)}, bf16[4,6,32,128]{3,2,1,0:T(8,128)(2,1)S(1)}, u32[]{:S(2)}, u32[]{:S(2)}) collective-permute-start(bf16[4,6,32,128]{3,2,1,0:T(8,128)(2,1)S(1)} %get-tuple-element.35), channel_id=1, source_target_pairs={{0,3},{1,2},{2,1},{3,0},{4,7},{5,6},{6,5},{7,4},{8,11},{9,10},{10,... | collective-permute-start | bytes 589832 | tf_op jit(solution)/shard_map/ppermute | solution.py:152
  34.8 16.0 %collective-permute-start.18 = (bf16[4,6,32,128]{3,2,1,0:T(8,128)(2,1)S(1)}, bf16[4,6,32,128]{3,2,1,0:T(8,128)(2,1)S(1)}, u32[]{:S(2)}, u32[]{:S(2)}) collective-permute-start(bf16[4,6,32,128]{3,2,1,0:T(8,128)(2,1)S(1)} %get-tuple-element.42), channel_id=1, source_target_pairs={{0,1},{1,0},{2,3},{3,2},{4,5},{5,4},{6,7},{7,6},{8,9},{9,8},{10,11... | collective-permute-start | bytes 589832 | tf_op jit(solution)/shard_map/ppermute | solution.py:152
  38.5 13.0 %collective-permute-start.19 = (bf16[4,6,32,128]{3,2,1,0:T(8,128)(2,1)S(1)}, bf16[4,6,32,128]{3,2,1,0:T(8,128)(2,1)S(1)}, u32[]{:S(2)}, u32[]{:S(2)}) collective-permute-start(bf16[4,6,32,128]{3,2,1,0:T(8,128)(2,1)S(1)} %get-tuple-element.43), channel_id=1, source_target_pairs={{0,2},{1,3},{2,0},{3,1},{4,6},{5,7},{6,4},{7,5},{8,10},{9,11},{10,... | collective-permute-start | bytes 589832 | tf_op jit(solution)/shard_map/ppermute | solution.py:152
  42.8 5.4 %collective-permute-start.1 = (s32[1,16]{1,0:T(1,128)S(1)}, s32[1,16]{1,0:T(1,128)S(1)}, u32[]{:S(2)}, u32[]{:S(2)}) collective-permute-start(s32[1,16]{1,0:T(1,128)S(1)} %add_bitcast_fusion.named), channel_id=1, source_target_pairs={{0,24},{4,28},{8,16},{12,20},{16,8},{20,12},{24,0},{28,4},{1,25},{... | collective-permute-start | bytes 200 | tf_op jit(solution)/shard_map/ppermute | solution.py:132
  44.9 8.8 %collective-permute-start.20 = (bf16[4,6,32,128]{3,2,1,0:T(8,128)(2,1)S(1)}, bf16[4,6,32,128]{3,2,1,0:T(8,128)(2,1)S(1)}, u32[]{:S(2)}, u32[]{:S(2)}) collective-permute-start(bf16[4,6,32,128]{3,2,1,0:T(8,128)(2,1)S(1)} %get-tuple-element.44), channel_id=1, source_target_pairs={{0,3},{1,2},{2,1},{3,0},{4,7},{5,6},{6,5},{7,4},{8,11},{9,10},{10,... | collective-permute-start | bytes 589832 | tf_op jit(solution)/shard_map/ppermute | solution.py:152
  45.6 16.1 %copy-start.3 = (f32[4,128]{1,0:T(4,128)S(1)}, f32[4,128]{1,0:T(4,128)}, u32[]{:S(2)}) copy-start(f32[4,128]{1,0:T(4,128)} %weight_ref.3) | copy-start | bytes 6148
  45.6 9.6 %collective-permute-start.13 = (bf16[4,6,32,128]{3,2,1,0:T(8,128)(2,1)S(1)}, bf16[4,6,32,128]{3,2,1,0:T(8,128)(2,1)S(1)}, u32[]{:S(2)}, u32[]{:S(2)}) collective-permute-start(bf16[4,6,32,128]{3,2,1,0:T(8,128)(2,1)S(1)} %total.5), channel_id=1, source_target_pairs={{0,16},{4,20},{8,24},{12,28},{16,0},{20,4},{24,8},{28,12},{1,17},{... | collective-permute-start | bytes 589832 | tf_op jit(solution)/shard_map/ppermute | solution.py:132
  48.8 7.9 %collective-permute-start.14 = (bf16[4,6,32,128]{3,2,1,0:T(8,128)(2,1)S(1)}, bf16[4,6,32,128]{3,2,1,0:T(8,128)(2,1)S(1)}, u32[]{:S(2)}, u32[]{:S(2)}) collective-permute-start(bf16[4,6,32,128]{3,2,1,0:T(8,128)(2,1)S(1)} %get-tuple-element.38), channel_id=1, source_target_pairs={{0,1},{1,0},{2,3},{3,2},{4,5},{5,4},{6,7},{7,6},{8,9},{9,8},{10,11... | collective-permute-start | bytes 589832 | tf_op jit(solution)/shard_map/ppermute | solution.py:152
  50.7 8.6 %collective-permute-start.15 = (bf16[4,6,32,128]{3,2,1,0:T(8,128)(2,1)S(1)}, bf16[4,6,32,128]{3,2,1,0:T(8,128)(2,1)S(1)}, u32[]{:S(2)}, u32[]{:S(2)}) collective-permute-start(bf16[4,6,32,128]{3,2,1,0:T(8,128)(2,1)S(1)} %get-tuple-element.39), channel_id=1, source_target_pairs={{0,2},{1,3},{2,0},{3,1},{4,6},{5,7},{6,4},{7,5},{8,10},{9,11},{10,... | collective-permute-start | bytes 589832 | tf_op jit(solution)/shard_map/ppermute | solution.py:152
  51.5 7.8 %collective-permute-start.16 = (bf16[4,6,32,128]{3,2,1,0:T(8,128)(2,1)S(1)}, bf16[4,6,32,128]{3,2,1,0:T(8,128)(2,1)S(1)}, u32[]{:S(2)}, u32[]{:S(2)}) collective-permute-start(bf16[4,6,32,128]{3,2,1,0:T(8,128)(2,1)S(1)} %get-tuple-element.40), channel_id=1, source_target_pairs={{0,3},{1,2},{2,1},{3,0},{4,7},{5,6},{6,5},{7,4},{8,11},{9,10},{10,... | collective-permute-start | bytes 589832 | tf_op jit(solution)/shard_map/ppermute | solution.py:152
  53.8 7.8 %collective-permute-start.21 = (bf16[4,6,32,128]{3,2,1,0:T(8,128)(2,1)S(1)}, bf16[4,6,32,128]{3,2,1,0:T(8,128)(2,1)S(1)}, u32[]{:S(2)}, u32[]{:S(2)}) collective-permute-start(bf16[4,6,32,128]{3,2,1,0:T(8,128)(2,1)S(1)} %total.7), channel_id=1, source_target_pairs={{0,8},{4,12},{8,0},{12,4},{16,24},{20,28},{24,16},{28,20},{1,9},{5... | collective-permute-start | bytes 589832 | tf_op jit(solution)/shard_map/ppermute | solution.py:132
  59.4 7.6 %collective-permute-start.17 = (bf16[4,6,32,128]{3,2,1,0:T(8,128)(2,1)S(1)}, bf16[4,6,32,128]{3,2,1,0:T(8,128)(2,1)S(1)}, u32[]{:S(2)}, u32[]{:S(2)}) collective-permute-start(bf16[4,6,32,128]{3,2,1,0:T(8,128)(2,1)S(1)} %total.6), channel_id=1, source_target_pairs={{0,24},{4,28},{8,16},{12,20},{16,8},{20,12},{24,0},{28,4},{1,25},{... | collective-permute-start | bytes 589832 | tf_op jit(solution)/shard_map/ppermute | solution.py:132
